TPU v7x, 128 devices: a whole 4x4x4 slice. The times are simulated.
128 devices in a mesh: ctx: 64 (over z_hi, y, x, core), tp: 2 (over z_lo).
Axes of the slice: x: 4, y: 4, z: 4 (z_hi: 2, z_lo: 2; z = z_hi * 2 + z_lo), core: 2. Of those that a mesh axis runs over, the one named last changes fastest.
Arguments:
- queries: bfloat16 [8192, 4096], P('ctx', 'tp'), may hold values from -140 to 140
- rotated_keys: bfloat16 [8192, 256], P('ctx', 'tp'), may hold values from -4.5 to 4.5
- value_matrix: bfloat16 [8192, 256], P('ctx', 'tp'), may hold values from -5 to 5
- lengths: int32 [8], replicated, may hold values from 1 to 4096, 8192 in all
- out_weight: bfloat16 [4096, 4096], P(('tp', 'ctx')), may hold values from -0.09375 to 0.09375
- residual: bfloat16 [8192, 4096], P(('ctx', 'tp')), may hold values from -3 to 3
- expert_ids: int32 [8192, 8], P(('ctx', 'tp')), may hold values from 0 to 127, all different within a row; in each aligned block of 64 rows (0 to 63, 64 to 127, ...) at most 6 rows name the same one
- router_gates: float32 [8192, 8], P(('ctx', 'tp')), may hold values from 0.02 to 0.25
- gate_proj: bfloat16 [128, 4096, 768], P(('ctx', 'tp')), may hold values from -0.09375 to 0.09375
- up_proj: bfloat16 [128, 4096, 768], P(('ctx', 'tp')), may hold values from -0.09375 to 0.09375
- down_proj: bfloat16 [128, 768, 4096], P(('ctx', 'tp')), may hold values from -0.21875 to 0.21875
Outputs:
- layer_out: bfloat16 [8192, 4096], P(('ctx', 'tp'))
Inputs may be any that keep to these rules, and one draw needn't show every extreme that they name: The lengths sum to 8192; the largest is half of 8192. `expert_ids`: each row names 8 different experts; in the rows of one device no expert is named by more than 6 rows, and in some device's rows one expert is named by exactly 6.
All inputs are finite; a program needn't handle non-finite values.
Results may differ from a plain program's by a relative error of at most 0.015.
Values may be sent and summed in bfloat16 or wider, within the bound.
No kernel may reach another device: no remote copies, remote signals or barrier semaphores. Data moves between devices by JAX's collectives and lax.ppermute only.
A program may use at most 128 MiB of HBM per device.

v0:
```python
import math

import jax
import jax.numpy as jnp
from jax import lax
from jax.sharding import PartitionSpec as P

HEAD_SIZE = 128
QUERY_HEAD_COUNT = 32
KEY_VALUE_HEADS = 2


def rollout_of(lengths, positions):
    ends = jnp.cumsum(lengths)
    return jnp.sum((positions[:, None] >= ends[None, :]).astype(jnp.int32), axis=1)


def body(
    queries,
    rotated_keys,
    value_matrix,
    lengths,
    out_weight,
    residual,
    expert_ids,
    router_gates,
    gate_proj,
    up_proj,
    down_proj,
):
    ctx_count = lax.axis_size("ctx")
    tp_count = lax.axis_size("tp")
    local_tokens = queries.shape[0]
    query_group = QUERY_HEAD_COUNT // KEY_VALUE_HEADS
    kv_local = rotated_keys.shape[1] // HEAD_SIZE
    query_first = lax.axis_index("ctx") * local_tokens
    query_pos = query_first + jnp.arange(local_tokens, dtype=jnp.int32)
    query_roll = rollout_of(lengths, query_pos)
    query_heads = queries.reshape(local_tokens, kv_local, query_group, HEAD_SIZE)
    scale = 1.0 / math.sqrt(HEAD_SIZE)
    last_query = query_first + local_tokens - 1
    initial = (
        jnp.full((kv_local, query_group, local_tokens), -jnp.inf, jnp.float32),
        jnp.zeros((kv_local, query_group, local_tokens), jnp.float32),
        jnp.zeros((local_tokens, kv_local, query_group, HEAD_SIZE), jnp.float32),
    )
    key_piece = lax.all_gather(rotated_keys, "ctx", axis=0, tiled=True)
    value_piece = lax.all_gather(value_matrix, "ctx", axis=0, tiled=True)
    count = key_piece.shape[0]
    feature_width = math.gcd(count, 512)

    def one_block(number, state):
        begin = number * feature_width

        def update(current):
            best, denom, accum = current
            key_block = lax.dynamic_slice_in_dim(key_piece, begin, feature_width, 0).reshape(
                feature_width, kv_local, HEAD_SIZE
            )
            value_block = lax.dynamic_slice_in_dim(value_piece, begin, feature_width, 0).reshape(
                feature_width, kv_local, HEAD_SIZE
            )
            key_pos = begin + jnp.arange(feature_width, dtype=jnp.int32)
            key_roll = rollout_of(lengths, key_pos)
            allowed = (key_pos[None, :] <= query_pos[:, None]) & (
                key_roll[None, :] == query_roll[:, None]
            )
            scores = (
                jnp.einsum(
                    "tgjd,sgd->gjts", query_heads, key_block, preferred_element_type=jnp.float32
                )
                * scale
            )
            scores = jnp.where(allowed[None, None], scores, -jnp.inf)
            fresh = jnp.maximum(best, jnp.max(scores, axis=-1))
            steady = jnp.where(jnp.isfinite(fresh), fresh, 0.0)
            expo = jnp.exp(scores - steady[..., None])
            factor = jnp.exp(best - steady)
            denom = denom * factor + jnp.sum(expo, axis=-1)
            added = jnp.einsum(
                "gjts,sgd->tgjd",
                expo.astype(jnp.bfloat16),
                value_block,
                preferred_element_type=jnp.float32,
            )
            accum = accum * jnp.transpose(factor, (2, 0, 1))[..., None] + added
            return (fresh, denom, accum)

        return lax.cond(begin <= last_query, update, lambda current: current, state)

    best, denom, accum = lax.fori_loop(0, count // feature_width, one_block, initial)
    attended = (
        (accum / jnp.transpose(denom, (2, 0, 1))[..., None])
        .reshape(local_tokens, kv_local * query_group * HEAD_SIZE)
        .astype(jnp.bfloat16)
    )
    model_width = residual.shape[1]
    partial_sum = jnp.dot(
        attended,
        lax.all_gather(out_weight, "ctx", axis=0, tiled=True),
        preferred_element_type=jnp.float32,
    )
    projected = lax.psum_scatter(
        partial_sum.astype(jnp.bfloat16), "tp", scatter_dimension=0, tiled=True
    ).astype(jnp.float32)
    hidden_state = (residual.astype(jnp.float32) + projected).astype(jnp.bfloat16)
    widened = hidden_state.astype(jnp.float32)
    normed = (
        widened * lax.rsqrt(jnp.mean(widened * widened, axis=1, keepdims=True) + 1e-06)
    ).astype(jnp.bfloat16)
    own_rows, top_count = expert_ids.shape
    local_experts = gate_proj.shape[0]
    devices = ctx_count * tp_count
    experts = devices * local_experts
    capacity = max(2, own_rows * top_count * 3 // (2 * experts))
    flat_ids = expert_ids.reshape(own_rows * top_count)
    onehot = (flat_ids[:, None] == jnp.arange(experts, dtype=jnp.int32)[None, :]).astype(jnp.int32)
    earlier = jnp.cumsum(onehot, axis=0) - onehot
    slot_index = jnp.sum(earlier * onehot, axis=1)
    target_rows = flat_ids * capacity + slot_index
    source_row = jnp.arange(own_rows * top_count, dtype=jnp.int32) // top_count
    outgoing = (
        jnp.zeros((experts * capacity, model_width), jnp.bfloat16)
        .at[target_rows]
        .set(normed[source_row])
    )
    shaped = outgoing.reshape(devices, local_experts, capacity, model_width)
    incoming = lax.all_to_all(shaped, ("ctx", "tp"), split_axis=0, concat_axis=0, tiled=True)
    gate = jnp.einsum("secd,edf->secf", incoming, gate_proj, preferred_element_type=jnp.float32)
    upward = jnp.einsum("secd,edf->secf", incoming, up_proj, preferred_element_type=jnp.float32)
    hidden = (jax.nn.silu(gate) * upward).astype(jnp.bfloat16)
    answered = lax.all_to_all(
        jnp.einsum("secf,efd->secd", hidden, down_proj, preferred_element_type=jnp.float32).astype(
            jnp.bfloat16
        ),
        ("ctx", "tp"),
        split_axis=0,
        concat_axis=0,
        tiled=True,
    )
    gathered_back = answered.reshape(experts * capacity, model_width)
    weighted = gathered_back[target_rows].astype(jnp.float32) * router_gates.reshape(
        own_rows * top_count, 1
    )
    mixed = jnp.sum(weighted.reshape(own_rows, top_count, model_width), axis=1)
    return (widened + mixed).astype(jnp.bfloat16)


def solution(mesh):
    in_specs = (
        P("ctx", "tp"),
        P("ctx", "tp"),
        P("ctx", "tp"),
        P(),
        P(("tp", "ctx"), None),
        P(("ctx", "tp"), None),
        P(("ctx", "tp"), None),
        P(("ctx", "tp"), None),
        P(("ctx", "tp"), None, None),
        P(("ctx", "tp"), None, None),
        P(("ctx", "tp"), None, None),
    )
    out_specs = P(("ctx", "tp"), None)
    return jax.shard_map(body, mesh=mesh, in_specs=in_specs, out_specs=out_specs, check_vma=False)
```

profile of v0, /device:TPU:5, one launch (start us, length us, event | category | flops | bytes accessed | tf_op | source)
XLA Modules:
  0.0 631.8 jit_solution(1346668057529644201)
XLA Ops:
  6.5 0.0 all-gather.6.cloned.1.call-start
  6.5 1.5 copy.42
  8.0 0.0 all-gather.6.cloned.1.call-update
  8.0 0.0 all-gather.4.cloned.1.call-start
  8.1 0.7 all-gather.4.cloned.1.call-update
  8.8 0.0 all-gather.8.cloned.1.call-start
  8.8 0.7 all-gather.8.cloned.1.call-update
  9.5 0.0 reduce-scatter.2.cloned.1.call-start
  9.6 0.8 reduce-window.26
  10.4 1.3 copy.41
  11.7 0.3 copy.43
  12.0 0.1 convert_reduce_fusion.1
  12.1 68.5 %all-gather.6.cloned.1.call-done = bf16[8192,128]{0,1:T(8,128)(2,1)} async-done(((bf16[128,128]{0,1:T(8,128)(2,1)}), bf16[8192,128]{0,1:T(8,128)(2,1)}) %all-gather.6.cloned.1.call-update) | async-done | bytes 2097168 | tf_op jit(solution)/shard_map/all_gather | solution.py:48
  80.6 70.1 %all-gather.4.cloned.1.call-done = bf16[8192,128]{1,0:T(8,128)(2,1)} async-done(((bf16[128,128]{1,0:T(8,128)(2,1)}), bf16[8192,128]{1,0:T(8,128)(2,1)}) %all-gather.4.cloned.1.call-update) | async-done | bytes 2097168 | tf_op jit(solution)/shard_map/all_gather | solution.py:47
  150.7 0.1 broadcast_in_dim.35
  150.8 13.0 %while.18 = (s32[]{:T(128)}, f32[1,16,128]{2,1,0:T(8,128)S(1)}, f32[1,16,128]{2,1,0:T(8,128)S(1)}, f32[128,1,16,128]{0,3,2,1:T(8,128)S(1)}, s32[]{:T(128)}, /*in...) while((s32[]{:T(128)}, f32[1,16,128]{2,1,0:T(8,128)S(1)}, ...), condition=%wide.region_9.10_spmd.clone, body=%wide.region_2.9_spmd.clone.sunk | while | flops 549157056 | bytes 15889341 | solution.py:91
  150.9 6.0 conditional.3
  150.9 0.8 reduce-window.17
  151.7 0.1 convert_reduce_fusion
  151.8 0.2 compare_and_fusion
  152.0 1.6 fusion.4
  153.7 2.3 fusion.12
  156.0 0.9 fusion.3
  156.9 6.0 conditional.3
  156.9 0.8 reduce-window.17
  157.8 0.1 convert_reduce_fusion
  157.9 0.2 compare_and_fusion
  158.1 1.6 fusion.4
  159.7 2.3 fusion.12
  162.0 0.9 fusion.3
  163.9 0.1 divide_convert_fusion
  164.0 94.5 %all-gather.8.cloned.1.call-done = bf16[2048,4096]{1,0:T(8,128)(2,1)} async-done(((bf16[32,4096]{1,0:T(8,128)(2,1)}), bf16[2048,4096]{1,0:T(8,128)(2,1)}) %all-gather.8.cloned.1.call-update) | async-done | bytes 16777232 | tf_op jit(solution)/shard_map/all_gather | solution.py:100
  258.5 9.2 %convolution_convert_fusion.1 = bf16[128,4096]{1,0:T(8,128)(2,1)} fusion(bf16[128,2048]{0,1:T(8,128)(2,1)S(1)} %bitcast.151, bf16[2048,4096]{1,0:T(8,128)(2,1)} %all-gather.8.cloned.1.call-done), kind=kOutput, calls=%fused_computation.45 | convolution fusion | flops 2148007936 | bytes 18350080 | tf_op jit(solution)/shard_map/dot_general | solution.py:98
  267.7 0.0 reduce-scatter.2.cloned.1.call-update
  267.7 0.0 copy-done.2
  267.7 0.1 copy.45
  267.8 0.1 eq.46
  267.9 0.1 eq.42
  268.0 0.1 copy.47
  268.1 0.2 fusion.61
  268.4 0.1 copy.44
  268.5 0.1 mul.81
  268.6 0.2 fusion.60
  268.9 19.2 %reduce-scatter.2.cloned.1.call-done = bf16[64,4096]{1,0:T(8,128)(2,1)} async-done(((bf16[128,4096]{1,0:T(8,128)(2,1)}), bf16[64,4096]{1,0:T(8,128)(2,1)}) %reduce-scatter.2.cloned.1.call-update) | async-done | bytes 524304 | tf_op jit(solution)/shard_map/reduce_scatter | solution.py:103
  288.1 0.0 copy-done
  288.1 1.3 fusion.56
  289.4 1.2 fusion.57
  290.6 22.6 %scatter_custom_fusion = bf16[768,4096]{1,0:T(8,128)(2,1)} fusion(s32[512]{0:T(512)S(1)} %bitcast.159, bf16[64,4096]{1,0:T(8,128)(2,1)S(1)} %fusion.57, s32[1024]{0:T(1024)S(1)} %pad_clamp_fusion.1, bf16[]{:T(256)} %constant.77.clone.1), kind=kCustom, calls=%fused_computation.48 | custom fusion | bytes 6291458 | tf_op jit(solution)/shard_map/scatter | solution.py:125
  313.2 10.2 %reshape.286 = bf16[128,1,6,4096]{3,2,0,1:T(8,128)(2,1)} reshape(bf16[768,4096]{1,0:T(8,128)(2,1)} %scatter_custom_fusion) | data formatting | bytes 12582912 | tf_op jit(solution)/shard_map/reshape | solution.py:127
  323.4 108.1 %all_to_all.10 = bf16[128,1,6,4096]{3,2,1,0:T(8,128)(2,1)S(1)} all-to-all(bf16[128,1,6,4096]{3,2,1,0:T(8,128)(2,1)} %bitcast.150), channel_id=1, replica_groups=mesh['ctx'=64,'tp'=2] {'ctx','tp'}, dimensions={0} | all-to-all | bytes 12582912 | tf_op jit(solution)/shard_map/all_to_all | solution.py:128
  431.5 22.8 %fusion.31 = f32[128,6,768]{2,0,1:T(8,128)S(1)} fusion(bf16[1,4096,768]{2,1,0:T(8,128)(2,1)} %param.23, bf16[128,1,6,4096]{3,2,1,0:T(8,128)(2,1)S(1)} %all_to_all.10), kind=kOutput, calls=%fused_computation.40 | convolution fusion | flops 4831838208 | bytes 14942208 | tf_op jit(solution)/shard_map/secd,edf->secf/dot_general | solution.py:129
  454.2 0.0 slice-done
  454.3 0.0 slice-done.1
  454.3 0.0 slice-start.3
  454.3 12.3 %fusion.51 = bf16[128,6,768]{2,0,1:T(8,128)(2,1)S(1)} fusion(bf16[1,4096,768]{2,1,0:T(8,128)(2,1)S(1)} %bitcast.163, bf16[128,1,6,4096]{3,2,1,0:T(8,128)(2,1)S(1)} %all_to_all.10, f32[128,6,768]{2,0,1:T(8,128)S(1)} %fusion.31), kind=kOutput, calls=%fused_computation.61 | convolution fusion | flops 4835377152 | bytes 16121856 | tf_op jit(solution)/shard_map/secd,edf->secf/dot_general | solution.py:130
  466.6 5.5 fusion.35
  472.1 6.7 %copy.51 = bf16[128,1,6,4096]{3,2,1,0:T(8,128)(2,1)} copy(bf16[128,1,6,4096]{3,0,2,1:T(8,128)(2,1)S(1)} %fusion.35) | data formatting | bytes 12582912 | tf_op jit(solution)/shard_map/convert_element_type | solution.py:133
  478.8 6.7 %all-to-all-start.1 = ((bf16[128,1,6,4096]{3,2,1,0:T(8,128)(2,1)}), bf16[128,1,6,4096]{3,2,1,0:T(8,128)(2,1)}, u32[]{:S(2)}, u32[]{:S(2)}) async-start(bf16[128,1,6,4096]{3,2,1,0:T(8,128)(2,1)} %copy.51), calls=%async_computation.2 | async-start | bytes 16777216 | tf_op jit(solution)/shard_map/all_to_all | solution.py:132
  485.5 0.1 copy.52
  485.6 110.1 %all-to-all-done.1 = bf16[128,1,6,4096]{3,2,1,0:T(8,128)(2,1)} async-done(((bf16[128,1,6,4096]{3,2,1,0:T(8,128)(2,1)}), bf16[128,1,6,4096]{3,2,1,0:T(8,128)(2,1)}, u32[]{:S(2)}, u32[]{:S(2)}) %all-to-all-start.1) | async-done | bytes 6291488 | tf_op jit(solution)/shard_map/all_to_all | solution.py:132
  595.7 10.2 %reshape.292 = bf16[768,4096]{1,0:T(8,128)(2,1)} reshape(bf16[128,1,6,4096]{3,2,1,0:T(8,128)(2,1)} %all-to-all-done.1) | data formatting | bytes 12582912 | tf_op jit(solution)/shard_map/reshape | solution.py:141
  605.9 12.2 %gather_fusion = bf16[512,4096]{1,0:T(8,128)(2,1)} fusion(bf16[768,4096]{1,0:T(8,128)(2,1)} %reshape.292, s32[1024]{0:T(1024)S(1)} %pad_clamp_fusion), kind=kCustom, calls=%fused_computation.1 | custom fusion | bytes 8390656 | tf_op jit(solution)/shard_map/gather | solution.py:142
  618.0 5.7 fusion.27
  623.8 1.0 fusion.58
  (70 shorter events, 0.4 us)
Async XLA Ops:
  6.5 74.1 %all-gather.6.cloned.1.call-start = ((), (), s32[]{:S(2)}) async-start(), calls=%async_computation.4 | async-start | bytes 2129920 | tf_op jit(solution)/shard_map/all_gather | solution.py:48
  8.0 142.7 %all-gather.4.cloned.1.call-start = ((), (), s32[]{:S(2)}) async-start(), calls=%async_computation.3 | async-start | bytes 2129920 | tf_op jit(solution)/shard_map/all_gather | solution.py:47
  8.8 249.7 %all-gather.8.cloned.1.call-start = ((), (), s32[]{:S(2)}) async-start(), calls=%async_computation.5 | async-start | bytes 17039360 | tf_op jit(solution)/shard_map/all_gather | solution.py:100
  9.5 278.6 %reduce-scatter.2.cloned.1.call-start = ((), (), s32[]{:S(2)}) async-start(), calls=%async_computation.6 | async-start | bytes 1572864 | tf_op jit(solution)/shard_map/reduce_scatter | solution.py:103
  258.5 9.2 %copy-start.2 = (s32[64,8]{0,1:T(8,128)S(1)}, s32[64,8]{0,1:T(8,128)}, u32[]{:S(2)}) copy-start(s32[64,8]{0,1:T(8,128)} %param.21) | copy-start | bytes 6148
  258.5 29.6 %copy-start = (bf16[64,4096]{1,0:T(8,128)(2,1)S(1)}, bf16[64,4096]{1,0:T(8,128)(2,1)}, u32[]{:S(2)}) copy-start(bf16[64,4096]{1,0:T(8,128)(2,1)} %param.20) | copy-start | bytes 1572868
  323.4 130.9 %slice-start = ((s8[6291456]{0:T(1024)(128)(4,1)}), s8[4194304]{0:T(1024)(128)(4,1)S(1)}, s32[]{:S(2)}) async-start(s8[6291456]{0:T(1024)(128)(4,1)} %bitcast.162), calls=%async_computation.7 | async-start | bytes 8388608
  431.5 22.8 %slice-start.1 = ((s8[6291456]{0:T(1024)(128)(4,1)}), s8[2097152]{0:T(1024)(128)(4,1)S(1)}, s32[]{:S(2)}) async-start(s8[6291456]{0:T(1024)(128)(4,1)} %bitcast.162), calls=%async_computation.8 | async-start | bytes 4194304
  431.5 35.1 %slice-start.2 = ((s8[6291456]{0:T(1024)(128)(4,1)}), s8[4194304]{0:T(1024)(128)(4,1)S(1)}, s32[]{:S(2)}) async-start(s8[6291456]{0:T(1024)(128)(4,1)} %bitcast.164), calls=%async_computation.9 | async-start | bytes 8388608
  454.3 12.3 %slice-start.3 = ((s8[6291456]{0:T(1024)(128)(4,1)}), s8[2097152]{0:T(1024)(128)(4,1)S(1)}, s32[]{:S(2)}) async-start(s8[6291456]{0:T(1024)(128)(4,1)} %bitcast.164), calls=%async_computation.10 | async-start | bytes 4194304
  478.8 6.7 %copy-start.3 = (f32[64,8]{0,1:T(8,128)S(1)}, f32[64,8]{0,1:T(8,128)}, u32[]{:S(2)}) copy-start(f32[64,8]{0,1:T(8,128)} %param.22) | copy-start | bytes 6148
  478.8 116.8 %all-to-all-start.1 = ((bf16[128,1,6,4096]{3,2,1,0:T(8,128)(2,1)}), bf16[128,1,6,4096]{3,2,1,0:T(8,128)(2,1)}, u32[]{:S(2)}, u32[]{:S(2)}) async-start(bf16[128,1,6,4096]{3,2,1,0:T(8,128)(2,1)} %copy.51), calls=%async_computation.2 | async-start | bytes 16777216 | tf_op jit(solution)/shard_map/all_to_all | solution.py:132
  618.0 5.7 copy-start.1
Sparse Core Ops, SparseCore 0:
  10.2 70.2 all-gather.5
  83.8 66.8 all-gather.3
  153.9 104.5 all-gather.7
  267.8 20.1 reduce-scatter.1
where the time goes:
time: 637 us; the launch traced here: 632 us
  waiting for transfers between devices  364 us (57%)
  blocking collectives  108 us (17%)
  local copies, waits for them, and re-layouts  65.7 us (10%)
  matrix products  57.5 us (9%)
  other arithmetic  14.8 us (2%)
  between operations  13.9 us (2%)
  starting transfers between devices  6.81 us (1%)
    all_to_all x1, waiting for transfers between devices, body(): lax.all_to_all(jnp.einsum('secf,efd->secd', hidden, down_proj, preferred_...  110 us
    all_to_all x1, blocking collectives, body(): lax.all_to_all(shaped, ('ctx', 'tp'), split_axis=0, concat_axis=0, tiled=...  108 us
    all_gather x1, waiting for transfers between devices, body(): lax.all_gather(out_weight, 'ctx', axis=0, tiled=True)  94.5 us
    all_gather x1, waiting for transfers between devices, body(): key_piece = lax.all_gather(rotated_keys, 'ctx', axis=0, tiled=True)  70.1 us
    all_gather x1, waiting for transfers between devices, body(): value_piece = lax.all_gather(value_matrix, 'ctx', axis=0, tiled=True)  68.5 us
    dot_general x1, matrix products, body(): jnp.einsum('secd,edf->secf', incoming, gate_proj, preferred_element_type=...  22.8 us
    scatter x1, local copies, waits for them, and re-layouts, body(): outgoing = jnp.zeros((experts * capacity, model_width), jnp.bfloat16).at[...  22.6 us
    reduce_scatter x1, waiting for transfers between devices, body(): lax.psum_scatter(partial_sum.astype(jnp.bfloat16), 'tp', scatter_dimensio...  19.2 us
  transfers between devices with their start and end apart: 5, of which 5 were waited for; matrix products, arithmetic and copies ran while one was open for 3% of the time, Pallas kernels for 0%

commit v1 on v0

v1 whole, which is shorter than its diff:
```python
import math

import jax
import jax.numpy as jnp
from jax import lax
from jax.experimental import pallas as pl
from jax.experimental.pallas import tpu as pltpu
from jax.sharding import Mesh
from jax.sharding import PartitionSpec as P

HEAD = 128
CAP = 6
ROWS = 64
GROUP = 8
SLOTS = GROUP * CAP
CHUNK = 512
NEG = -1e30
BF16 = jnp.bfloat16
F32 = jnp.float32
AXES = ("zh", "y", "x", "c", "zl")
LINE = ("zh", "c", "zl")
Z = ("zh", "zl")


def rotated(count, step):
    return [(i, (i + step) % count) for i in range(count)]


def flipped(count, bits):
    return [(i, i ^ bits) for i in range(count)]


def attention_kernel(lim, low, high, order, q, kv, kpos, qpos, qstart, out, best, accum):
    scale = math.log2(math.e) / math.sqrt(HEAD)
    heads = q.shape[1] // HEAD
    tokens = q.shape[0]
    best[...] = jnp.full(best.shape, NEG, F32)
    accum[...] = jnp.zeros(accum.shape, F32)

    def update(number, masked):
        begin = pl.multiple_of(number * CHUNK, CHUNK)
        keys = kv[pl.ds(begin, CHUNK), :HEAD]
        values = kv[pl.ds(begin, CHUNK), HEAD:]
        values = jnp.concatenate([values, jnp.ones((CHUNK, HEAD), BF16)], axis=1)
        if masked:
            at = kpos[number]
            allowed = (at <= qpos[...]) & (at >= qstart[...])
        for head in range(heads):
            rows = pl.ds(head * tokens, tokens)
            scores = lax.dot_general(
                q[:, head * HEAD : (head + 1) * HEAD],
                keys,
                (((1,), (1,)), ((), ())),
                preferred_element_type=F32,
            )
            if masked:
                scores = jnp.where(allowed, scores, NEG)
            old = best[rows, :]
            new = jnp.maximum(old, jnp.max(scores, axis=1, keepdims=True))
            factor = jnp.exp2((old - new) * scale)
            expo = jnp.exp2((scores - jnp.concatenate([new] * (CHUNK // HEAD), axis=1)) * scale)
            added = jnp.dot(expo.astype(BF16), values, preferred_element_type=F32)
            accum[rows, :] = accum[rows, :] * jnp.concatenate([factor, factor], axis=1) + added
            best[rows, :] = new

    def step(i, carry):
        number = order[i]
        used = (low[number] <= lim[1]) & (high[number] >= lim[2])
        whole = (high[number] <= lim[0]) & (low[number] >= lim[3])

        @pl.when(used & whole)
        def _():
            update(number, False)

        @pl.when(used & jnp.logical_not(whole))
        def _():
            update(number, True)

        return carry

    lax.fori_loop(0, order.shape[0], step, 0)
    for head in range(heads):
        rows = pl.ds(head * tokens, tokens)
        state = accum[rows, :]
        out[:, head * HEAD : (head + 1) * HEAD] = (state[:, :HEAD] / state[:, HEAD:]).astype(BF16)


def attend(queries, kv, key_pos, low, high, order, query_pos, query_start):
    tokens, width = queries.shape
    heads_a_step = 4
    lim = jnp.stack(
        [query_pos[0], query_pos[-1], jnp.min(query_start), jnp.max(query_start)]
    ).astype(jnp.int32)
    smem = pl.BlockSpec(memory_space=pltpu.SMEM)
    cols = heads_a_step * HEAD
    return pl.pallas_call(
        attention_kernel,
        grid=(width // cols,),
        in_specs=[
            smem,
            smem,
            smem,
            smem,
            pl.BlockSpec((tokens, cols), lambda i: (0, i)),
            pl.BlockSpec(kv.shape, lambda i: (0, 0)),
            pl.BlockSpec(key_pos.shape, lambda i: (0, 0, 0)),
            pl.BlockSpec((tokens, 1), lambda i: (0, 0)),
            pl.BlockSpec((tokens, 1), lambda i: (0, 0)),
        ],
        out_specs=pl.BlockSpec((tokens, cols), lambda i: (0, i)),
        out_shape=jax.ShapeDtypeStruct((tokens, width), BF16),
        scratch_shapes=[
            pltpu.VMEM((heads_a_step * tokens, HEAD), F32),
            pltpu.VMEM((heads_a_step * tokens, 2 * HEAD), F32),
        ],
        compiler_params=pltpu.CompilerParams(vmem_limit_bytes=40 << 20),
        name="attention",
    )(lim, low, high, order, queries, kv, key_pos, query_pos[:, None], query_start[:, None])


def projection_kernel(slot, parts, weight, residual, hidden, accum):
    step = pl.program_id(0)

    @pl.when(step == 0)
    def _():
        accum[...] = residual[...].astype(F32)

    total = accum[...]
    for half in range(2):
        left = jnp.concatenate([parts[slot[2 * block + half]] for block in range(4)], axis=0)
        total = total + jnp.dot(left, weight[half], preferred_element_type=F32)
    accum[...] = total

    @pl.when(step == pl.num_programs(0) - 1)
    def _():
        hidden[...] = total.astype(BF16)


def project(slot, parts, weight, residual):
    steps = 4
    depth = weight.shape[1] // steps
    tokens, width = residual.shape
    return pl.pallas_call(
        projection_kernel,
        grid=(steps,),
        in_specs=[
            pl.BlockSpec(memory_space=pltpu.SMEM),
            pl.BlockSpec((8, parts.shape[1], depth), lambda k: (0, 0, k)),
            pl.BlockSpec((2, depth, width), lambda k: (0, k, 0)),
            pl.BlockSpec((tokens, width), lambda k: (0, 0)),
        ],
        out_specs=pl.BlockSpec((tokens, width), lambda k: (0, 0)),
        out_shape=jax.ShapeDtypeStruct((tokens, width), BF16),
        scratch_shapes=[pltpu.VMEM((tokens, width), F32)],
        compiler_params=pltpu.CompilerParams(vmem_limit_bytes=40 << 20),
        name="projection",
    )(slot, parts, weight, residual)


def slots_of(ids, experts):
    tokens = ids.shape[1]
    expert = lax.broadcasted_iota(jnp.int32, (experts, tokens), 0)
    named = jnp.zeros((experts, tokens), F32)
    for k in range(ids.shape[0]):
        named = named + jnp.where(ids[k : k + 1, :] == expert, 1.0, 0.0)
    first = lax.broadcasted_iota(jnp.int32, (tokens, tokens), 0)
    second = lax.broadcasted_iota(jnp.int32, (tokens, tokens), 1)
    before = (first < second) & (first // ROWS == second // ROWS)
    rank = jnp.dot(
        named.astype(BF16), jnp.where(before, 1.0, 0.0).astype(BF16), preferred_element_type=F32
    )
    block = lax.broadcasted_iota(jnp.int32, (experts, tokens), 1) // ROWS
    return jnp.where(named > 0, rank + (block * CAP).astype(F32), -1.0)


def dispatch_kernel(ids, hidden, out, slots):
    step = pl.program_id(0)
    tokens = hidden.shape[0]
    count = out.shape[0]

    @pl.when(step == 0)
    def _():
        slots[...] = slots_of(ids[...], slots.shape[0])

    row = lax.broadcasted_iota(jnp.int32, (SLOTS, tokens), 0).astype(F32)
    mine = slots[pl.ds(pl.multiple_of(step * count, count), count), :]
    picks = [jnp.where(mine[e : e + 1, :] == row, 1.0, 0.0).astype(BF16) for e in range(count)]
    rows = jnp.dot(jnp.concatenate(picks, axis=0), hidden[...], preferred_element_type=F32)
    out[...] = rows.astype(BF16).reshape(out.shape)


def dispatch(ids, hidden, experts):
    tokens, width = hidden.shape
    count = 8
    return pl.pallas_call(
        dispatch_kernel,
        grid=(experts // count,),
        in_specs=[
            pl.BlockSpec(ids.shape, lambda i: (0, 0)),
            pl.BlockSpec((tokens, width), lambda i: (0, 0)),
        ],
        out_specs=pl.BlockSpec((count, SLOTS, width), lambda i: (i, 0, 0)),
        out_shape=jax.ShapeDtypeStruct((experts, SLOTS, width), BF16),
        scratch_shapes=[pltpu.VMEM((experts, tokens), F32)],
        compiler_params=pltpu.CompilerParams(vmem_limit_bytes=40 << 20),
        name="dispatch",
    )(ids, hidden)


def expert_kernel(rows, gate_w, up_w, down_w, out, gate, up, squares, act):
    step = pl.program_id(0)
    half = pl.num_programs(0) // 2
    width = rows.shape[-1]
    count = act.shape[0]

    @pl.when(step == 0)
    def _():
        gate[...] = jnp.zeros(gate.shape, F32)
        up[...] = jnp.zeros(up.shape, F32)
        squares[...] = jnp.zeros(squares.shape, F32)

    @pl.when(step < half)
    def _():
        block = rows[...].reshape(count, width)
        gate[...] += jnp.dot(block, gate_w[0], preferred_element_type=F32)
        up[...] += jnp.dot(block, up_w[0], preferred_element_type=F32)
        wide = block.astype(F32)
        wide = wide * wide
        total = wide[:, :HEAD]
        for i in range(1, width // HEAD):
            total = total + wide[:, i * HEAD : (i + 1) * HEAD]
        squares[...] += total

    @pl.when(step == half - 1)
    def _():
        mean = jnp.sum(squares[...], axis=1, keepdims=True) / (width * half)
        factor = lax.rsqrt(mean + 1e-06)
        value = gate[...] * factor
        act[...] = (value / (1.0 + jnp.exp(-value)) * (up[...] * factor)).astype(BF16)

    @pl.when(step >= half)
    def _():
        result = jnp.dot(act[...], down_w[0], preferred_element_type=F32)
        out[...] = result.astype(BF16).reshape(out.shape)


def expert(rows, gate_w, up_w, down_w):
    high, groups, low, slots, width = rows.shape
    steps = high * low
    hidden_units = gate_w.shape[2]
    count = groups * slots
    last = steps - 1

    def first(i):
        return jnp.minimum(i, last)

    def second(i):
        return jnp.maximum(i - steps, 0)

    return pl.pallas_call(
        expert_kernel,
        grid=(2 * steps,),
        in_specs=[
            pl.BlockSpec(
                (1, groups, 1, slots, width),
                lambda i: (first(i) // low, 0, lax.rem(first(i), low), 0, 0),
            ),
            pl.BlockSpec((1, width, hidden_units), lambda i: (0, first(i), 0)),
            pl.BlockSpec((1, width, hidden_units), lambda i: (0, first(i), 0)),
            pl.BlockSpec((1, hidden_units, width), lambda i: (0, 0, second(i))),
        ],
        out_specs=pl.BlockSpec(
            (1, groups, 1, slots, width),
            lambda i: (second(i) // low, 0, lax.rem(second(i), low), 0, 0),
        ),
        out_shape=jax.ShapeDtypeStruct(rows.shape, BF16),
        scratch_shapes=[
            pltpu.VMEM((count, hidden_units), F32),
            pltpu.VMEM((count, hidden_units), F32),
            pltpu.VMEM((count, HEAD), F32),
            pltpu.VMEM((count, hidden_units), BF16),
        ],
        compiler_params=pltpu.CompilerParams(vmem_limit_bytes=48 << 20),
        name="expert",
    )(rows, gate_w, up_w, down_w)


def combine_kernel(ids, gates, answers, hidden, out, slots, weights, accum):
    step = pl.program_id(0)
    tokens = hidden.shape[0]
    count = answers.shape[0]
    experts = slots.shape[0]

    @pl.when(step == 0)
    def _():
        slots[...] = slots_of(ids[...], experts)
        number = lax.broadcasted_iota(jnp.int32, (experts, tokens), 0)
        total = jnp.zeros((experts, tokens), F32)
        for k in range(ids.shape[0]):
            total = total + jnp.where(ids[k : k + 1, :] == number, gates[k : k + 1, :], 0.0)
        weights[...] = total
        accum[...] = hidden[...].astype(F32)

    row = lax.broadcasted_iota(jnp.int32, (SLOTS, tokens), 0).astype(F32)
    begin = pl.ds(pl.multiple_of(step * count, count), count)
    mine, scale = slots[begin, :], weights[begin, :]
    picks = [
        jnp.where(mine[e : e + 1, :] == row, scale[e : e + 1, :], 0.0).astype(BF16)
        for e in range(count)
    ]
    total = accum[...] + lax.dot_general(
        jnp.concatenate(picks, axis=0),
        answers[...].reshape(count * SLOTS, answers.shape[2]),
        (((0,), (0,)), ((), ())),
        preferred_element_type=F32,
    )
    accum[...] = total

    @pl.when(step == pl.num_programs(0) - 1)
    def _():
        out[...] = total.astype(BF16)


def combine(ids, gates, answers, hidden):
    tokens, width = hidden.shape
    experts = answers.shape[0]
    count = 8
    return pl.pallas_call(
        combine_kernel,
        grid=(experts // count,),
        in_specs=[
            pl.BlockSpec(ids.shape, lambda i: (0, 0)),
            pl.BlockSpec(gates.shape, lambda i: (0, 0)),
            pl.BlockSpec((count, SLOTS, width), lambda i: (i, 0, 0)),
            pl.BlockSpec((tokens, width), lambda i: (0, 0)),
        ],
        out_specs=pl.BlockSpec((tokens, width), lambda i: (0, 0)),
        out_shape=jax.ShapeDtypeStruct((tokens, width), BF16),
        scratch_shapes=[
            pltpu.VMEM((experts, tokens), F32),
            pltpu.VMEM((experts, tokens), F32),
            pltpu.VMEM((tokens, width), F32),
        ],
        compiler_params=pltpu.CompilerParams(vmem_limit_bytes=40 << 20),
        name="combine",
    )(ids, gates, answers, hidden)


def gather_kv(rotated_keys, value_matrix):
    own = jnp.concatenate([rotated_keys, value_matrix], axis=1)
    tokens = own.shape[0]
    row = jnp.stack([own] + [lax.ppermute(own, "x", rotated(4, k)) for k in range(1, 4)])
    row_other = lax.ppermute(row, "c", flipped(2, 1))
    rest = jnp.concatenate([lax.ppermute(row, ("zh", "y"), rotated(8, k)) for k in range(1, 5)])
    rest_other = lax.ppermute(rest, "c", flipped(2, 1))
    kv = jnp.concatenate([row, row_other, rest, rest_other]).reshape(-1, own.shape[1])
    slab = lax.axis_index(("zh", "y"))
    core = lax.axis_index("c")
    place = (lax.axis_index("x") - jnp.arange(4, dtype=jnp.int32)) % 4
    back = jnp.array([0, 0, 1, 2, 3, 4, 1, 2, 3, 4], jnp.int32)
    side = jnp.array([0, 1, 0, 0, 0, 0, 1, 1, 1, 1], jnp.int32)
    begin = ((slab - back) % 8) * 8 * tokens + (core ^ side) * tokens
    pos = begin[:, None, None] + (place * 2 * tokens)[None, :, None]
    pos = pos + jnp.arange(tokens, dtype=jnp.int32)[None, None, :]
    low = begin.astype(jnp.int32)
    high = (begin + 7 * tokens - 1).astype(jnp.int32)
    return kv, pos.astype(jnp.int32).reshape(10, 1, 4 * tokens), low, high


def gather_attended(own):
    near = lax.ppermute(own, Z, flipped(4, 1))
    far = lax.ppermute(own, Z, flipped(4, 3))
    cut = own.shape[0] // 2
    opposite = jnp.concatenate(
        [
            lax.ppermute(near[:cut], Z, flipped(4, 3)),
            lax.ppermute(far[cut:], Z, flipped(4, 1)),
        ]
    )
    mine = jnp.stack([own, near, opposite, far])
    other = lax.ppermute(mine, "c", flipped(2, 1))
    z, core = lax.axis_index(Z), lax.axis_index("c")
    slot = []
    for zh in range(2):
        for c in range(2):
            for half in range(2):
                slot.append((core ^ c) * 4 + (z ^ (zh * 2 + half)))
    return jnp.concatenate([mine, other]), jnp.stack(slot).astype(jnp.int32)


def body(
    queries,
    rotated_keys,
    value_matrix,
    lengths,
    out_weight,
    residual,
    expert_ids,
    router_gates,
    gate_proj,
    up_proj,
    down_proj,
):
    tokens = queries.shape[0]
    own_rows, model_width = residual.shape
    experts = 2 * 4 * 4 * 2 * 2
    width = model_width // GROUP

    kv, key_pos, low, high = gather_kv(rotated_keys, value_matrix)

    weight_rows = out_weight.shape[0]
    meta = jnp.concatenate([expert_ids.astype(BF16), router_gates.astype(BF16)], axis=1)
    meta = meta.reshape(-1, width)
    used = meta.shape[0]
    meta = jnp.pad(meta, ((0, 16 - used), (0, 0)))
    sent = jnp.concatenate(
        [
            out_weight.reshape(weight_rows, GROUP, width).transpose(1, 0, 2),
            residual.reshape(own_rows, GROUP, width).transpose(1, 0, 2),
            jnp.broadcast_to(meta[None], (GROUP, 16, width)),
        ],
        axis=1,
    )
    got = lax.all_to_all(sent, LINE, split_axis=0, concat_axis=0, tiled=True)
    weight_part = got[:, :weight_rows].reshape(GROUP * weight_rows, width)
    line_residual = got[:, weight_rows : weight_rows + own_rows].reshape(GROUP * own_rows, width)
    meta = got[:, weight_rows + own_rows : weight_rows + own_rows + used]
    meta = meta.reshape(GROUP * own_rows, 16).T
    ids = meta[:8].astype(jnp.int32)
    gates = meta[8:].astype(F32)

    weight = lax.all_gather(weight_part, ("y", "x"), axis=0, tiled=True)
    weight = weight.reshape(16, 2, 2, 2, weight_rows, width).transpose(3, 1, 0, 2, 4, 5)
    weight = weight.reshape(2, model_width // 2, width)

    query_pos = lax.axis_index(("zh", "y", "x", "c")) * tokens + jnp.arange(tokens, dtype=jnp.int32)
    starts = jnp.cumsum(lengths) - lengths
    query_start = jnp.max(
        jnp.where(starts[None, :] <= query_pos[:, None], starts[None, :], 0), axis=1
    ).astype(jnp.int32)
    order = jnp.array([0, 1, 2, 6, 3, 7, 4, 8, 5, 9], jnp.int32)
    attended = attend(queries, kv, key_pos, low, high, order, query_pos, query_start)

    parts, slot = gather_attended(attended)
    hidden = project(slot, parts, weight, line_residual)

    outgoing = dispatch(ids, hidden, experts)
    incoming = lax.all_to_all(outgoing, AXES, split_axis=0, concat_axis=0, tiled=True)
    produced = expert(
        incoming.reshape(2, 16, 4, SLOTS, width), gate_proj, up_proj, down_proj
    ).reshape(experts, SLOTS, width)
    answers = lax.all_to_all(produced, AXES, split_axis=0, concat_axis=0, tiled=True)
    mixed = combine(ids, gates, answers, hidden)
    final = lax.all_to_all(
        mixed.reshape(GROUP, own_rows, width), LINE, split_axis=0, concat_axis=0, tiled=True
    )
    return final.transpose(1, 0, 2).reshape(own_rows, model_width)


def solution(mesh):
    fine = Mesh(mesh.devices.reshape(2, 4, 4, 2, 2), AXES)
    ctx = ("zh", "y", "x", "c")
    both = P(AXES, None)
    in_specs = (
        P(ctx, "zl"),
        P(ctx, "zl"),
        P(ctx, "zl"),
        P(),
        P(("zl",) + ctx, None),
        both,
        both,
        both,
        P(AXES, None, None),
        P(AXES, None, None),
        P(AXES, None, None),
    )
    return jax.shard_map(body, mesh=fine, in_specs=in_specs, out_specs=both, check_vma=False)
```

time: 637 us -> 357 us (0.56)
  waiting for transfers between devices: 364 us -> 31.2 us
  blocking collectives: 108 us -> 201 us
  matrix products: 57.5 us -> 0 us
  local copies, waits for them, and re-layouts: 65.7 us -> 13.2 us
  Pallas kernels: 0 us -> 51.6 us
  starting transfers between devices: 6.81 us -> 31.6 us
  other arithmetic: 14.8 us -> 8.36 us
    all_gather x3 -> x1, waiting for transfers between devices: 233 us -> 0.01 us  [body(): weight = lax.all_gather(weight_part, ('y', 'x'), axis=0, tiled=True)]
    all_to_all x1 -> x0, waiting for transfers between devices: 110 us -> none  [body(): lax.all_to_all(jnp.einsum('secf,efd->secd', hidden, down_proj, preferred_...]
    all_to_all x1 -> x4, blocking collectives: 108 us -> 201 us  [the longest x1 88.1 us: body(): lax.all_to_all(outgoing, AXES, split_axis=0, concat_axis=0, tiled=True)]
    dot_general x8 -> x0, matrix products: 57.5 us -> none  [the longest x1 22.8 us: body(): jnp.einsum('secd,edf->secf', incoming, gate_proj, preferred_element_type=...]
    pallas_call x0 -> x5, Pallas kernels: none -> 51.6 us  [the longest x1 24.9 us: expert(): pl.pallas_call(expert_kernel, grid=(2 * steps,), in_specs=[pl.BlockSpec((...]
    ppermute x0 -> x14, starting transfers between devices: none -> 31.6 us  [the longest x4 7.74 us: gather_kv(): lax.ppermute(row, ('zh', 'y'), rotated(8, k))]
    ppermute x0 -> x14, waiting for transfers between devices: none -> 31.2 us  [the longest x4 14.7 us: gather_kv(): lax.ppermute(row, ('zh', 'y'), rotated(8, k))]
    scatter x1 -> x0, local copies, waits for them, and re-layouts: 22.6 us -> none  [body(): outgoing = jnp.zeros((experts * capacity, model_width), jnp.bfloat16).at[...]
  transfers between devices with their start and end apart: 5 -> 15, of which waited for: 5 -> 10; matrix products, arithmetic and copies ran while one was open for 3% -> 3% of each run, Pallas kernels for 0% -> 2%
where the time goes in v1:
time: 357 us; the launch traced here: 351 us
  blocking collectives  201 us (56%)
  Pallas kernels  51.6 us (14%)
  starting transfers between devices  31.6 us (9%)
  waiting for transfers between devices  31.2 us (9%)
  between operations  13.8 us (4%)
  local copies, waits for them, and re-layouts  13.2 us (4%)
  other arithmetic  8.36 us (2%)
    all_to_all x1, blocking collectives, body(): lax.all_to_all(outgoing, AXES, split_axis=0, concat_axis=0, tiled=True)  88.1 us
    all_to_all x1, blocking collectives, body(): lax.all_to_all(produced, AXES, split_axis=0, concat_axis=0, tiled=True)  81.4 us
    pallas_call x1, Pallas kernels, expert(): pl.pallas_call(expert_kernel, grid=(2 * steps,), in_specs=[pl.BlockSpec((...  24.9 us
    all_to_all x1, blocking collectives, body(): got = lax.all_to_all(sent, LINE, split_axis=0, concat_axis=0, tiled=True)  19.3 us
    ppermute x4, waiting for transfers between devices, gather_kv(): lax.ppermute(row, ('zh', 'y'), rotated(8, k))  14.7 us
    all_to_all x1, blocking collectives, body(): lax.all_to_all(mixed.reshape(GROUP, own_rows, width), LINE, split_axis=0,...  12.3 us
    pallas_call x1, Pallas kernels, combine(): pl.pallas_call(combine_kernel, grid=(experts // count,), in_specs=[pl.Blo...  8.63 us
    ppermute x4, starting transfers between devices, gather_kv(): lax.ppermute(row, ('zh', 'y'), rotated(8, k))  7.74 us
  transfers between devices with their start and end apart: 15, of which 10 were waited for; matrix products, arithmetic and copies ran while one was open for 3% of the time, Pallas kernels for 2%

profile of v1, /device:TPU:5, one launch (start us, length us, event | category | flops | bytes accessed | tf_op | source)
XLA Modules:
  0.0 350.8 jit_solution(9780276600453483933)
XLA Ops:
  6.5 1.1 copy.38
  7.7 0.0 copy-start.6
  7.7 1.0 copy.39
  8.7 0.7 convert_element_type.14
  9.4 0.7 convert_element_type.15
  10.1 0.1 copy.28
  10.2 0.1 reshape.161
  10.3 0.1 pad_maximum_fusion.2
  10.4 19.3 %all_to_all.20 = bf16[8,112,512]{2,1,0:T(8,128)(2,1)S(1)} all-to-all(bf16[8,112,512]{2,1,0:T(8,128)(2,1)S(1)} %pad_maximum_fusion.2), channel_id=1, replica_groups=mesh['zh'=2,'y'=4,'x'=4,'c'=2,'zl'=2] {'zh','c','zl'}, dimensions={0} | all-to-all | bytes 1835008 | tf_op jit(solution)/shard_map/all_to_all | solution.py:424
  29.7 0.7 slice.41
  30.4 0.0 all-gather.2.cloned.1.call-update
  30.5 1.0 collective-permute-start
  31.5 0.5 collective-permute-start.1
  32.0 0.9 collective-permute-start.2
  32.8 0.2 reduce-window.9
  33.0 0.7 select_reduce_fusion.1
  33.7 0.7 reduce_min.9
  34.5 0.1 broadcast_add_fusion.1
  34.6 0.1 add.147
  34.7 0.6 fusion.6
  35.3 0.8 collective-permute-done.1
  36.1 0.1 collective-permute-done.2
  36.2 1.4 collective-permute-start.4
  37.6 2.6 collective-permute-start.5
  40.2 2.5 collective-permute-start.6
  42.7 1.2 collective-permute-start.7
  43.9 2.6 pad_add_fusion.lim
  46.6 0.1 copy.30.qstart
  46.7 3.7 %collective-permute-start.3 = (bf16[4,128,256]{2,1,0:T(8,128)(2,1)S(1)}, bf16[4,128,256]{2,1,0:T(8,128)(2,1)S(1)}, u32[]{:S(2)}, u32[]{:S(2)}) collective-permute-start(bf16[4,128,256]{2,1,0:T(8,128)(2,1)S(1)} %pad_maximum_fusion.3), channel_id=1, source_target_pairs={{0,2},{2,0},{1,3},{3,1},{4,6},{6,4},{5,7},{7,5},{8,10},{10,8},{9,1... | collective-permute-start | bytes 786440 | tf_op jit(solution)/shard_map/ppermute | solution.py:353
  50.4 5.2 %collective-permute-done.5 = bf16[4,128,256]{2,1,0:T(8,128)(2,1)S(1)} collective-permute-done((bf16[4,128,256]{2,1,0:T(8,128)(2,1)S(1)}, bf16[4,128,256]{2,1,0:T(8,128)(2,1)S(1)}, u32[]{:S(2)}, u32[]{:S(2)}) %collective-permute-start.5) | collective-permute-done | bytes 262176 | tf_op jit(solution)/shard_map/ppermute | solution.py:354
  55.6 0.7 collective-permute-done.6
  56.3 8.8 %collective-permute-done.7 = bf16[4,128,256]{2,1,0:T(8,128)(2,1)S(1)} collective-permute-done((bf16[4,128,256]{2,1,0:T(8,128)(2,1)S(1)}, bf16[4,128,256]{2,1,0:T(8,128)(2,1)S(1)}, u32[]{:S(2)}, u32[]{:S(2)}) %collective-permute-start.7) | collective-permute-done | bytes 262176 | tf_op jit(solution)/shard_map/ppermute | solution.py:354
  65.1 0.1 pad_maximum_fusion.1
  65.2 0.0 copy-start.3
  65.2 0.6 collective-permute-start.8
  66.0 2.1 collective-permute-done.8
  68.1 0.1 constant_dynamic-update-slice_fusion.2
  68.2 7.5 %attention.1 = bf16[128,2048]{1,0:T(8,128)(2,1)S(1)} custom-call(s32[4]{0:T(128)S(1)} %pad_add_fusion.lim, s32[10]{0:T(128)S(1)} %get-tuple-element.8.low, s32[10]{0:T(128)S(1)} %get-tuple-element.7.high, s32[10]{0:T(128)S(1)} %copy-done.3, bf16[128,2048]{1,0:T(8,128)(2,1)S(1)} %copy-done.2, bf16[5120,256]{1,0:T(8,128)(2,1)S(1)} %bitcast.65, ...), custom_call_target="tpu_custom_call" | custom-call | tf_op jit(solution)/shard_map/attention/pallas_call | solution.py:96
  75.8 0.2 collective-permute-start.9
  76.0 7.4 %collective-permute-start.11 = (bf16[128,2048]{1,0:T(8,128)(2,1)S(1)}, bf16[128,2048]{1,0:T(8,128)(2,1)S(1)}, u32[]{:S(2)}, u32[]{:S(2)}) collective-permute-start(bf16[128,2048]{1,0:T(8,128)(2,1)S(1)} %attention.1), channel_id=1, source_target_pairs={{0,65},{1,64},{64,1},{65,0},{2,67},{3,66},{66,3},{67,2},{4,69},{5,... | collective-permute-start | bytes 1572872 | tf_op jit(solution)/shard_map/ppermute | solution.py:372
  83.4 5.5 %collective-permute-done.9 = bf16[128,2048]{1,0:T(8,128)(2,1)S(1)} collective-permute-done((bf16[128,2048]{1,0:T(8,128)(2,1)S(1)}, bf16[128,2048]{1,0:T(8,128)(2,1)S(1)}, u32[]{:S(2)}, u32[]{:S(2)}) %collective-permute-start.9) | collective-permute-done | bytes 524320 | tf_op jit(solution)/shard_map/ppermute | solution.py:371
  89.0 6.5 %collective-permute-start.10 = (bf16[64,2048]{1,0:T(8,128)(2,1)S(1)}, bf16[64,2048]{1,0:T(8,128)(2,1)S(1)}, u32[]{:S(2)}, u32[]{:S(2)}) collective-permute-start(bf16[64,2048]{1,0:T(8,128)(2,1)S(1)} %slice.39), channel_id=1, source_target_pairs={{0,65},{1,64},{64,1},{65,0},{2,67},{3,66},{66,3},{67,2},{4,69},{5,... | collective-permute-start | bytes 786440 | tf_op jit(solution)/shard_map/ppermute | solution.py:376
  95.5 0.7 collective-permute-start.12
  96.2 4.7 %collective-permute-done.10 = bf16[64,2048]{1,0:T(8,128)(2,1)S(1)} collective-permute-done((bf16[64,2048]{1,0:T(8,128)(2,1)S(1)}, bf16[64,2048]{1,0:T(8,128)(2,1)S(1)}, u32[]{:S(2)}, u32[]{:S(2)}) %collective-permute-start.10) | collective-permute-done | bytes 262176 | tf_op jit(solution)/shard_map/ppermute | solution.py:376
  100.9 1.0 collective-permute-done.12
  101.9 1.6 pad_maximum_fusion
  103.5 2.4 collective-permute-start.13
  106.0 0.1 stack.74.slot
  106.1 0.1 reshape.162
  106.2 0.7 copy.29
  106.9 0.7 slice_convert_fusion
  107.8 2.3 collective-permute-done.13
  110.1 1.7 constant_dynamic-update-slice_fusion.12.parts
  111.8 2.0 copy-done
  113.8 2.9 copy.31
  116.7 0.5 copy-done.1
  117.3 4.0 %projection.1.hidden = bf16[512,512]{1,0:T(8,128)(2,1)S(1)} custom-call(s32[8]{0:T(128)S(1)} %stack.74.slot, bf16[8,128,2048]{2,1,0:T(8,128)(2,1)S(1)} %copy-done.1, bf16[2,2048,512]{2,1,0:T(8,128)(2,1)S(1)} %bitcast.63, bf16[512,512]{1,0:T(8,128)(2,1)S(1)} %bitcast.67), custom_call_target="tpu_custom_call" | custom-call | tf_op jit(solution)/shard_map/projection/pallas_call | solution.py:143
  121.3 6.5 %dispatch.1 = bf16[128,48,512]{2,1,0:T(8,128)(2,1)S(1)} custom-call(s32[8,512]{1,0:T(8,128)S(1)} %get-tuple-element.10.ids, bf16[512,512]{1,0:T(8,128)(2,1)S(1)} %projection.1.hidden), custom_call_target="tpu_custom_call" | custom-call | tf_op jit(solution)/shard_map/dispatch/pallas_call | solution.py:195
  127.8 88.1 %all_to_all.21 = bf16[128,48,512]{2,1,0:T(8,128)(2,1)} all-to-all(bf16[128,48,512]{2,1,0:T(8,128)(2,1)S(1)} %dispatch.1), channel_id=1, replica_groups=mesh['zh'=2,'y'=4,'x'=4,'c'=2,'zl'=2] {'zh','y','x','c','zl'}, dimensions={0} | all-to-all | bytes 12582912 | tf_op jit(solution)/shard_map/all_to_all | solution.py:448
  215.8 24.9 %expert.1 = bf16[2,16,4,48,512]{4,3,2,1,0:T(8,128)(2,1)} custom-call(bf16[2,16,4,48,512]{4,3,2,1,0:T(8,128)(2,1)} %bitcast.68, bf16[1,4096,768]{2,1,0:T(8,128)(2,1)} %gate_w.1, bf16[1,4096,768]{2,1,0:T(8,128)(2,1)} %up_w.1, bf16[1,768,4096]{2,1,0:T(8,128)(2,1)} %down_w.1), custom_call_target="tpu_custom_call" | custom-call | tf_op jit(solution)/shard_map/expert/pallas_call | solution.py:260
  240.7 81.4 %all_to_all.22.answers = bf16[128,48,512]{2,1,0:T(8,128)(2,1)S(1)} all-to-all(bf16[128,48,512]{2,1,0:T(8,128)(2,1)} %bitcast.69), channel_id=1, replica_groups=mesh['zh'=2,'y'=4,'x'=4,'c'=2,'zl'=2] {'zh','y','x','c','zl'}, dimensions={0} | all-to-all | bytes 12582912 | tf_op jit(solution)/shard_map/all_to_all | solution.py:452
  322.1 8.6 %combine.1 = bf16[512,512]{1,0:T(8,128)(2,1)S(1)} custom-call(s32[8,512]{1,0:T(8,128)S(1)} %get-tuple-element.10.ids, f32[8,512]{1,0:T(8,128)S(1)} %get-tuple-element.9.gates, bf16[128,48,512]{2,1,0:T(8,128)(2,1)S(1)} %all_to_all.22.answers, bf16[512,512]{1,0:T(8,128)(2,1)S(1)} %projection.1.hidden), custom_call_target="tpu_custom_call" | custom-call | tf_op jit(solution)/shard_map/combine/pallas_call | solution.py:328
  330.8 12.3 %all_to_all.23 = bf16[8,64,512]{2,1,0:T(8,128)(2,1)S(1)} all-to-all(bf16[8,64,512]{2,1,0:T(8,128)(2,1)S(1)} %bitcast.66), channel_id=1, replica_groups=mesh['zh'=2,'y'=4,'x'=4,'c'=2,'zl'=2] {'zh','c','zl'}, dimensions={0} | all-to-all | bytes 1048576 | tf_op jit(solution)/shard_map/all_to_all | solution.py:454
  343.1 0.8 copy.35
  (51 shorter events, 0.6 us)
Async XLA Ops:
  6.5 107.3 %all-gather.2.cloned.1.call-start = ((), (), s32[]{:S(2)}) async-start(), calls=%async_computation.4 | async-start | bytes 4456448 | tf_op jit(solution)/shard_map/all_gather | solution.py:432
  7.6 22.8 %copy-start.4 = (bf16[128,128]{1,0:T(8,128)(2,1)S(1)}, bf16[128,128]{1,0:T(8,128)(2,1)}, u32[]{:S(2)}) copy-start(bf16[128,128]{1,0:T(8,128)(2,1)} %param.15) | copy-start | bytes 98308
  7.6 22.8 %copy-start.5 = (bf16[128,128]{1,0:T(8,128)(2,1)S(1)}, bf16[128,128]{1,0:T(8,128)(2,1)}, u32[]{:S(2)}) copy-start(bf16[128,128]{1,0:T(8,128)(2,1)} %param.16) | copy-start | bytes 98308
  7.6 25.2 %copy-start.8 = (s32[8]{0:T(128)S(1)}, s32[8]{0:T(128)}, u32[]{:S(2)}) copy-start(s32[8]{0:T(128)} %param.17) | copy-start | bytes 100
  7.7 26.8 %copy-start.6 = (s32[10]{0:T(128)S(1)}, s32[10]{0:T(128)}, u32[]{:S(2)}) copy-start(s32[10]{0:T(128)} %constant.87.clone) | copy-start | bytes 124
  7.7 26.8 %copy-start.7 = (s32[10]{0:T(128)S(1)}, s32[10]{0:T(128)}, u32[]{:S(2)}) copy-start(s32[10]{0:T(128)} %constant.98) | copy-start | bytes 124
  30.5 4.8 %collective-permute-start = (bf16[128,256]{1,0:T(8,128)(2,1)S(1)}, bf16[128,256]{1,0:T(8,128)(2,1)S(1)}, u32[]{:S(2)}, u32[]{:S(2)}) collective-permute-start(bf16[128,256]{1,0:T(8,128)(2,1)S(1)} %constant_dynamic-update-slice_fusion), channel_id=1, source_target_pairs={{0,4},{4,8},{8,12},{12,0},{1,5},{5,9},{9,13},{13,1},{2,6},{6,10},{... | collective-permute-start | bytes 196616 | tf_op jit(solution)/shard_map/ppermute | solution.py:352
  31.5 4.6 %collective-permute-start.1 = (bf16[128,256]{1,0:T(8,128)(2,1)S(1)}, bf16[128,256]{1,0:T(8,128)(2,1)S(1)}, u32[]{:S(2)}, u32[]{:S(2)}) collective-permute-start(bf16[128,256]{1,0:T(8,128)(2,1)S(1)} %constant_dynamic-update-slice_fusion), channel_id=1, source_target_pairs={{0,8},{4,12},{8,0},{12,4},{1,9},{5,13},{9,1},{13,5},{2,10},{6,14},... | collective-permute-start | bytes 196616 | tf_op jit(solution)/shard_map/ppermute | solution.py:352
  32.0 4.2 %collective-permute-start.2 = (bf16[128,256]{1,0:T(8,128)(2,1)S(1)}, bf16[128,256]{1,0:T(8,128)(2,1)S(1)}, u32[]{:S(2)}, u32[]{:S(2)}) collective-permute-start(bf16[128,256]{1,0:T(8,128)(2,1)S(1)} %constant_dynamic-update-slice_fusion), channel_id=1, source_target_pairs={{0,12},{4,0},{8,4},{12,8},{1,13},{5,1},{9,5},{13,9},{2,14},{6,2},{... | collective-permute-start | bytes 196616 | tf_op jit(solution)/shard_map/ppermute | solution.py:352
  36.2 14.2 %collective-permute-start.4 = (bf16[4,128,256]{2,1,0:T(8,128)(2,1)S(1)}, bf16[4,128,256]{2,1,0:T(8,128)(2,1)S(1)}, u32[]{:S(2)}, u32[]{:S(2)}) collective-permute-start(bf16[4,128,256]{2,1,0:T(8,128)(2,1)S(1)} %pad_maximum_fusion.3), channel_id=1, source_target_pairs={{0,16},{16,32},{32,48},{48,64},{64,80},{80,96},{96,112},{112,0},{1... | collective-permute-start | bytes 786440 | tf_op jit(solution)/shard_map/ppermute | solution.py:354
  37.6 18.0 %collective-permute-start.5 = (bf16[4,128,256]{2,1,0:T(8,128)(2,1)S(1)}, bf16[4,128,256]{2,1,0:T(8,128)(2,1)S(1)}, u32[]{:S(2)}, u32[]{:S(2)}) collective-permute-start(bf16[4,128,256]{2,1,0:T(8,128)(2,1)S(1)} %pad_maximum_fusion.3), channel_id=1, source_target_pairs={{0,32},{16,48},{32,64},{48,80},{64,96},{80,112},{96,0},{112,16},{1... | collective-permute-start | bytes 786440 | tf_op jit(solution)/shard_map/ppermute | solution.py:354
  40.2 16.1 %collective-permute-start.6 = (bf16[4,128,256]{2,1,0:T(8,128)(2,1)S(1)}, bf16[4,128,256]{2,1,0:T(8,128)(2,1)S(1)}, u32[]{:S(2)}, u32[]{:S(2)}) collective-permute-start(bf16[4,128,256]{2,1,0:T(8,128)(2,1)S(1)} %pad_maximum_fusion.3), channel_id=1, source_target_pairs={{0,48},{16,64},{32,80},{48,96},{64,112},{80,0},{96,16},{112,32},{1... | collective-permute-start | bytes 786440 | tf_op jit(solution)/shard_map/ppermute | solution.py:354
  42.7 22.4 %collective-permute-start.7 = (bf16[4,128,256]{2,1,0:T(8,128)(2,1)S(1)}, bf16[4,128,256]{2,1,0:T(8,128)(2,1)S(1)}, u32[]{:S(2)}, u32[]{:S(2)}) collective-permute-start(bf16[4,128,256]{2,1,0:T(8,128)(2,1)S(1)} %pad_maximum_fusion.3), channel_id=1, source_target_pairs={{0,64},{16,80},{32,96},{48,112},{64,0},{80,16},{96,32},{112,48},{1... | collective-permute-start | bytes 786440 | tf_op jit(solution)/shard_map/ppermute | solution.py:354
  46.7 19.1 %collective-permute-start.3 = (bf16[4,128,256]{2,1,0:T(8,128)(2,1)S(1)}, bf16[4,128,256]{2,1,0:T(8,128)(2,1)S(1)}, u32[]{:S(2)}, u32[]{:S(2)}) collective-permute-start(bf16[4,128,256]{2,1,0:T(8,128)(2,1)S(1)} %pad_maximum_fusion.3), channel_id=1, source_target_pairs={{0,2},{2,0},{1,3},{3,1},{4,6},{6,4},{5,7},{7,5},{8,10},{10,8},{9,1... | collective-permute-start | bytes 786440 | tf_op jit(solution)/shard_map/ppermute | solution.py:353
  65.2 3.0 copy-start.2
  65.2 3.0 copy-start.3
  65.2 2.9 collective-permute-start.8
  75.8 13.2 %collective-permute-start.9 = (bf16[128,2048]{1,0:T(8,128)(2,1)S(1)}, bf16[128,2048]{1,0:T(8,128)(2,1)S(1)}, u32[]{:S(2)}, u32[]{:S(2)}) collective-permute-start(bf16[128,2048]{1,0:T(8,128)(2,1)S(1)} %attention.1), channel_id=1, source_target_pairs={{0,1},{1,0},{64,65},{65,64},{2,3},{3,2},{66,67},{67,66},{4,5},{5,4... | collective-permute-start | bytes 1572872 | tf_op jit(solution)/shard_map/ppermute | solution.py:371
  76.0 19.5 %collective-permute-start.11 = (bf16[128,2048]{1,0:T(8,128)(2,1)S(1)}, bf16[128,2048]{1,0:T(8,128)(2,1)S(1)}, u32[]{:S(2)}, u32[]{:S(2)}) collective-permute-start(bf16[128,2048]{1,0:T(8,128)(2,1)S(1)} %attention.1), channel_id=1, source_target_pairs={{0,65},{1,64},{64,1},{65,0},{2,67},{3,66},{66,3},{67,2},{4,69},{5,... | collective-permute-start | bytes 1572872 | tf_op jit(solution)/shard_map/ppermute | solution.py:372
  89.0 11.9 %collective-permute-start.10 = (bf16[64,2048]{1,0:T(8,128)(2,1)S(1)}, bf16[64,2048]{1,0:T(8,128)(2,1)S(1)}, u32[]{:S(2)}, u32[]{:S(2)}) collective-permute-start(bf16[64,2048]{1,0:T(8,128)(2,1)S(1)} %slice.39), channel_id=1, source_target_pairs={{0,65},{1,64},{64,1},{65,0},{2,67},{3,66},{66,3},{67,2},{4,69},{5,... | collective-permute-start | bytes 786440 | tf_op jit(solution)/shard_map/ppermute | solution.py:376
  95.5 6.4 %collective-permute-start.12 = (bf16[64,2048]{1,0:T(8,128)(2,1)S(1)}, bf16[64,2048]{1,0:T(8,128)(2,1)S(1)}, u32[]{:S(2)}, u32[]{:S(2)}) collective-permute-start(bf16[64,2048]{1,0:T(8,128)(2,1)S(1)} %slice.40), channel_id=1, source_target_pairs={{0,1},{1,0},{64,65},{65,64},{2,3},{3,2},{66,67},{67,66},{4,5},{5,4... | collective-permute-start | bytes 786440 | tf_op jit(solution)/shard_map/ppermute | solution.py:377
  103.5 6.5 %collective-permute-start.13 = (bf16[4,128,2048]{2,1,0:T(8,128)(2,1)}, bf16[4,128,2048]{2,1,0:T(8,128)(2,1)}, u32[]{:S(2)}, u32[]{:S(2)}) collective-permute-start(bf16[4,128,2048]{2,1,0:T(8,128)(2,1)} %pad_maximum_fusion), channel_id=1, source_target_pairs={{0,2},{2,0},{1,3},{3,1},{4,6},{6,4},{5,7},{7,5},{8,10},{10,8},{9,1... | collective-permute-start | bytes 6291464 | tf_op jit(solution)/shard_map/ppermute | solution.py:381
  111.8 2.0 copy-start
  113.8 3.4 copy-start.1
Sparse Core Ops, SparseCore 0:
  30.5 55.4 all-gather.1

commit v2 on v1

v2 whole, which is shorter than its diff:
```python
import functools
import math

import jax
import jax.numpy as jnp
from jax import lax
from jax.experimental import pallas as pl
from jax.experimental.pallas import tpu as pltpu
from jax.sharding import Mesh
from jax.sharding import PartitionSpec as P

HEAD = 128
CAP = 6
ROWS = 64
GROUP = 8
SLOTS = GROUP * CAP
CHUNK = 512
EDGE = 640
FIRST, SECOND = 4, 2
NEG = -1e30
BF16 = jnp.bfloat16
F32 = jnp.float32
AXES = ("zh", "y", "x", "c", "zl")
LINE = ("zh", "c", "zl")
Z = ("zh", "zl")


def rotated(count, step):
    return [(i, (i + step) % count) for i in range(count)]


def flipped(count, bits):
    return [(i, i ^ bits) for i in range(count)]


def attention_kernel(lim, low, high, q, kv, other, kpos, qpos, qstart, out, best, accum):
    scale = math.log2(math.e) / math.sqrt(HEAD)
    heads = q.shape[1] // HEAD
    tokens = q.shape[0]
    best[...] = jnp.full(best.shape, NEG, F32)
    accum[...] = jnp.zeros(accum.shape, F32)

    def update(source, begin, count, allowed):
        keys = source[pl.ds(begin, count), :HEAD]
        values = source[pl.ds(begin, count), HEAD:]
        values = jnp.concatenate([values, jnp.ones((count, HEAD), BF16)], axis=1)
        for head in range(heads):
            rows = pl.ds(head * tokens, tokens)
            scores = lax.dot_general(
                q[:, head * HEAD : (head + 1) * HEAD],
                keys,
                (((1,), (1,)), ((), ())),
                preferred_element_type=F32,
            )
            if allowed is not None:
                scores = jnp.where(allowed, scores, NEG)
            old = best[rows, :]
            new = jnp.maximum(old, jnp.max(scores, axis=1, keepdims=True))
            factor = jnp.exp2((old - new) * scale)
            expo = jnp.exp2((scores - jnp.concatenate([new] * (count // HEAD), axis=1)) * scale)
            added = jnp.dot(expo.astype(BF16), values, preferred_element_type=F32)
            accum[rows, :] = accum[rows, :] * jnp.concatenate([factor, factor], axis=1) + added
            best[rows, :] = new

    def inside(at):
        return (at <= qpos[...]) & (at >= qstart[...])

    for side, source in enumerate((kv, other)):
        update(source, 0, EDGE, inside(kpos[side, :, :EDGE]))

    full = (kv.shape[0] - EDGE) // CHUNK
    for side, source in enumerate((kv, other)):

        def step(i, carry, side=side, source=source):
            number = side * full + i
            used = (low[number] <= lim[1]) & (high[number] >= lim[2])
            whole = (high[number] <= lim[0]) & (low[number] >= lim[3])
            begin = pl.multiple_of(EDGE + i * CHUNK, HEAD)

            @pl.when(used & whole)
            def _():
                update(source, begin, CHUNK, None)

            @pl.when(used & jnp.logical_not(whole))
            def _():
                at = kpos[side, :, pl.ds(begin, CHUNK)]
                update(source, begin, CHUNK, inside(at))

            return carry

        lax.fori_loop(0, full, step, 0)

    for head in range(heads):
        rows = pl.ds(head * tokens, tokens)
        state = accum[rows, :]
        out[:, head * HEAD : (head + 1) * HEAD] = (state[:, :HEAD] / state[:, HEAD:]).astype(BF16)


def attend(queries, kv, other, key_pos, low, high, lim, query_pos, query_start):
    tokens, width = queries.shape
    smem = pl.BlockSpec(memory_space=pltpu.SMEM)
    vmem = pl.BlockSpec(memory_space=pltpu.VMEM)
    rows = width // HEAD * tokens
    return pl.pallas_call(
        attention_kernel,
        in_specs=[smem] * 3 + [vmem] * 6,
        out_specs=vmem,
        out_shape=jax.ShapeDtypeStruct((tokens, width), BF16),
        scratch_shapes=[pltpu.VMEM((rows, HEAD), F32), pltpu.VMEM((rows, 2 * HEAD), F32)],
        compiler_params=pltpu.CompilerParams(vmem_limit_bytes=32 << 20),
        cost_estimate=pl.CostEstimate(
            flops=10_000_000_000, bytes_accessed=4_000_000, transcendentals=8_000_000
        ),
        name="attention",
    )(lim, low, high, queries, kv, other, key_pos, query_pos, query_start)


def projection_kernel(steps, *refs):
    slot = refs[0]
    weight, residual, slots, hidden, outgoing, accum = refs[21:]
    step = pl.program_id(0)
    blocks, rows_each, width = residual.shape
    tokens = blocks * rows_each
    count = outgoing.shape[0]

    @pl.when(step < steps)
    def _():
        total = None
        for high in range(2):
            own, own_c, near, near_c, far, far_c, first, first_c, second, second_c = refs[
                1 + high : 21 : 2
            ]
            rows = ((own, own_c, first, second, first_c, second_c), (near, near_c, far, far_c))
            for other in range(2):
                pieces = []
                for x in range(4):
                    for core in range(2):
                        pieces.append(weight[0, x, slot[(high * 2 + core) * 2 + other]])
                part = jnp.dot(
                    jnp.concatenate([ref[...] for ref in rows[other]], axis=0),
                    jnp.concatenate(pieces, axis=0),
                    preferred_element_type=F32,
                )
                total = part if total is None else total + part

        @pl.when(step == 0)
        def _():
            accum[...] = total

        @pl.when(step > 0)
        def _():
            accum[...] += total

    @pl.when(step == steps - 1)
    def _():
        share = tokens // 4
        for block in range(4):
            place = slot[8 + block]
            part = accum[block * share : (block + 1) * share, :]
            base = jnp.concatenate([residual[2 * place], residual[2 * place + 1]], axis=0)
            here = pl.ds(pl.multiple_of(place * share, share), share)
            hidden[here, :] = (base.astype(F32) + part).astype(BF16)

    @pl.when(step >= steps)
    def _():
        row = lax.broadcasted_iota(jnp.int32, (SLOTS, tokens), 0).astype(F32)
        mine = slots[...]
        picks = [jnp.where(mine[e : e + 1, :] == row, 1.0, 0.0).astype(BF16) for e in range(count)]
        sent = jnp.dot(jnp.concatenate(picks, axis=0), hidden[...], preferred_element_type=F32)
        outgoing[...] = sent.astype(BF16).reshape(outgoing.shape)


def project(slot, blocks, weight, residual, slots):
    width = residual.shape[2]
    tokens = residual.shape[0] * residual.shape[1]
    experts = slots.shape[0]
    count = 16
    steps = weight.shape[0]
    depth = blocks[0].shape[1] // (2 * steps)

    def early(k):
        return jnp.minimum(k, steps - 1)

    def late(k):
        return jnp.maximum(k - steps, 0)

    specs = []
    for ref in blocks:
        specs.append(pl.BlockSpec((ref.shape[0], depth), lambda k: (0, early(k))))
        specs.append(pl.BlockSpec((ref.shape[0], depth), lambda k: (0, early(k) + steps)))
    return pl.pallas_call(
        functools.partial(projection_kernel, steps),
        grid=(steps + experts // count,),
        in_specs=[pl.BlockSpec(memory_space=pltpu.SMEM)]
        + specs
        + [
            pl.BlockSpec((1,) + weight.shape[1:], lambda k: (early(k), 0, 0, 0, 0)),
            pl.BlockSpec(residual.shape, lambda k: (0, 0, 0)),
            pl.BlockSpec((count, tokens), lambda k: (late(k), 0)),
        ],
        out_specs=(
            pl.BlockSpec((tokens, width), lambda k: (0, 0)),
            pl.BlockSpec((count, SLOTS, width), lambda k: (late(k), 0, 0)),
        ),
        out_shape=(
            jax.ShapeDtypeStruct((tokens, width), BF16),
            jax.ShapeDtypeStruct((experts, SLOTS, width), BF16),
        ),
        scratch_shapes=[pltpu.VMEM((tokens, width), F32)],
        compiler_params=pltpu.CompilerParams(vmem_limit_bytes=36 << 20),
        name="projection",
    )(slot, *[ref for ref in blocks for _ in range(2)], weight, residual, slots)


def slots_of(ids, experts):
    tokens = ids.shape[1]
    expert = lax.broadcasted_iota(jnp.int32, (experts, tokens), 0)
    named = jnp.zeros((experts, tokens), F32)
    for k in range(ids.shape[0]):
        named = named + jnp.where(ids[k : k + 1, :] == expert, 1.0, 0.0)
    first = lax.broadcasted_iota(jnp.int32, (tokens, tokens), 0)
    second = lax.broadcasted_iota(jnp.int32, (tokens, tokens), 1)
    before = (first < second) & (first // ROWS == second // ROWS)
    rank = jnp.dot(
        named.astype(BF16), jnp.where(before, 1.0, 0.0).astype(BF16), preferred_element_type=F32
    )
    block = lax.broadcasted_iota(jnp.int32, (experts, tokens), 1) // ROWS
    return jnp.where(named > 0, rank + (block * CAP).astype(F32), -1.0)


def routing_kernel(ids, gates, slots, weights):
    experts, tokens = slots.shape
    slots[...] = slots_of(ids[...], experts)
    number = lax.broadcasted_iota(jnp.int32, (experts, tokens), 0)
    total = jnp.zeros((experts, tokens), F32)
    for k in range(ids.shape[0]):
        total = total + jnp.where(ids[k : k + 1, :] == number, gates[k : k + 1, :], 0.0)
    weights[...] = total


def route(ids, gates, experts):
    shape = jax.ShapeDtypeStruct((experts, ids.shape[1]), F32)
    return pl.pallas_call(
        routing_kernel,
        out_shape=(shape, shape),
        compiler_params=pltpu.CompilerParams(vmem_limit_bytes=16 << 20),
        name="routing",
    )(ids, gates)


def expert_kernel(rows, gate_w, up_w, down_w, out, gate, up, squares, act):
    step = pl.program_id(0)
    groups, taken, slots, width = rows.shape[1:]
    count = groups * slots
    model_width = gate_w.shape[1] * FIRST

    @pl.when(step < FIRST)
    def _():
        block = jnp.concatenate(
            [rows[0, :, i].reshape(count, width) for i in range(taken)], axis=1
        )
        gate_part = jnp.dot(block, gate_w[0], preferred_element_type=F32)
        up_part = jnp.dot(block, up_w[0], preferred_element_type=F32)
        wide = block.astype(F32)
        wide = wide * wide
        total = wide[:, :HEAD]
        for i in range(1, taken * width // HEAD):
            total = total + wide[:, i * HEAD : (i + 1) * HEAD]

        @pl.when(step == 0)
        def _():
            gate[...] = gate_part
            up[...] = up_part
            squares[...] = total

        @pl.when(step > 0)
        def _():
            gate[...] += gate_part
            up[...] += up_part
            squares[...] += total

    @pl.when(step == FIRST - 1)
    def _():
        mean = jnp.sum(squares[...], axis=1, keepdims=True) / model_width
        factor = lax.rsqrt(mean + 1e-06)
        value = gate[...] * factor
        act[...] = (value / (1.0 + jnp.exp(-value)) * (up[...] * factor)).astype(BF16)

    @pl.when(step >= FIRST)
    def _():
        result = jnp.dot(act[...], down_w[0], preferred_element_type=F32).astype(BF16)
        for i in range(out.shape[2]):
            out[0, :, i] = result[:, i * width : (i + 1) * width].reshape(groups, slots, width)


def expert(rows, gate_w, up_w, down_w):
    high, groups, low, slots, width = rows.shape
    hidden_units = gate_w.shape[2]
    count = groups * slots
    taken, given = high * low // FIRST, high * low // SECOND

    def first(i):
        return jnp.minimum(i, FIRST - 1)

    def second(i):
        return jnp.maximum(i - FIRST, 0)

    def block_at(i, size):
        return (i * size // low, 0, lax.rem(i, low // size), 0, 0)

    weight_spec = pl.BlockSpec((1, taken * width, hidden_units), lambda i: (0, first(i), 0))
    return pl.pallas_call(
        expert_kernel,
        grid=(FIRST + SECOND,),
        in_specs=[
            pl.BlockSpec((1, groups, taken, slots, width), lambda i: block_at(first(i), taken)),
            weight_spec,
            weight_spec,
            pl.BlockSpec((1, hidden_units, given * width), lambda i: (0, 0, second(i))),
        ],
        out_specs=pl.BlockSpec(
            (1, groups, given, slots, width), lambda i: block_at(second(i), given)
        ),
        out_shape=jax.ShapeDtypeStruct(rows.shape, BF16),
        scratch_shapes=[
            pltpu.VMEM((count, hidden_units), F32),
            pltpu.VMEM((count, hidden_units), F32),
            pltpu.VMEM((count, HEAD), F32),
            pltpu.VMEM((count, hidden_units), BF16),
        ],
        compiler_params=pltpu.CompilerParams(vmem_limit_bytes=56 << 20),
        name="expert",
    )(rows, gate_w, up_w, down_w)


def combine_kernel(slots, weights, answers, hidden, out, accum):
    step = pl.program_id(0)
    tokens = hidden.shape[0]
    count = answers.shape[0]

    @pl.when(step == 0)
    def _():
        accum[...] = hidden[...].astype(F32)

    row = lax.broadcasted_iota(jnp.int32, (SLOTS, tokens), 0).astype(F32)
    mine, scale = slots[...], weights[...]
    picks = [
        jnp.where(mine[e : e + 1, :] == row, scale[e : e + 1, :], 0.0).astype(BF16)
        for e in range(count)
    ]
    total = accum[...] + lax.dot_general(
        jnp.concatenate(picks, axis=0),
        answers[...].reshape(count * SLOTS, answers.shape[2]),
        (((0,), (0,)), ((), ())),
        preferred_element_type=F32,
    )
    accum[...] = total

    @pl.when(step == pl.num_programs(0) - 1)
    def _():
        out[...] = total.astype(BF16)


def combine(slots, weights, answers, hidden):
    tokens, width = hidden.shape
    experts = answers.shape[0]
    count = 16
    return pl.pallas_call(
        combine_kernel,
        grid=(experts // count,),
        in_specs=[
            pl.BlockSpec((count, tokens), lambda i: (i, 0)),
            pl.BlockSpec((count, tokens), lambda i: (i, 0)),
            pl.BlockSpec((count, SLOTS, width), lambda i: (i, 0, 0)),
            pl.BlockSpec((tokens, width), lambda i: (0, 0)),
        ],
        out_specs=pl.BlockSpec((tokens, width), lambda i: (0, 0)),
        out_shape=jax.ShapeDtypeStruct((tokens, width), BF16),
        scratch_shapes=[pltpu.VMEM((tokens, width), F32)],
        compiler_params=pltpu.CompilerParams(vmem_limit_bytes=32 << 20),
        name="combine",
    )(slots, weights, answers, hidden)


def gather_row(rotated_keys, value_matrix):
    own = jnp.concatenate([rotated_keys, value_matrix], axis=1)
    row = [own] + [lax.ppermute(own, "x", rotated(4, k)) for k in range(1, 4)]
    return jnp.concatenate(row)


def shift_row(row):
    return [lax.ppermute(row, ("zh", "y"), rotated(8, k)) for k in range(1, 5)]


def gather_kv(row, shifted):
    tokens = row.shape[0] // 4
    x, core = lax.axis_index("x"), lax.axis_index("c")
    slab = lax.axis_index(("zh", "y"))
    middle, oldest = shifted[:3], shifted[3]
    steps = jnp.arange(1, 4, dtype=jnp.int32)
    near = steps <= x
    picked = jnp.where(jnp.repeat(near, tokens)[:, None], row[tokens:], oldest[tokens:])
    mine = jnp.concatenate([row[:tokens], oldest[:tokens], picked] + middle)
    other = lax.ppermute(mine, "c", flipped(2, 1))

    back = jnp.concatenate(
        [jnp.array([0, 4], jnp.int32), jnp.where(near, 0, 4), jnp.repeat(steps, 4)]
    )
    turn = jnp.array([0, 0, 1, 2, 3] + [0, 1, 2, 3] * 3, jnp.int32)
    begin = ((slab - back) % 8) * 8 + ((x - turn) % 4) * 2
    begin = begin[None, :] + (core ^ jnp.arange(2, dtype=jnp.int32))[:, None]
    pos = begin[:, :, None] * tokens + jnp.arange(tokens, dtype=jnp.int32)
    chunks = begin[:, 5:].reshape(6, 4)
    low = jnp.min(chunks, axis=1) * tokens
    high = jnp.max(chunks, axis=1) * tokens + tokens - 1
    return mine, other, pos.reshape(2, 1, 17 * tokens), low, high


def gather_attended(own):
    def both(block):
        return [block, lax.ppermute(block, "c", flipped(2, 1))]

    near = lax.ppermute(own, Z, flipped(4, 1))
    far = lax.ppermute(own, Z, flipped(4, 3))
    cut = own.shape[0] // 2
    first = lax.ppermute(near[:cut], Z, flipped(4, 3))
    second = lax.ppermute(far[cut:], Z, flipped(4, 1))
    return both(own) + both(near) + both(far) + both(first) + both(second)


def body(
    queries,
    rotated_keys,
    value_matrix,
    lengths,
    out_weight,
    residual,
    expert_ids,
    router_gates,
    gate_proj,
    up_proj,
    down_proj,
):
    tokens = queries.shape[0]
    own_rows, model_width = residual.shape
    experts = 2 * 4 * 4 * 2 * 2
    width = model_width // GROUP

    row = gather_row(rotated_keys, value_matrix)

    weight_rows = out_weight.shape[0]
    meta = jnp.concatenate([expert_ids.astype(BF16), router_gates.astype(BF16)], axis=1)
    meta = meta.reshape(-1, width)
    used = meta.shape[0]
    meta = jnp.pad(meta, ((0, 16 - used), (0, 0)))
    sent = jnp.concatenate(
        [
            out_weight.reshape(weight_rows, GROUP, width).transpose(1, 0, 2),
            residual.reshape(own_rows, GROUP, width).transpose(1, 0, 2),
            jnp.broadcast_to(meta[None], (GROUP, 16, width)),
        ],
        axis=1,
    )
    got = lax.all_to_all(sent, LINE, split_axis=0, concat_axis=0, tiled=True)
    got, row = lax.optimization_barrier((got, row))
    shifted = shift_row(row)
    kv, other, key_pos, low, high = gather_kv(row, shifted)
    weight = lax.all_gather(got[:, :weight_rows], ("y", "x"), axis=0, tiled=True)
    weight = weight.reshape(4, 4, GROUP, weight_rows, width)
    line_residual = got[:, weight_rows : weight_rows + own_rows]
    meta = got[:, weight_rows + own_rows : weight_rows + own_rows + used]
    meta = meta.reshape(GROUP * own_rows, 16).T
    ids = meta[:8].astype(jnp.int32)
    gates = meta[8:].astype(F32)
    slots, weights = route(ids, gates, experts)

    query_pos = lax.axis_index(("zh", "y", "x", "c")) * tokens + jnp.arange(tokens, dtype=jnp.int32)
    starts = jnp.cumsum(lengths) - lengths
    query_start = jnp.max(
        jnp.where(starts[None, :] <= query_pos[:, None], starts[None, :], 0), axis=1
    ).astype(jnp.int32)
    lim = jnp.stack([query_pos[0], query_pos[-1], query_start[0], query_start[-1]])
    line_residual, slots, weights, queries = lax.optimization_barrier(
        (line_residual, slots, weights, queries)
    )
    attended = attend(
        queries, kv, other, key_pos, low, high, lim, query_pos[:, None], query_start[:, None]
    )

    zl, core, zh = lax.axis_index("zl"), lax.axis_index("c"), lax.axis_index("zh")
    halves = []
    for high_part in range(2):
        for c in range(2):
            for k in range(2):
                halves.append((high_part * 2 + c) * 2 + (zl ^ k))
    places = [(zh ^ h) * 2 + (core ^ c) for h in range(2) for c in range(2)]
    table = jnp.stack(halves + places).astype(jnp.int32)
    hidden, outgoing = project(table, gather_attended(attended), weight, line_residual, slots)
    incoming = lax.all_to_all(outgoing, AXES, split_axis=0, concat_axis=0, tiled=True)
    produced = expert(
        incoming.reshape(2, 16, 4, SLOTS, width), gate_proj, up_proj, down_proj
    ).reshape(experts, SLOTS, width)
    answers = lax.all_to_all(produced, AXES, split_axis=0, concat_axis=0, tiled=True)
    mixed = combine(slots, weights, answers, hidden)
    final = lax.all_to_all(
        mixed.reshape(GROUP, own_rows, width), LINE, split_axis=0, concat_axis=0, tiled=True
    )
    return final.transpose(1, 0, 2).reshape(own_rows, model_width)


def solution(mesh):
    fine = Mesh(mesh.devices.reshape(2, 4, 4, 2, 2), AXES)
    ctx = ("zh", "y", "x", "c")
    both = P(AXES, None)
    in_specs = (
        P(ctx, "zl"),
        P(ctx, "zl"),
        P(ctx, "zl"),
        P(),
        P(("zl",) + ctx, None),
        both,
        both,
        both,
        P(AXES, None, None),
        P(AXES, None, None),
        P(AXES, None, None),
    )
    return jax.shard_map(body, mesh=fine, in_specs=in_specs, out_specs=both, check_vma=False)
```

time: 357 us -> 332 us (0.930); the launches traced: 351 us -> 331 us
  blocking collectives: 201 us -> 175 us
  waiting for transfers between devices: 31.2 us -> 45.6 us
  Pallas kernels: 51.6 us -> 47.3 us
    all_to_all x1 -> x0, blocking collectives: 19.3 us -> none  [body(): got = lax.all_to_all(sent, LINE, split_axis=0, concat_axis=0, tiled=True)]
    ppermute x1, waiting for transfers between devices: 0.01 us -> 10.8 us  [gather_attended(): far = lax.ppermute(own, Z, flipped(4, 3))]
    all_to_all x1, blocking collectives: 88.1 us -> 80.8 us  [body(): lax.all_to_all(outgoing, AXES, split_axis=0, concat_axis=0, tiled=True)]
    all_to_all x0 -> x1, waiting for transfers between devices: none -> 6.67 us  [body(): got = lax.all_to_all(sent, LINE, split_axis=0, concat_axis=0, tiled=True)]
    all_to_all x0 -> x1, starting transfers between devices: none -> 6.12 us  [body(): got = lax.all_to_all(sent, LINE, split_axis=0, concat_axis=0, tiled=True)]
    ppermute x12 -> x15, starting transfers between devices: 23.9 us -> 18.3 us  [the longest x4 6.54 us: shift_row(): return [lax.ppermute(row, ('zh', 'y'), rotated(8, k)) for k in range(1, 5)]]
    ppermute x1, waiting for transfers between devices: 5.53 us -> 0.44 us  [gather_attended(): near = lax.ppermute(own, Z, flipped(4, 1))]
    ppermute x12 -> x15, waiting for transfers between devices: 25.6 us -> 27.7 us  [the longest x4 19 us: shift_row(): return [lax.ppermute(row, ('zh', 'y'), rotated(8, k)) for k in range(1, 5)]]
  transfers between devices with their start and end apart: 15 -> 19, of which waited for: 10 -> 9; matrix products, arithmetic and copies ran while one was open for 3% -> 2% of each run, Pallas kernels for 2% -> 2%
where the time goes in v2:
time: 332 us; the launch traced here: 331 us
  blocking collectives  175 us (53%)
  Pallas kernels  47.3 us (14%)
  waiting for transfers between devices  45.6 us (14%)
  starting transfers between devices  32.8 us (10%)
  between operations  13.7 us (4%)
  local copies, waits for them, and re-layouts  10.8 us (3%)
  other arithmetic  5.78 us (2%)
    all_to_all x1, blocking collectives, body(): lax.all_to_all(produced, AXES, split_axis=0, concat_axis=0, tiled=True)  81.4 us
    all_to_all x1, blocking collectives, body(): lax.all_to_all(outgoing, AXES, split_axis=0, concat_axis=0, tiled=True)  80.8 us
    pallas_call x1, Pallas kernels, expert(): pl.pallas_call(expert_kernel, grid=(FIRST + SECOND,), in_specs=[pl.BlockS...  23.8 us
    ppermute x4, waiting for transfers between devices, shift_row(): return [lax.ppermute(row, ('zh', 'y'), rotated(8, k)) for k in range(1, 5)]  19 us
    all_to_all x1, blocking collectives, body(): lax.all_to_all(mixed.reshape(GROUP, own_rows, width), LINE, split_axis=0,...  12.3 us
    ppermute x1, waiting for transfers between devices, gather_attended(): far = lax.ppermute(own, Z, flipped(4, 3))  10.8 us
    pallas_call x1, Pallas kernels, project(): pl.pallas_call(functools.partial(projection_kernel, steps), grid=(steps +...  10.5 us
    ppermute x1, starting transfers between devices, gather_attended(): far = lax.ppermute(own, Z, flipped(4, 3))  8.06 us
  transfers between devices with their start and end apart: 19, of which 9 were waited for; matrix products, arithmetic and copies ran while one was open for 2% of the time, Pallas kernels for 2%

profile of v2, /device:TPU:5, one launch (start us, length us, event | category | flops | bytes accessed | tf_op | source)
XLA Modules:
  0.0 330.6 jit_solution(16720904312683892859)
XLA Ops:
  6.5 0.7 convert_element_type.14
  7.2 0.7 convert_element_type.15
  7.9 0.1 copy.40
  8.0 0.1 reshape.138
  8.1 1.0 copy.52
  9.1 1.1 copy.51
  10.2 1.0 pad_maximum_fusion
  11.2 6.1 %all-to-all-start = ((bf16[8,112,512]{2,1,0:T(8,128)(2,1)}), bf16[8,112,512]{2,1,0:T(8,128)(2,1)S(1)}, u32[]{:S(2)}, u32[]{:S(2)}) async-start(bf16[8,112,512]{2,1,0:T(8,128)(2,1)} %pad_maximum_fusion), calls=%async_computation | async-start | bytes 1835008 | tf_op jit(solution)/shard_map/all_to_all | solution.py:464
  17.5 0.3 collective-permute-start.2
  17.8 2.5 collective-permute-start.1
  20.2 1.0 collective-permute-done.2
  21.2 1.5 collective-permute-done.1
  22.7 1.7 collective-permute-done
  24.4 6.7 %all-to-all-done = bf16[8,112,512]{2,1,0:T(8,128)(2,1)S(1)} async-done(((bf16[8,112,512]{2,1,0:T(8,128)(2,1)}), bf16[8,112,512]{2,1,0:T(8,128)(2,1)S(1)}, u32[]{:S(2)}, u32[]{:S(2)}) %all-to-all-start) | async-done | bytes 917536 | tf_op jit(solution)/shard_map/all_to_all | solution.py:464
  31.1 0.8 slice.63
  31.9 0.1 broadcast_in_dim.55
  32.0 0.1 reshape.142
  32.1 0.1 fusion.3
  32.2 0.1 broadcast_multiply_fusion
  32.3 0.1 slice.56
  32.3 0.1 reshape.143
  32.4 0.2 reduce-window.9
  32.6 0.1 fusion.6
  32.8 0.1 select_reduce_fusion
  32.9 0.7 fusion.7
  33.5 0.1 broadcast_bitcast_fusion
  33.6 0.6 collective-permute-start.3
  34.2 2.6 pad_add_fusion.lim
  36.8 0.1 add.150
  36.9 0.1 copy.44.qstart
  37.0 2.8 collective-permute-start.6
  39.8 2.4 collective-permute-start.5
  42.3 0.7 collective-permute-start.4
  43.0 0.1 fusion
  43.1 19.0 %collective-permute-done.4 = bf16[512,256]{1,0:T(8,128)(2,1)S(1)} collective-permute-done((bf16[512,256]{1,0:T(8,128)(2,1)S(1)}, bf16[512,256]{1,0:T(8,128)(2,1)S(1)}, u32[]{:S(2)}, u32[]{:S(2)}) %collective-permute-start.4) | collective-permute-done | bytes 262176 | tf_op jit(solution)/shard_map/ppermute | solution.py:392
  62.2 0.7 collective-permute-start.7
  63.0 1.1 slice.48.refs_22_
  64.1 0.1 reshape.139
  64.2 0.1 copy.41
  64.3 0.9 routing.1
  65.3 0.7 copy-done.1
  66.0 1.2 copy-done.4
  67.2 7.0 %attention.1.refs_1_.refs_2_ = bf16[128,2048]{1,0:T(8,128)(2,1)S(1)} custom-call(s32[4]{0:T(128)S(1)} %pad_add_fusion.lim, s32[6]{0:T(128)S(1)} %get-tuple-element.38.low, s32[6]{0:T(128)S(1)} %get-tuple-element.37.high, bf16[128,2048]{1,0:T(8,128)(2,1)S(1)} %copy-done.5, bf16[2176,256]{1,0:T(8,128)(2,1)S(1)} %copy-done.4, ...), custom_call_target="tpu_custom_call" | custom-call | flops 10000000000 | bytes 4000000 | tf_op jit(solution)/shard_map/attention/pallas_call | solution.py:104
  74.2 8.1 %collective-permute-start.11 = (bf16[128,2048]{1,0:T(8,128)(2,1)S(1)}, bf16[128,2048]{1,0:T(8,128)(2,1)S(1)}, u32[]{:S(2)}, u32[]{:S(2)}) collective-permute-start(bf16[128,2048]{1,0:T(8,128)(2,1)S(1)} %attention.1.refs_1_.refs_2_), channel_id=1, source_target_pairs={{0,65},{1,64},{64,1},{65,0},{2,67},{3,66},{66,3},{67,2},{4,69},{5,... | collective-permute-start | bytes 1572872 | tf_op jit(solution)/shard_map/ppermute | solution.py:424
  82.3 0.3 collective-permute-start.9
  82.6 0.9 collective-permute-start.8
  83.5 10.8 %collective-permute-done.11.refs_9_.refs_10_ = bf16[128,2048]{1,0:T(8,128)(2,1)S(1)} collective-permute-done((bf16[128,2048]{1,0:T(8,128)(2,1)S(1)}, bf16[128,2048]{1,0:T(8,128)(2,1)S(1)}, u32[]{:S(2)}, u32[]{:S(2)}) %collective-permute-start.11) | collective-permute-done | bytes 524320 | tf_op jit(solution)/shard_map/ppermute | solution.py:424
  94.3 0.4 collective-permute-start.15
  94.7 0.4 collective-permute-done.9.refs_5_.refs_6_
  95.2 1.7 collective-permute-start.13
  96.9 1.5 collective-permute-start.12
  98.4 3.1 collective-permute-done.15.refs_17_.refs_18_
  101.5 1.8 collective-permute-start.16
  103.2 2.0 collective-permute-start.14
  105.3 0.1 stack.54.refs_0_
  105.4 1.4 collective-permute-done.14.refs_15_.refs_16_
  106.8 2.2 copy-done
  109.0 10.5 %projection.1 = (bf16[512,512]{1,0:T(8,128)(2,1)S(1)}, bf16[128,48,512]{2,1,0:T(8,128)(2,1)S(1)}) custom-call(s32[12]{0:T(128)S(1)} %stack.54.refs_0_, bf16[128,2048]{1,0:T(8,128)(2,1)S(1)} %attention.1.refs_1_.refs_2_, bf16[128,2048]{1,0:T(8,128)(2,1)S(1)} %attention.1.refs_1_.refs_2_, bf16[128,2048]{1,0:T(8,128)(2,1)S(1)} %collective-permute-done.8.refs_3_.refs_4_, ...), custom_call_target="tpu_custom_call" | custom-call | tf_op jit(solution)/shard_map/projection/pallas_call | solution.py:191
  119.5 80.8 %all_to_all.20 = bf16[128,48,512]{2,1,0:T(8,128)(2,1)} all-to-all(bf16[128,48,512]{2,1,0:T(8,128)(2,1)S(1)} %get-tuple-element.23), channel_id=1, replica_groups=mesh['zh'=2,'y'=4,'x'=4,'c'=2,'zl'=2] {'zh','y','x','c','zl'}, dimensions={0} | all-to-all | bytes 12582912 | tf_op jit(solution)/shard_map/all_to_all | solution.py:499
  200.3 23.8 %expert.1 = bf16[2,16,4,48,512]{4,3,2,1,0:T(8,128)(2,1)} custom-call(bf16[2,16,4,48,512]{4,3,2,1,0:T(8,128)(2,1)} %bitcast.44, bf16[1,4096,768]{2,1,0:T(8,128)(2,1)} %gate_w.1, bf16[1,4096,768]{2,1,0:T(8,128)(2,1)} %up_w.1, bf16[1,768,4096]{2,1,0:T(8,128)(2,1)} %down_w.1), custom_call_target="tpu_custom_call" | custom-call | tf_op jit(solution)/shard_map/expert/pallas_call | solution.py:312
  224.1 81.4 %all_to_all.21.answers = bf16[128,48,512]{2,1,0:T(8,128)(2,1)S(1)} all-to-all(bf16[128,48,512]{2,1,0:T(8,128)(2,1)} %bitcast.45), channel_id=1, replica_groups=mesh['zh'=2,'y'=4,'x'=4,'c'=2,'zl'=2] {'zh','y','x','c','zl'}, dimensions={0} | all-to-all | bytes 12582912 | tf_op jit(solution)/shard_map/all_to_all | solution.py:503
  305.6 5.1 %combine.1 = bf16[512,512]{1,0:T(8,128)(2,1)S(1)} custom-call(f32[128,512]{1,0:T(8,128)S(1)} %get-tuple-element.18.refs_23_.slots, f32[128,512]{1,0:T(8,128)S(1)} %copy-done.2, bf16[128,48,512]{2,1,0:T(8,128)(2,1)S(1)} %all_to_all.21.answers, bf16[512,512]{1,0:T(8,128)(2,1)S(1)} %get-tuple-element.24.hidden), custom_call_target="tpu_custom_call" | custom-call | tf_op jit(solution)/shard_map/combine/pallas_call | solution.py:368
  310.7 12.3 %all_to_all.22 = bf16[8,64,512]{2,1,0:T(8,128)(2,1)S(1)} all-to-all(bf16[8,64,512]{2,1,0:T(8,128)(2,1)S(1)} %bitcast.43), channel_id=1, replica_groups=mesh['zh'=2,'y'=4,'x'=4,'c'=2,'zl'=2] {'zh','c','zl'}, dimensions={0} | all-to-all | bytes 1048576 | tf_op jit(solution)/shard_map/all_to_all | solution.py:505
  323.0 0.8 copy.48
  (60 shorter events, 0.4 us)
Async XLA Ops:
  11.2 6.2 %copy-start.7 = (bf16[128,128]{1,0:T(8,128)(2,1)S(1)}, bf16[128,128]{1,0:T(8,128)(2,1)}, u32[]{:S(2)}) copy-start(bf16[128,128]{1,0:T(8,128)(2,1)} %param.14) | copy-start | bytes 98308
  11.2 6.2 %copy-start.8 = (bf16[128,128]{1,0:T(8,128)(2,1)S(1)}, bf16[128,128]{1,0:T(8,128)(2,1)}, u32[]{:S(2)}) copy-start(bf16[128,128]{1,0:T(8,128)(2,1)} %param.15) | copy-start | bytes 98308
  11.2 19.9 %all-to-all-start = ((bf16[8,112,512]{2,1,0:T(8,128)(2,1)}), bf16[8,112,512]{2,1,0:T(8,128)(2,1)S(1)}, u32[]{:S(2)}, u32[]{:S(2)}) async-start(bf16[8,112,512]{2,1,0:T(8,128)(2,1)} %pad_maximum_fusion), calls=%async_computation | async-start | bytes 1835008 | tf_op jit(solution)/shard_map/all_to_all | solution.py:464
  17.4 14.7 %copy-start.9 = (s32[17]{0:T(128)S(1)}, s32[17]{0:T(128)}, u32[]{:S(2)}) copy-start(s32[17]{0:T(128)} %constant.90) | copy-start | bytes 208
  17.4 15.1 %copy-start.10 = (s32[8]{0:T(128)S(1)}, s32[8]{0:T(128)}, u32[]{:S(2)}) copy-start(s32[8]{0:T(128)} %param.16) | copy-start | bytes 100
  17.4 89.4 %all-gather.2.cloned.1.call-start = ((), (), s32[]{:S(2)}) async-start(), calls=%async_computation.4 | async-start | bytes 4456448 | tf_op jit(solution)/shard_map/all_gather | solution.py:468
  17.5 3.8 %collective-permute-start.2 = (bf16[128,256]{1,0:T(8,128)(2,1)S(1)}, bf16[128,256]{1,0:T(8,128)(2,1)S(1)}, u32[]{:S(2)}, u32[]{:S(2)}) collective-permute-start(bf16[128,256]{1,0:T(8,128)(2,1)S(1)} %constant_dynamic-update-slice_fusion), channel_id=1, source_target_pairs={{0,12},{4,0},{8,4},{12,8},{1,13},{5,1},{9,5},{13,9},{2,14},{6,2},{... | collective-permute-start | bytes 196616 | tf_op jit(solution)/shard_map/ppermute | solution.py:387
  17.8 4.9 %collective-permute-start.1 = (bf16[128,256]{1,0:T(8,128)(2,1)S(1)}, bf16[128,256]{1,0:T(8,128)(2,1)S(1)}, u32[]{:S(2)}, u32[]{:S(2)}) collective-permute-start(bf16[128,256]{1,0:T(8,128)(2,1)S(1)} %constant_dynamic-update-slice_fusion), channel_id=1, source_target_pairs={{0,8},{4,12},{8,0},{12,4},{1,9},{5,13},{9,1},{13,5},{2,10},{6,14},... | collective-permute-start | bytes 196616 | tf_op jit(solution)/shard_map/ppermute | solution.py:387
  20.2 4.2 %collective-permute-start = (bf16[128,256]{1,0:T(8,128)(2,1)S(1)}, bf16[128,256]{1,0:T(8,128)(2,1)S(1)}, u32[]{:S(2)}, u32[]{:S(2)}) collective-permute-start(bf16[128,256]{1,0:T(8,128)(2,1)S(1)} %constant_dynamic-update-slice_fusion), channel_id=1, source_target_pairs={{0,4},{4,8},{8,12},{12,0},{1,5},{5,9},{9,13},{13,1},{2,6},{6,10},{... | collective-permute-start | bytes 196616 | tf_op jit(solution)/shard_map/ppermute | solution.py:387
  31.1 31.9 %copy-start.6 = (bf16[8,112,512]{2,1,0:T(8,128)(2,1)}, bf16[8,112,512]{2,1,0:T(8,128)(2,1)S(1)}, u32[]{:S(2)}) copy-start(bf16[8,112,512]{2,1,0:T(8,128)(2,1)S(1)} %all-to-all-done) | copy-start | bytes 2752516
  33.6 9.4 %collective-permute-start.3 = (bf16[512,256]{1,0:T(8,128)(2,1)S(1)}, bf16[512,256]{1,0:T(8,128)(2,1)S(1)}, u32[]{:S(2)}, u32[]{:S(2)}) collective-permute-start(bf16[512,256]{1,0:T(8,128)(2,1)S(1)} %pad_maximum_fusion.1), channel_id=1, source_target_pairs={{0,64},{16,80},{32,96},{48,112},{64,0},{80,16},{96,32},{112,48},{1... | collective-permute-start | bytes 786440 | tf_op jit(solution)/shard_map/ppermute | solution.py:392
  37.0 25.1 %collective-permute-start.6 = (bf16[512,256]{1,0:T(8,128)(2,1)S(1)}, bf16[512,256]{1,0:T(8,128)(2,1)S(1)}, u32[]{:S(2)}, u32[]{:S(2)}) collective-permute-start(bf16[512,256]{1,0:T(8,128)(2,1)S(1)} %pad_maximum_fusion.1), channel_id=1, source_target_pairs={{0,48},{16,64},{32,80},{48,96},{64,112},{80,0},{96,16},{112,32},{1... | collective-permute-start | bytes 786440 | tf_op jit(solution)/shard_map/ppermute | solution.py:392
  39.8 22.3 %collective-permute-start.5 = (bf16[512,256]{1,0:T(8,128)(2,1)S(1)}, bf16[512,256]{1,0:T(8,128)(2,1)S(1)}, u32[]{:S(2)}, u32[]{:S(2)}) collective-permute-start(bf16[512,256]{1,0:T(8,128)(2,1)S(1)} %pad_maximum_fusion.1), channel_id=1, source_target_pairs={{0,32},{16,48},{32,64},{48,80},{64,96},{80,112},{96,0},{112,16},{1... | collective-permute-start | bytes 786440 | tf_op jit(solution)/shard_map/ppermute | solution.py:392
  42.3 19.8 %collective-permute-start.4 = (bf16[512,256]{1,0:T(8,128)(2,1)S(1)}, bf16[512,256]{1,0:T(8,128)(2,1)S(1)}, u32[]{:S(2)}, u32[]{:S(2)}) collective-permute-start(bf16[512,256]{1,0:T(8,128)(2,1)S(1)} %pad_maximum_fusion.1), channel_id=1, source_target_pairs={{0,16},{16,32},{32,48},{48,64},{64,80},{80,96},{96,112},{112,0},{1... | collective-permute-start | bytes 786440 | tf_op jit(solution)/shard_map/ppermute | solution.py:392
  62.2 3.8 %copy-start.5 = (bf16[128,2048]{1,0:T(8,128)(2,1)S(1)}, bf16[128,2048]{1,0:T(8,128)(2,1)}, u32[]{:S(2)}) copy-start(bf16[128,2048]{1,0:T(8,128)(2,1)} %q) | copy-start | bytes 1572868
  62.2 3.8 %copy-start.3 = (bf16[2176,256]{1,0:T(8,128)(2,1)}, bf16[2176,256]{1,0:T(8,128)(2,1)S(1)}, u32[]{:S(2)}) copy-start(bf16[2176,256]{1,0:T(8,128)(2,1)S(1)} %constant_dynamic-update-slice_fusion.2.kv) | copy-start | bytes 3342340
  62.2 3.8 %collective-permute-start.7 = (bf16[2176,256]{1,0:T(8,128)(2,1)S(1)}, bf16[2176,256]{1,0:T(8,128)(2,1)}, u32[]{:S(2)}, u32[]{:S(2)}) collective-permute-start(bf16[2176,256]{1,0:T(8,128)(2,1)S(1)} %constant_dynamic-update-slice_fusion.2.kv), channel_id=1, source_target_pairs={{0,2},{2,0},{1,3},{3,1},{4,6},{6,4},{5,7},{7,5},{8,10},{10,8},{9,1... | collective-permute-start | bytes 3342344 | tf_op jit(solution)/shard_map/ppermute | solution.py:404
  65.3 0.7 copy-start.1
  66.0 1.2 copy-start.4
  74.2 20.1 %collective-permute-start.11 = (bf16[128,2048]{1,0:T(8,128)(2,1)S(1)}, bf16[128,2048]{1,0:T(8,128)(2,1)S(1)}, u32[]{:S(2)}, u32[]{:S(2)}) collective-permute-start(bf16[128,2048]{1,0:T(8,128)(2,1)S(1)} %attention.1.refs_1_.refs_2_), channel_id=1, source_target_pairs={{0,65},{1,64},{64,1},{65,0},{2,67},{3,66},{66,3},{67,2},{4,69},{5,... | collective-permute-start | bytes 1572872 | tf_op jit(solution)/shard_map/ppermute | solution.py:424
  82.3 12.8 %collective-permute-start.9 = (bf16[128,2048]{1,0:T(8,128)(2,1)S(1)}, bf16[128,2048]{1,0:T(8,128)(2,1)S(1)}, u32[]{:S(2)}, u32[]{:S(2)}) collective-permute-start(bf16[128,2048]{1,0:T(8,128)(2,1)S(1)} %attention.1.refs_1_.refs_2_), channel_id=1, source_target_pairs={{0,1},{1,0},{64,65},{65,64},{2,3},{3,2},{66,67},{67,66},{4,5},{5,4... | collective-permute-start | bytes 1572872 | tf_op jit(solution)/shard_map/ppermute | solution.py:423
  82.6 22.8 %collective-permute-start.8 = (bf16[128,2048]{1,0:T(8,128)(2,1)S(1)}, bf16[128,2048]{1,0:T(8,128)(2,1)S(1)}, u32[]{:S(2)}, u32[]{:S(2)}) collective-permute-start(bf16[128,2048]{1,0:T(8,128)(2,1)S(1)} %attention.1.refs_1_.refs_2_), channel_id=1, source_target_pairs={{0,2},{2,0},{1,3},{3,1},{4,6},{6,4},{5,7},{7,5},{8,10},{10,8},{9,1... | collective-permute-start | bytes 1572872 | tf_op jit(solution)/shard_map/ppermute | solution.py:421
  94.3 7.1 %collective-permute-start.15 = (bf16[64,2048]{1,0:T(8,128)(2,1)S(1)}, bf16[64,2048]{1,0:T(8,128)(2,1)}, u32[]{:S(2)}, u32[]{:S(2)}) collective-permute-start(bf16[64,2048]{1,0:T(8,128)(2,1)S(1)} %slice.69), channel_id=1, source_target_pairs={{0,1},{1,0},{64,65},{65,64},{2,3},{3,2},{66,67},{67,66},{4,5},{5,4... | collective-permute-start | bytes 786440 | tf_op jit(solution)/shard_map/ppermute | solution.py:427
  95.2 8.1 %collective-permute-start.13 = (bf16[64,2048]{1,0:T(8,128)(2,1)S(1)}, bf16[64,2048]{1,0:T(8,128)(2,1)}, u32[]{:S(2)}, u32[]{:S(2)}) collective-permute-start(bf16[64,2048]{1,0:T(8,128)(2,1)S(1)} %slice.68), channel_id=1, source_target_pairs={{0,65},{1,64},{64,1},{65,0},{2,67},{3,66},{66,3},{67,2},{4,69},{5,... | collective-permute-start | bytes 786440 | tf_op jit(solution)/shard_map/ppermute | solution.py:426
  96.9 8.5 %collective-permute-start.12 = (bf16[128,2048]{1,0:T(8,128)(2,1)S(1)}, bf16[128,2048]{1,0:T(8,128)(2,1)S(1)}, u32[]{:S(2)}, u32[]{:S(2)}) collective-permute-start(bf16[128,2048]{1,0:T(8,128)(2,1)S(1)} %collective-permute-done.11.refs_9_.refs_10_), channel_id=1, source_target_pairs={{0,2},{2,0},{1,3},{3,1},{4,6},{6,4},{5,7},{7,5},{8,10},{10,8},{9,1... | collective-permute-start | bytes 1572872 | tf_op jit(solution)/shard_map/ppermute | solution.py:421
  98.4 8.4 %collective-permute-start.10 = (bf16[128,2048]{1,0:T(8,128)(2,1)S(1)}, bf16[128,2048]{1,0:T(8,128)(2,1)}, u32[]{:S(2)}, u32[]{:S(2)}) collective-permute-start(bf16[128,2048]{1,0:T(8,128)(2,1)S(1)} %collective-permute-done.9.refs_5_.refs_6_), channel_id=1, source_target_pairs={{0,2},{2,0},{1,3},{3,1},{4,6},{6,4},{5,7},{7,5},{8,10},{10,8},{9,1... | collective-permute-start | bytes 1572872 | tf_op jit(solution)/shard_map/ppermute | solution.py:421
  101.5 3.9 %collective-permute-start.16 = (bf16[64,2048]{1,0:T(8,128)(2,1)}, bf16[64,2048]{1,0:T(8,128)(2,1)}, u32[]{:S(2)}, u32[]{:S(2)}) collective-permute-start(bf16[64,2048]{1,0:T(8,128)(2,1)} %collective-permute-done.15.refs_17_.refs_18_), channel_id=1, source_target_pairs={{0,2},{2,0},{1,3},{3,1},{4,6},{6,4},{5,7},{7,5},{8,10},{10,8},{9,1... | collective-permute-start | bytes 786440 | tf_op jit(solution)/shard_map/ppermute | solution.py:421
  103.2 3.5 %collective-permute-start.14 = (bf16[64,2048]{1,0:T(8,128)(2,1)}, bf16[64,2048]{1,0:T(8,128)(2,1)}, u32[]{:S(2)}, u32[]{:S(2)}) collective-permute-start(bf16[64,2048]{1,0:T(8,128)(2,1)} %collective-permute-done.13.refs_13_.refs_14_), channel_id=1, source_target_pairs={{0,2},{2,0},{1,3},{3,1},{4,6},{6,4},{5,7},{7,5},{8,10},{10,8},{9,1... | collective-permute-start | bytes 786440 | tf_op jit(solution)/shard_map/ppermute | solution.py:421
  106.8 2.2 copy-start
  224.1 81.4 %copy-start.2 = (f32[128,512]{1,0:T(8,128)S(1)}, f32[128,512]{1,0:T(8,128)}, u32[]{:S(2)}) copy-start(f32[128,512]{1,0:T(8,128)} %copy-done.1) | copy-start | bytes 786436
Sparse Core Ops, SparseCore 0:
  32.0 55.9 all-gather.1

commit v3 on v2

--- a/solution.py
+++ b/solution.py
@@ -388,8 +388,8 @@
     return jnp.concatenate(row)
 
 
-def shift_row(row):
-    return [lax.ppermute(row, ("zh", "y"), rotated(8, k)) for k in range(1, 5)]
+def shift_row(row, step):
+    return lax.ppermute(row, ("zh", "y"), rotated(8, step))
 
 
 def gather_kv(row, shifted):
@@ -416,16 +416,17 @@
     return mine, other, pos.reshape(2, 1, 17 * tokens), low, high
 
 
-def gather_attended(own):
+def gather_attended(own, others):
     def both(block):
         return [block, lax.ppermute(block, "c", flipped(2, 1))]
 
     near = lax.ppermute(own, Z, flipped(4, 1))
     far = lax.ppermute(own, Z, flipped(4, 3))
+    near, far, *others = lax.optimization_barrier((near, far, *others))
     cut = own.shape[0] // 2
     first = lax.ppermute(near[:cut], Z, flipped(4, 3))
     second = lax.ppermute(far[cut:], Z, flipped(4, 1))
-    return both(own) + both(near) + both(far) + both(first) + both(second)
+    return both(own) + both(near) + both(far) + both(first) + both(second), others
 
 
 def body(
@@ -461,9 +462,14 @@
         ],
         axis=1,
     )
+    before, third = shift_row(row, 1), shift_row(row, 3)
+    sent, before, third = lax.optimization_barrier((sent, before, third))
     got = lax.all_to_all(sent, LINE, split_axis=0, concat_axis=0, tiled=True)
-    got, row = lax.optimization_barrier((got, row))
-    shifted = shift_row(row)
+    half = row.shape[0] // 2
+    got, second, rest, oldest = lax.optimization_barrier(
+        (got, shift_row(before[:half], 1), shift_row(third[half:], -1), shift_row(row, 4))
+    )
+    shifted = [before, jnp.concatenate([second, rest]), third, oldest]
     kv, other, key_pos, low, high = gather_kv(row, shifted)
     weight = lax.all_gather(got[:, :weight_rows], ("y", "x"), axis=0, tiled=True)
     weight = weight.reshape(4, 4, GROUP, weight_rows, width)
@@ -480,9 +486,6 @@
         jnp.where(starts[None, :] <= query_pos[:, None], starts[None, :], 0), axis=1
     ).astype(jnp.int32)
     lim = jnp.stack([query_pos[0], query_pos[-1], query_start[0], query_start[-1]])
-    line_residual, slots, weights, queries = lax.optimization_barrier(
-        (line_residual, slots, weights, queries)
-    )
     attended = attend(
         queries, kv, other, key_pos, low, high, lim, query_pos[:, None], query_start[:, None]
     )
@@ -495,7 +498,10 @@
                 halves.append((high_part * 2 + c) * 2 + (zl ^ k))
     places = [(zh ^ h) * 2 + (core ^ c) for h in range(2) for c in range(2)]
     table = jnp.stack(halves + places).astype(jnp.int32)
-    hidden, outgoing = project(table, gather_attended(attended), weight, line_residual, slots)
+    blocks, (line_residual, slots, weights) = gather_attended(
+        attended, (line_residual, slots, weights)
+    )
+    hidden, outgoing = project(table, blocks, weight, line_residual, slots)
     incoming = lax.all_to_all(outgoing, AXES, split_axis=0, concat_axis=0, tiled=True)
     produced = expert(
         incoming.reshape(2, 16, 4, SLOTS, width), gate_proj, up_proj, down_proj

time: 332 us -> 336 us (1.012)
  starting transfers between devices: 32.8 us -> 39.2 us
    all_to_all x1, waiting for transfers between devices: 6.67 us -> 0.01 us  [body(): got = lax.all_to_all(sent, LINE, split_axis=0, concat_axis=0, tiled=True)]
    ppermute x4 -> x5, waiting for transfers between devices: 19 us -> 23.6 us  [shift_row(): return lax.ppermute(row, ('zh', 'y'), rotated(8, step))]
    ppermute x1, starting transfers between devices: 8.06 us -> 11.5 us  [gather_attended(): far = lax.ppermute(own, Z, flipped(4, 3))]
    ppermute x4 -> x5, starting transfers between devices: 6.54 us -> 9.35 us  [shift_row(): return lax.ppermute(row, ('zh', 'y'), rotated(8, step))]
  transfers between devices with their start and end apart: 19 -> 20, of which waited for: 9 -> 10; matrix products, arithmetic and copies ran while one was open for 2% -> 3% of each run, Pallas kernels for 2% -> 2%
where the time goes in v3:
time: 336 us; the launch traced here: 335 us
  blocking collectives  175 us (52%)
  Pallas kernels  46.5 us (14%)
  waiting for transfers between devices  44 us (13%)
  starting transfers between devices  39.2 us (12%)
  between operations  13.7 us (4%)
  local copies, waits for them, and re-layouts  9.89 us (3%)
  other arithmetic  5.79 us (2%)
    all_to_all x1, blocking collectives, body(): lax.all_to_all(outgoing, AXES, split_axis=0, concat_axis=0, tiled=True)  81.7 us
    all_to_all x1, blocking collectives, body(): lax.all_to_all(produced, AXES, split_axis=0, concat_axis=0, tiled=True)  81.5 us
    pallas_call x1, Pallas kernels, expert(): pl.pallas_call(expert_kernel, grid=(FIRST + SECOND,), in_specs=[pl.BlockS...  23.8 us
    ppermute x5, waiting for transfers between devices, shift_row(): return lax.ppermute(row, ('zh', 'y'), rotated(8, step))  23.6 us
    all_to_all x1, blocking collectives, body(): lax.all_to_all(mixed.reshape(GROUP, own_rows, width), LINE, split_axis=0,...  12.3 us
    ppermute x1, starting transfers between devices, gather_attended(): far = lax.ppermute(own, Z, flipped(4, 3))  11.5 us
    pallas_call x1, Pallas kernels, project(): pl.pallas_call(functools.partial(projection_kernel, steps), grid=(steps +...  10.6 us
    ppermute x1, waiting for transfers between devices, gather_attended(): far = lax.ppermute(own, Z, flipped(4, 3))  10 us
  transfers between devices with their start and end apart: 20, of which 10 were waited for; matrix products, arithmetic and copies ran while one was open for 3% of the time, Pallas kernels for 2%

profile of v3, /device:TPU:5, one launch (start us, length us, event | category | flops | bytes accessed | tf_op | source)
XLA Modules:
  0.0 334.6 jit_solution(2067361827496738816)
XLA Ops:
  6.5 0.8 constant_dynamic-update-slice_fusion.1
  7.4 0.8 constant_dynamic-update-slice_fusion
  8.1 0.3 collective-permute-start.2
  8.5 2.5 collective-permute-start.1
  10.9 0.4 collective-permute-done.2
  11.3 1.8 collective-permute-done.1
  13.1 1.7 collective-permute-done
  14.8 2.8 collective-permute-start.4
  17.6 2.0 collective-permute-start.3
  19.7 0.7 convert_element_type.14
  20.4 0.7 convert_element_type.15
  21.1 0.1 copy.40
  21.2 0.1 reshape.142
  21.3 1.0 copy.52
  22.3 1.0 pad_maximum_fusion
  23.3 1.4 collective-permute-done.4
  24.7 4.6 %collective-permute-done.3 = bf16[512,256]{1,0:T(8,128)(2,1)S(1)} collective-permute-done((bf16[512,256]{1,0:T(8,128)(2,1)S(1)}, bf16[512,256]{1,0:T(8,128)(2,1)S(1)}, u32[]{:S(2)}, u32[]{:S(2)}) %collective-permute-start.3) | collective-permute-done | bytes 262176 | tf_op jit(solution)/shard_map/ppermute | solution.py:392
  29.3 7.6 %all-to-all-start = ((bf16[8,112,512]{2,1,0:T(8,128)(2,1)}), bf16[8,112,512]{2,1,0:T(8,128)(2,1)S(1)}, u32[]{:S(2)}, u32[]{:S(2)}) async-start(bf16[8,112,512]{2,1,0:T(8,128)(2,1)} %pad_maximum_fusion), calls=%async_computation | async-start | bytes 1835008 | tf_op jit(solution)/shard_map/all_to_all | solution.py:467
  37.0 3.0 collective-permute-start.7
  40.0 0.1 collective-permute-start.6
  40.1 1.5 collective-permute-start.5
  41.5 17.6 %collective-permute-done.7 = bf16[512,256]{1,0:T(8,128)(2,1)S(1)} collective-permute-done((bf16[512,256]{1,0:T(8,128)(2,1)S(1)}, bf16[512,256]{1,0:T(8,128)(2,1)S(1)}, u32[]{:S(2)}, u32[]{:S(2)}) %collective-permute-start.7) | collective-permute-done | bytes 262176 | tf_op jit(solution)/shard_map/ppermute | solution.py:392
  59.1 0.7 slice.65
  59.9 0.1 broadcast_in_dim.54
  60.0 0.1 reshape.138
  60.1 0.1 fusion.3
  60.2 0.1 broadcast_multiply_fusion
  60.2 0.1 slice.54
  60.3 0.1 reshape.139
  60.5 0.2 reduce-window.9
  60.7 0.1 select_reduce_fusion
  60.8 0.1 copy.43.qstart
  60.9 0.1 fusion.6
  61.1 0.6 fusion.7
  61.7 0.1 broadcast_bitcast_fusion
  61.8 0.1 fusion
  62.0 0.9 constant_dynamic-update-slice_fusion.4
  62.9 1.1 collective-permute-start.8
  64.0 2.6 pad_add_fusion.lim
  66.7 6.1 %attention.1.refs_1_.refs_2_ = bf16[128,2048]{1,0:T(8,128)(2,1)S(1)} custom-call(s32[4]{0:T(128)S(1)} %pad_add_fusion.lim, s32[6]{0:T(128)S(1)} %get-tuple-element.54.low, s32[6]{0:T(128)S(1)} %get-tuple-element.53.high, bf16[128,2048]{1,0:T(8,128)(2,1)S(1)} %copy-done.3, bf16[2176,256]{1,0:T(8,128)(2,1)S(1)} %constant_dynamic-update-slice_fusion.2.kv, ...), custom_call_target="tpu_custom_call" | custom-call | flops 10000000000 | bytes 4000000 | tf_op jit(solution)/shard_map/attention/pallas_call | solution.py:104
  72.9 11.5 %collective-permute-start.10 = (bf16[128,2048]{1,0:T(8,128)(2,1)S(1)}, bf16[128,2048]{1,0:T(8,128)(2,1)S(1)}, u32[]{:S(2)}, u32[]{:S(2)}) collective-permute-start(bf16[128,2048]{1,0:T(8,128)(2,1)S(1)} %attention.1.refs_1_.refs_2_), channel_id=1, source_target_pairs={{0,65},{1,64},{64,1},{65,0},{2,67},{3,66},{66,3},{67,2},{4,69},{5,... | collective-permute-start | bytes 1572872 | tf_op jit(solution)/shard_map/ppermute | solution.py:424
  84.5 0.1 reshape.143
  84.6 0.1 copy.44
  84.7 0.9 routing.1
  85.6 0.7 copy-done.1
  86.3 0.3 collective-permute-start.11
  86.7 10.0 %collective-permute-done.10.refs_9_.refs_10_ = bf16[128,2048]{1,0:T(8,128)(2,1)S(1)} collective-permute-done((bf16[128,2048]{1,0:T(8,128)(2,1)S(1)}, bf16[128,2048]{1,0:T(8,128)(2,1)S(1)}, u32[]{:S(2)}, u32[]{:S(2)}) %collective-permute-start.10) | collective-permute-done | bytes 524320 | tf_op jit(solution)/shard_map/ppermute | solution.py:424
  96.7 1.0 collective-permute-done.9.refs_5_.refs_6_
  97.7 0.4 collective-permute-start.16
  98.1 1.3 collective-permute-start.14
  99.4 1.0 collective-permute-start.12
  100.5 4.1 %collective-permute-done.16.refs_17_.refs_18_ = bf16[64,2048]{1,0:T(8,128)(2,1)} collective-permute-done((bf16[64,2048]{1,0:T(8,128)(2,1)S(1)}, bf16[64,2048]{1,0:T(8,128)(2,1)}, u32[]{:S(2)}, u32[]{:S(2)}) %collective-permute-start.16) | collective-permute-done | bytes 262176 | tf_op jit(solution)/shard_map/ppermute | solution.py:428
  104.6 2.0 collective-permute-start.17
  106.6 1.6 collective-permute-start.15
  108.2 0.1 stack.55.refs_0_
  108.4 1.4 collective-permute-done.15.refs_15_.refs_16_
  109.8 2.2 copy-done
  112.0 10.6 %projection.1 = (bf16[512,512]{1,0:T(8,128)(2,1)S(1)}, bf16[128,48,512]{2,1,0:T(8,128)(2,1)S(1)}) custom-call(s32[12]{0:T(128)S(1)} %stack.55.refs_0_, bf16[128,2048]{1,0:T(8,128)(2,1)S(1)} %attention.1.refs_1_.refs_2_, bf16[128,2048]{1,0:T(8,128)(2,1)S(1)} %attention.1.refs_1_.refs_2_, bf16[128,2048]{1,0:T(8,128)(2,1)S(1)} %collective-permute-done.11.refs_3_.refs_4_, ...), custom_call_target="tpu_custom_call" | custom-call | tf_op jit(solution)/shard_map/projection/pallas_call | solution.py:191
  122.6 81.7 %all_to_all.20 = bf16[128,48,512]{2,1,0:T(8,128)(2,1)} all-to-all(bf16[128,48,512]{2,1,0:T(8,128)(2,1)S(1)} %get-tuple-element.35), channel_id=1, replica_groups=mesh['zh'=2,'y'=4,'x'=4,'c'=2,'zl'=2] {'zh','y','x','c','zl'}, dimensions={0} | all-to-all | bytes 12582912 | tf_op jit(solution)/shard_map/all_to_all | solution.py:505
  204.3 23.8 %expert.1 = bf16[2,16,4,48,512]{4,3,2,1,0:T(8,128)(2,1)} custom-call(bf16[2,16,4,48,512]{4,3,2,1,0:T(8,128)(2,1)} %bitcast.44, bf16[1,4096,768]{2,1,0:T(8,128)(2,1)} %gate_w.1, bf16[1,4096,768]{2,1,0:T(8,128)(2,1)} %up_w.1, bf16[1,768,4096]{2,1,0:T(8,128)(2,1)} %down_w.1), custom_call_target="tpu_custom_call" | custom-call | tf_op jit(solution)/shard_map/expert/pallas_call | solution.py:312
  228.0 81.5 %all_to_all.21.answers = bf16[128,48,512]{2,1,0:T(8,128)(2,1)S(1)} all-to-all(bf16[128,48,512]{2,1,0:T(8,128)(2,1)} %bitcast.45), channel_id=1, replica_groups=mesh['zh'=2,'y'=4,'x'=4,'c'=2,'zl'=2] {'zh','y','x','c','zl'}, dimensions={0} | all-to-all | bytes 12582912 | tf_op jit(solution)/shard_map/all_to_all | solution.py:509
  309.5 5.1 %combine.1 = bf16[512,512]{1,0:T(8,128)(2,1)S(1)} custom-call(f32[128,512]{1,0:T(8,128)S(1)} %get-tuple-element.30.refs_23_.slots, f32[128,512]{1,0:T(8,128)S(1)} %copy-done.2, bf16[128,48,512]{2,1,0:T(8,128)(2,1)S(1)} %all_to_all.21.answers, bf16[512,512]{1,0:T(8,128)(2,1)S(1)} %get-tuple-element.36.hidden), custom_call_target="tpu_custom_call" | custom-call | tf_op jit(solution)/shard_map/combine/pallas_call | solution.py:368
  314.6 12.3 %all_to_all.22 = bf16[8,64,512]{2,1,0:T(8,128)(2,1)S(1)} all-to-all(bf16[8,64,512]{2,1,0:T(8,128)(2,1)S(1)} %bitcast.43), channel_id=1, replica_groups=mesh['zh'=2,'y'=4,'x'=4,'c'=2,'zl'=2] {'zh','c','zl'}, dimensions={0} | all-to-all | bytes 1048576 | tf_op jit(solution)/shard_map/all_to_all | solution.py:511
  326.9 0.8 copy.48
  (56 shorter events, 0.5 us)
Async XLA Ops:
  6.5 15.7 %copy-start.4 = (bf16[64,4096]{1,0:T(8,128)(2,1)S(1)}, bf16[64,4096]{1,0:T(8,128)(2,1)}, u32[]{:S(2)}) copy-start(bf16[64,4096]{1,0:T(8,128)(2,1)} %param.18) | copy-start | bytes 1572868
  8.1 3.2 collective-permute-start.2
  8.5 4.6 %collective-permute-start.1 = (bf16[128,256]{1,0:T(8,128)(2,1)S(1)}, bf16[128,256]{1,0:T(8,128)(2,1)S(1)}, u32[]{:S(2)}, u32[]{:S(2)}) collective-permute-start(bf16[128,256]{1,0:T(8,128)(2,1)S(1)} %get-tuple-element.39), channel_id=1, source_target_pairs={{0,8},{4,12},{8,0},{12,4},{1,9},{5,13},{9,1},{13,5},{2,10},{6,14},... | collective-permute-start | bytes 196616 | tf_op jit(solution)/shard_map/ppermute | solution.py:387
  10.9 3.9 %collective-permute-start = (bf16[128,256]{1,0:T(8,128)(2,1)S(1)}, bf16[128,256]{1,0:T(8,128)(2,1)S(1)}, u32[]{:S(2)}, u32[]{:S(2)}) collective-permute-start(bf16[128,256]{1,0:T(8,128)(2,1)S(1)} %get-tuple-element.39), channel_id=1, source_target_pairs={{0,4},{4,8},{8,12},{12,0},{1,5},{5,9},{9,13},{13,1},{2,6},{6,10},{... | collective-permute-start | bytes 196616 | tf_op jit(solution)/shard_map/ppermute | solution.py:387
  14.8 9.9 %collective-permute-start.4 = (bf16[512,256]{1,0:T(8,128)(2,1)S(1)}, bf16[512,256]{1,0:T(8,128)(2,1)S(1)}, u32[]{:S(2)}, u32[]{:S(2)}) collective-permute-start(bf16[512,256]{1,0:T(8,128)(2,1)S(1)} %pad_maximum_fusion.1), channel_id=1, source_target_pairs={{0,48},{16,64},{32,80},{48,96},{64,112},{80,0},{96,16},{112,32},{1... | collective-permute-start | bytes 786440 | tf_op jit(solution)/shard_map/ppermute | solution.py:392
  17.6 11.7 %collective-permute-start.3 = (bf16[512,256]{1,0:T(8,128)(2,1)S(1)}, bf16[512,256]{1,0:T(8,128)(2,1)S(1)}, u32[]{:S(2)}, u32[]{:S(2)}) collective-permute-start(bf16[512,256]{1,0:T(8,128)(2,1)S(1)} %pad_maximum_fusion.1), channel_id=1, source_target_pairs={{0,16},{16,32},{32,48},{48,64},{64,80},{80,96},{96,112},{112,0},{1... | collective-permute-start | bytes 786440 | tf_op jit(solution)/shard_map/ppermute | solution.py:392
  29.3 29.8 %all-to-all-start = ((bf16[8,112,512]{2,1,0:T(8,128)(2,1)}), bf16[8,112,512]{2,1,0:T(8,128)(2,1)S(1)}, u32[]{:S(2)}, u32[]{:S(2)}) async-start(bf16[8,112,512]{2,1,0:T(8,128)(2,1)} %pad_maximum_fusion), calls=%async_computation | async-start | bytes 1835008 | tf_op jit(solution)/shard_map/all_to_all | solution.py:467
  36.9 23.1 %copy-start.5 = (s32[17]{0:T(128)S(1)}, s32[17]{0:T(128)}, u32[]{:S(2)}) copy-start(s32[17]{0:T(128)} %constant.90) | copy-start | bytes 208
  37.0 23.6 %copy-start.6 = (s32[8]{0:T(128)S(1)}, s32[8]{0:T(128)}, u32[]{:S(2)}) copy-start(s32[8]{0:T(128)} %param.16) | copy-start | bytes 100
  37.0 72.8 %all-gather.2.cloned.1.call-start = ((), (), s32[]{:S(2)}) async-start(), calls=%async_computation.4 | async-start | bytes 4456448 | tf_op jit(solution)/shard_map/all_gather | solution.py:474
  37.0 22.1 %collective-permute-start.7 = (bf16[512,256]{1,0:T(8,128)(2,1)S(1)}, bf16[512,256]{1,0:T(8,128)(2,1)S(1)}, u32[]{:S(2)}, u32[]{:S(2)}) collective-permute-start(bf16[512,256]{1,0:T(8,128)(2,1)S(1)} %pad_maximum_fusion.1), channel_id=1, source_target_pairs={{0,64},{16,80},{32,96},{48,112},{64,0},{80,16},{96,32},{112,48},{1... | collective-permute-start | bytes 786440 | tf_op jit(solution)/shard_map/ppermute | solution.py:392
  40.0 19.1 %collective-permute-start.6 = (bf16[256,256]{1,0:T(8,128)(2,1)S(1)}, bf16[256,256]{1,0:T(8,128)(2,1)S(1)}, u32[]{:S(2)}, u32[]{:S(2)}) collective-permute-start(bf16[256,256]{1,0:T(8,128)(2,1)S(1)} %slice.56), channel_id=1, source_target_pairs={{0,112},{16,0},{32,16},{48,32},{64,48},{80,64},{96,80},{112,96},{1... | collective-permute-start | bytes 393224 | tf_op jit(solution)/shard_map/ppermute | solution.py:392
  40.1 19.0 %collective-permute-start.5 = (bf16[256,256]{1,0:T(8,128)(2,1)S(1)}, bf16[256,256]{1,0:T(8,128)(2,1)}, u32[]{:S(2)}, u32[]{:S(2)}) collective-permute-start(bf16[256,256]{1,0:T(8,128)(2,1)S(1)} %slice.55), channel_id=1, source_target_pairs={{0,16},{16,32},{32,48},{48,64},{64,80},{80,96},{96,112},{112,0},{1... | collective-permute-start | bytes 393224 | tf_op jit(solution)/shard_map/ppermute | solution.py:392
  61.8 4.9 %copy-start.3 = (bf16[128,2048]{1,0:T(8,128)(2,1)S(1)}, bf16[128,2048]{1,0:T(8,128)(2,1)}, u32[]{:S(2)}) copy-start(bf16[128,2048]{1,0:T(8,128)(2,1)} %q.1) | copy-start | bytes 1572868
  62.9 3.8 %collective-permute-start.8 = (bf16[2176,256]{1,0:T(8,128)(2,1)S(1)}, bf16[2176,256]{1,0:T(8,128)(2,1)S(1)}, u32[]{:S(2)}, u32[]{:S(2)}) collective-permute-start(bf16[2176,256]{1,0:T(8,128)(2,1)S(1)} %constant_dynamic-update-slice_fusion.2.kv), channel_id=1, source_target_pairs={{0,2},{2,0},{1,3},{3,1},{4,6},{6,4},{5,7},{7,5},{8,10},{10,8},{9,1... | collective-permute-start | bytes 3342344 | tf_op jit(solution)/shard_map/ppermute | solution.py:404
  72.9 23.9 %collective-permute-start.10 = (bf16[128,2048]{1,0:T(8,128)(2,1)S(1)}, bf16[128,2048]{1,0:T(8,128)(2,1)S(1)}, u32[]{:S(2)}, u32[]{:S(2)}) collective-permute-start(bf16[128,2048]{1,0:T(8,128)(2,1)S(1)} %attention.1.refs_1_.refs_2_), channel_id=1, source_target_pairs={{0,65},{1,64},{64,1},{65,0},{2,67},{3,66},{66,3},{67,2},{4,69},{5,... | collective-permute-start | bytes 1572872 | tf_op jit(solution)/shard_map/ppermute | solution.py:424
  84.4 13.3 %collective-permute-start.9 = (bf16[128,2048]{1,0:T(8,128)(2,1)S(1)}, bf16[128,2048]{1,0:T(8,128)(2,1)S(1)}, u32[]{:S(2)}, u32[]{:S(2)}) collective-permute-start(bf16[128,2048]{1,0:T(8,128)(2,1)S(1)} %attention.1.refs_1_.refs_2_), channel_id=1, source_target_pairs={{0,1},{1,0},{64,65},{65,64},{2,3},{3,2},{66,67},{67,66},{4,5},{5,4... | collective-permute-start | bytes 1572872 | tf_op jit(solution)/shard_map/ppermute | solution.py:423
  85.6 0.7 copy-start.1
  86.3 22.0 %collective-permute-start.11 = (bf16[128,2048]{1,0:T(8,128)(2,1)S(1)}, bf16[128,2048]{1,0:T(8,128)(2,1)S(1)}, u32[]{:S(2)}, u32[]{:S(2)}) collective-permute-start(bf16[128,2048]{1,0:T(8,128)(2,1)S(1)} %attention.1.refs_1_.refs_2_), channel_id=1, source_target_pairs={{0,2},{2,0},{1,3},{3,1},{4,6},{6,4},{5,7},{7,5},{8,10},{10,8},{9,1... | collective-permute-start | bytes 1572872 | tf_op jit(solution)/shard_map/ppermute | solution.py:421
  97.7 6.9 %collective-permute-start.16 = (bf16[64,2048]{1,0:T(8,128)(2,1)S(1)}, bf16[64,2048]{1,0:T(8,128)(2,1)}, u32[]{:S(2)}, u32[]{:S(2)}) collective-permute-start(bf16[64,2048]{1,0:T(8,128)(2,1)S(1)} %slice.64), channel_id=1, source_target_pairs={{0,1},{1,0},{64,65},{65,64},{2,3},{3,2},{66,67},{67,66},{4,5},{5,4... | collective-permute-start | bytes 786440 | tf_op jit(solution)/shard_map/ppermute | solution.py:428
  98.1 8.5 %collective-permute-start.14 = (bf16[64,2048]{1,0:T(8,128)(2,1)S(1)}, bf16[64,2048]{1,0:T(8,128)(2,1)}, u32[]{:S(2)}, u32[]{:S(2)}) collective-permute-start(bf16[64,2048]{1,0:T(8,128)(2,1)S(1)} %slice.63), channel_id=1, source_target_pairs={{0,65},{1,64},{64,1},{65,0},{2,67},{3,66},{66,3},{67,2},{4,69},{5,... | collective-permute-start | bytes 786440 | tf_op jit(solution)/shard_map/ppermute | solution.py:427
  99.4 10.3 %collective-permute-start.12 = (bf16[128,2048]{1,0:T(8,128)(2,1)S(1)}, bf16[128,2048]{1,0:T(8,128)(2,1)S(1)}, u32[]{:S(2)}, u32[]{:S(2)}) collective-permute-start(bf16[128,2048]{1,0:T(8,128)(2,1)S(1)} %collective-permute-done.9.refs_5_.refs_6_), channel_id=1, source_target_pairs={{0,2},{2,0},{1,3},{3,1},{4,6},{6,4},{5,7},{7,5},{8,10},{10,8},{9,1... | collective-permute-start | bytes 1572872 | tf_op jit(solution)/shard_map/ppermute | solution.py:421
  100.5 9.3 %collective-permute-start.13 = (bf16[128,2048]{1,0:T(8,128)(2,1)S(1)}, bf16[128,2048]{1,0:T(8,128)(2,1)}, u32[]{:S(2)}, u32[]{:S(2)}) collective-permute-start(bf16[128,2048]{1,0:T(8,128)(2,1)S(1)} %collective-permute-done.10.refs_9_.refs_10_), channel_id=1, source_target_pairs={{0,2},{2,0},{1,3},{3,1},{4,6},{6,4},{5,7},{7,5},{8,10},{10,8},{9,1... | collective-permute-start | bytes 1572872 | tf_op jit(solution)/shard_map/ppermute | solution.py:421
  104.6 3.7 %collective-permute-start.17 = (bf16[64,2048]{1,0:T(8,128)(2,1)}, bf16[64,2048]{1,0:T(8,128)(2,1)}, u32[]{:S(2)}, u32[]{:S(2)}) collective-permute-start(bf16[64,2048]{1,0:T(8,128)(2,1)} %collective-permute-done.16.refs_17_.refs_18_), channel_id=1, source_target_pairs={{0,2},{2,0},{1,3},{3,1},{4,6},{6,4},{5,7},{7,5},{8,10},{10,8},{9,1... | collective-permute-start | bytes 786440 | tf_op jit(solution)/shard_map/ppermute | solution.py:421
  106.6 3.1 collective-permute-start.15
  109.8 2.2 copy-start
  228.0 81.5 %copy-start.2 = (f32[128,512]{1,0:T(8,128)S(1)}, f32[128,512]{1,0:T(8,128)}, u32[]{:S(2)}) copy-start(f32[128,512]{1,0:T(8,128)} %copy-done.1) | copy-start | bytes 786436
Sparse Core Ops, SparseCore 0:
  60.0 48.4 all-gather.1

commit v4 on v3

--- a/solution.py
+++ b/solution.py
@@ -364,7 +364,7 @@
 def combine(slots, weights, answers, hidden):
     tokens, width = hidden.shape
     experts = answers.shape[0]
-    count = 16
+    count = 32
     return pl.pallas_call(
         combine_kernel,
         grid=(experts // count,),
@@ -394,17 +394,19 @@
 
 def gather_kv(row, shifted):
     tokens = row.shape[0] // 4
+    middle, oldest = shifted[:3], shifted[3]
+    near = jnp.arange(1, 4, dtype=jnp.int32) <= lax.axis_index("x")
+    picked = jnp.where(jnp.repeat(near, tokens)[:, None], row[tokens:], oldest[tokens:])
+    mine = jnp.concatenate([row[:tokens], oldest[:tokens], picked] + middle)
+    return mine, lax.ppermute(mine, "c", flipped(2, 1))
+
+
+def key_tables(tokens):
     x, core = lax.axis_index("x"), lax.axis_index("c")
     slab = lax.axis_index(("zh", "y"))
-    middle, oldest = shifted[:3], shifted[3]
     steps = jnp.arange(1, 4, dtype=jnp.int32)
-    near = steps <= x
-    picked = jnp.where(jnp.repeat(near, tokens)[:, None], row[tokens:], oldest[tokens:])
-    mine = jnp.concatenate([row[:tokens], oldest[:tokens], picked] + middle)
-    other = lax.ppermute(mine, "c", flipped(2, 1))
-
     back = jnp.concatenate(
-        [jnp.array([0, 4], jnp.int32), jnp.where(near, 0, 4), jnp.repeat(steps, 4)]
+        [jnp.array([0, 4], jnp.int32), jnp.where(steps <= x, 0, 4), jnp.repeat(steps, 4)]
     )
     turn = jnp.array([0, 0, 1, 2, 3] + [0, 1, 2, 3] * 3, jnp.int32)
     begin = ((slab - back) % 8) * 8 + ((x - turn) % 4) * 2
@@ -413,7 +415,17 @@
     chunks = begin[:, 5:].reshape(6, 4)
     low = jnp.min(chunks, axis=1) * tokens
     high = jnp.max(chunks, axis=1) * tokens + tokens - 1
-    return mine, other, pos.reshape(2, 1, 17 * tokens), low, high
+    return pos.reshape(2, 1, 17 * tokens), low, high
+
+
+def query_tables(tokens, lengths):
+    query_pos = lax.axis_index(("zh", "y", "x", "c")) * tokens + jnp.arange(tokens, dtype=jnp.int32)
+    starts = jnp.cumsum(lengths) - lengths
+    query_start = jnp.max(
+        jnp.where(starts[None, :] <= query_pos[:, None], starts[None, :], 0), axis=1
+    ).astype(jnp.int32)
+    lim = jnp.stack([query_pos[0], query_pos[-1], query_start[0], query_start[-1]])
+    return lim, query_pos[:, None], query_start[:, None]
 
 
 def gather_attended(own, others):
@@ -462,15 +474,16 @@
         ],
         axis=1,
     )
-    before, third = shift_row(row, 1), shift_row(row, 3)
-    sent, before, third = lax.optimization_barrier((sent, before, third))
     got = lax.all_to_all(sent, LINE, split_axis=0, concat_axis=0, tiled=True)
+    tables = key_tables(tokens) + query_tables(tokens, lengths)
+    got, before, third, *tables = lax.optimization_barrier(
+        (got, shift_row(row, 1), shift_row(row, 3)) + tables
+    )
     half = row.shape[0] // 2
-    got, second, rest, oldest = lax.optimization_barrier(
-        (got, shift_row(before[:half], 1), shift_row(third[half:], -1), shift_row(row, 4))
-    )
-    shifted = [before, jnp.concatenate([second, rest]), third, oldest]
-    kv, other, key_pos, low, high = gather_kv(row, shifted)
+    second, rest, oldest = lax.optimization_barrier(
+        (shift_row(before[:half], 1), shift_row(third[half:], -1), shift_row(row, 4))
+    )
+    kv, other = gather_kv(row, [before, jnp.concatenate([second, rest]), third, oldest])
     weight = lax.all_gather(got[:, :weight_rows], ("y", "x"), axis=0, tiled=True)
     weight = weight.reshape(4, 4, GROUP, weight_rows, width)
     line_residual = got[:, weight_rows : weight_rows + own_rows]
@@ -480,15 +493,7 @@
     gates = meta[8:].astype(F32)
     slots, weights = route(ids, gates, experts)
 
-    query_pos = lax.axis_index(("zh", "y", "x", "c")) * tokens + jnp.arange(tokens, dtype=jnp.int32)
-    starts = jnp.cumsum(lengths) - lengths
-    query_start = jnp.max(
-        jnp.where(starts[None, :] <= query_pos[:, None], starts[None, :], 0), axis=1
-    ).astype(jnp.int32)
-    lim = jnp.stack([query_pos[0], query_pos[-1], query_start[0], query_start[-1]])
-    attended = attend(
-        queries, kv, other, key_pos, low, high, lim, query_pos[:, None], query_start[:, None]
-    )
+    attended = attend(queries, kv, other, *tables)
 
     zl, core, zh = lax.axis_index("zl"), lax.axis_index("c"), lax.axis_index("zh")
     halves = []
@@ -498,8 +503,8 @@
                 halves.append((high_part * 2 + c) * 2 + (zl ^ k))
     places = [(zh ^ h) * 2 + (core ^ c) for h in range(2) for c in range(2)]
     table = jnp.stack(halves + places).astype(jnp.int32)
-    blocks, (line_residual, slots, weights) = gather_attended(
-        attended, (line_residual, slots, weights)
+    blocks, (line_residual, slots, weights, weight) = gather_attended(
+        attended, (line_residual, slots, weights, weight)
     )
     hidden, outgoing = project(table, blocks, weight, line_residual, slots)
     incoming = lax.all_to_all(outgoing, AXES, split_axis=0, concat_axis=0, tiled=True)

time: 336 us -> 335 us (level)
    all_to_all x1, waiting for transfers between devices: 0.01 us -> 7.34 us  [body(): got = lax.all_to_all(sent, LINE, split_axis=0, concat_axis=0, tiled=True)]
    ppermute x5, waiting for transfers between devices: 23.6 us -> 18 us  [shift_row(): return lax.ppermute(row, ('zh', 'y'), rotated(8, step))]
    ppermute x3, waiting for transfers between devices: 3.88 us -> 0.01 us  [gather_row(): row = [own] + [lax.ppermute(own, 'x', rotated(4, k)) for k in range(1, 4)]]
  transfers between devices with their start and end apart: 20 -> 20, of which waited for: 10 -> 11; matrix products, arithmetic and copies ran while one was open for 3% -> 3% of each run, Pallas kernels for 2% -> 2%
where the time goes in v4:
time: 335 us; the launch traced here: 333 us
  blocking collectives  175 us (52%)
  Pallas kernels  45.5 us (14%)
  waiting for transfers between devices  45.2 us (13%)
  starting transfers between devices  37.3 us (11%)
  between operations  13.8 us (4%)
  local copies, waits for them, and re-layouts  10.1 us (3%)
  other arithmetic  5.75 us (2%)
    all_to_all x1, blocking collectives, body(): lax.all_to_all(outgoing, AXES, split_axis=0, concat_axis=0, tiled=True)  81.7 us
    all_to_all x1, blocking collectives, body(): lax.all_to_all(produced, AXES, split_axis=0, concat_axis=0, tiled=True)  81.5 us
    pallas_call x1, Pallas kernels, expert(): pl.pallas_call(expert_kernel, grid=(FIRST + SECOND,), in_specs=[pl.BlockS...  23.7 us
    ppermute x5, waiting for transfers between devices, shift_row(): return lax.ppermute(row, ('zh', 'y'), rotated(8, step))  18 us
    all_to_all x1, blocking collectives, body(): lax.all_to_all(mixed.reshape(GROUP, own_rows, width), LINE, split_axis=0,...  12.3 us
    ppermute x1, starting transfers between devices, gather_attended(): far = lax.ppermute(own, Z, flipped(4, 3))  10.8 us
    pallas_call x1, Pallas kernels, project(): pl.pallas_call(functools.partial(projection_kernel, steps), grid=(steps +...  10.6 us
    ppermute x1, waiting for transfers between devices, gather_attended(): far = lax.ppermute(own, Z, flipped(4, 3))  9.52 us
  transfers between devices with their start and end apart: 20, of which 11 were waited for; matrix products, arithmetic and copies ran while one was open for 3% of the time, Pallas kernels for 2%

profile of v4, /device:TPU:5, one launch (start us, length us, event | category | flops | bytes accessed | tf_op | source)
XLA Modules:
  0.0 333.1 jit_solution(5548439530359749303)
XLA Ops:
  6.5 0.8 constant_dynamic-update-slice_fusion.7
  7.4 0.8 constant_dynamic-update-slice_fusion.6
  8.1 0.3 collective-permute-start.2
  8.5 2.5 collective-permute-start.1
  10.9 0.7 convert_element_type.14
  11.6 0.7 convert_element_type.15
  12.3 0.1 copy.33
  12.4 0.1 reshape.139
  12.5 1.0 copy.44
  13.6 1.0 pad_maximum_fusion
  14.6 6.7 %all-to-all-start = ((bf16[8,112,512]{2,1,0:T(8,128)(2,1)}), bf16[8,112,512]{2,1,0:T(8,128)(2,1)S(1)}, u32[]{:S(2)}, u32[]{:S(2)}) async-start(bf16[8,112,512]{2,1,0:T(8,128)(2,1)} %pad_maximum_fusion), calls=%async_computation | async-start | bytes 1835008 | tf_op jit(solution)/shard_map/all_to_all | solution.py:477
  21.4 0.2 reduce-window.9
  21.6 0.1 reshape.140
  21.7 0.1 fusion.3
  21.8 0.1 broadcast_add_fusion.1
  21.9 0.1 add.136
  22.0 0.1 select_reduce_fusion
  22.2 0.1 reshape.141
  22.2 0.7 fusion.7
  22.9 0.1 fusion.6
  23.1 2.8 collective-permute-start.4
  25.9 1.3 collective-permute-start.3
  27.2 2.6 pad_add_fusion.lim
  29.8 5.1 %collective-permute-done.4 = bf16[512,256]{1,0:T(8,128)(2,1)S(1)} collective-permute-done((bf16[512,256]{1,0:T(8,128)(2,1)S(1)}, bf16[512,256]{1,0:T(8,128)(2,1)S(1)}, u32[]{:S(2)}, u32[]{:S(2)}) %collective-permute-start.4) | collective-permute-done | bytes 262176 | tf_op jit(solution)/shard_map/ppermute | solution.py:392
  34.9 3.9 %collective-permute-done.3 = bf16[512,256]{1,0:T(8,128)(2,1)S(1)} collective-permute-done((bf16[512,256]{1,0:T(8,128)(2,1)S(1)}, bf16[512,256]{1,0:T(8,128)(2,1)S(1)}, u32[]{:S(2)}, u32[]{:S(2)}) %collective-permute-start.3) | collective-permute-done | bytes 262176 | tf_op jit(solution)/shard_map/ppermute | solution.py:392
  38.8 7.3 %all-to-all-done = bf16[8,112,512]{2,1,0:T(8,128)(2,1)S(1)} async-done(((bf16[8,112,512]{2,1,0:T(8,128)(2,1)}), bf16[8,112,512]{2,1,0:T(8,128)(2,1)S(1)}, u32[]{:S(2)}, u32[]{:S(2)}) %all-to-all-start) | async-done | bytes 917536 | tf_op jit(solution)/shard_map/all_to_all | solution.py:477
  46.2 0.8 slice.63
  47.0 0.7 collective-permute-start.7
  47.7 0.1 collective-permute-start.6
  47.8 1.5 collective-permute-start.5
  49.3 0.1 broadcast_bitcast_fusion
  49.4 9.0 %collective-permute-done.7 = bf16[512,256]{1,0:T(8,128)(2,1)S(1)} collective-permute-done((bf16[512,256]{1,0:T(8,128)(2,1)S(1)}, bf16[512,256]{1,0:T(8,128)(2,1)S(1)}, u32[]{:S(2)}, u32[]{:S(2)}) %collective-permute-start.7) | collective-permute-done | bytes 262176 | tf_op jit(solution)/shard_map/ppermute | solution.py:392
  58.3 0.1 fusion
  58.6 2.0 collective-permute-start.8
  60.6 0.1 copy.35.qstart
  60.7 2.3 collective-permute-done.8.other
  63.0 1.0 copy-done.3
  64.0 6.0 %attention.1.refs_1_.refs_2_ = bf16[128,2048]{1,0:T(8,128)(2,1)S(1)} custom-call(s32[4]{0:T(128)S(1)} %pad_add_fusion.lim, s32[6]{0:T(128)S(1)} %get-tuple-element.28.low, s32[6]{0:T(128)S(1)} %get-tuple-element.29.high, bf16[128,2048]{1,0:T(8,128)(2,1)S(1)} %copy-done.3, bf16[2176,256]{1,0:T(8,128)(2,1)S(1)} %constant_dynamic-update-slice_fusion.2.kv, ...), custom_call_target="tpu_custom_call" | custom-call | flops 10000000000 | bytes 4000000 | tf_op jit(solution)/shard_map/attention/pallas_call | solution.py:104
  70.0 10.8 %collective-permute-start.10 = (bf16[128,2048]{1,0:T(8,128)(2,1)S(1)}, bf16[128,2048]{1,0:T(8,128)(2,1)S(1)}, u32[]{:S(2)}, u32[]{:S(2)}) collective-permute-start(bf16[128,2048]{1,0:T(8,128)(2,1)S(1)} %attention.1.refs_1_.refs_2_), channel_id=1, source_target_pairs={{0,65},{1,64},{64,1},{65,0},{2,67},{3,66},{66,3},{67,2},{4,69},{5,... | collective-permute-start | bytes 1572872 | tf_op jit(solution)/shard_map/ppermute | solution.py:436
  80.9 0.1 reshape.144
  81.1 0.1 copy.36
  81.2 0.9 routing.1
  82.1 0.7 copy-done.1
  82.8 0.7 collective-permute-start.11
  83.4 9.5 %collective-permute-done.10.refs_9_.refs_10_ = bf16[128,2048]{1,0:T(8,128)(2,1)S(1)} collective-permute-done((bf16[128,2048]{1,0:T(8,128)(2,1)S(1)}, bf16[128,2048]{1,0:T(8,128)(2,1)S(1)}, u32[]{:S(2)}, u32[]{:S(2)}) %collective-permute-start.10) | collective-permute-done | bytes 524320 | tf_op jit(solution)/shard_map/ppermute | solution.py:436
  92.9 0.8 collective-permute-done.9.refs_5_.refs_6_
  93.8 2.3 all-gather.2.cloned.1.call-done
  96.1 1.4 collective-permute-start.16
  97.5 2.0 collective-permute-start.14
  99.5 1.2 collective-permute-start.12
  100.7 2.8 collective-permute-done.16.refs_17_.refs_18_
  103.5 1.5 collective-permute-start.17
  105.0 0.7 collective-permute-done.14.refs_13_.refs_14_
  105.8 1.9 collective-permute-start.15
  107.6 0.1 stack.55.refs_0_
  107.7 1.4 collective-permute-done.15.refs_15_.refs_16_
  109.1 2.2 copy-done
  111.3 10.6 %projection.1 = (bf16[512,512]{1,0:T(8,128)(2,1)S(1)}, bf16[128,48,512]{2,1,0:T(8,128)(2,1)S(1)}) custom-call(s32[12]{0:T(128)S(1)} %stack.55.refs_0_, bf16[128,2048]{1,0:T(8,128)(2,1)S(1)} %attention.1.refs_1_.refs_2_, bf16[128,2048]{1,0:T(8,128)(2,1)S(1)} %attention.1.refs_1_.refs_2_, bf16[128,2048]{1,0:T(8,128)(2,1)S(1)} %collective-permute-done.11.refs_3_.refs_4_, ...), custom_call_target="tpu_custom_call" | custom-call | tf_op jit(solution)/shard_map/projection/pallas_call | solution.py:191
  122.0 81.7 %all_to_all.20 = bf16[128,48,512]{2,1,0:T(8,128)(2,1)} all-to-all(bf16[128,48,512]{2,1,0:T(8,128)(2,1)S(1)} %get-tuple-element.47), channel_id=1, replica_groups=mesh['zh'=2,'y'=4,'x'=4,'c'=2,'zl'=2] {'zh','y','x','c','zl'}, dimensions={0} | all-to-all | bytes 12582912 | tf_op jit(solution)/shard_map/all_to_all | solution.py:510
  203.7 23.7 %expert.1 = bf16[2,16,4,48,512]{4,3,2,1,0:T(8,128)(2,1)} custom-call(bf16[2,16,4,48,512]{4,3,2,1,0:T(8,128)(2,1)} %bitcast.44, bf16[1,4096,768]{2,1,0:T(8,128)(2,1)} %gate_w.1, bf16[1,4096,768]{2,1,0:T(8,128)(2,1)} %up_w.1, bf16[1,768,4096]{2,1,0:T(8,128)(2,1)} %down_w.1), custom_call_target="tpu_custom_call" | custom-call | tf_op jit(solution)/shard_map/expert/pallas_call | solution.py:312
  227.4 81.5 %all_to_all.21.answers = bf16[128,48,512]{2,1,0:T(8,128)(2,1)S(1)} all-to-all(bf16[128,48,512]{2,1,0:T(8,128)(2,1)} %bitcast.45), channel_id=1, replica_groups=mesh['zh'=2,'y'=4,'x'=4,'c'=2,'zl'=2] {'zh','y','x','c','zl'}, dimensions={0} | all-to-all | bytes 12582912 | tf_op jit(solution)/shard_map/all_to_all | solution.py:514
  308.9 4.2 %combine.1 = bf16[512,512]{1,0:T(8,128)(2,1)S(1)} custom-call(f32[128,512]{1,0:T(8,128)S(1)} %get-tuple-element.41.refs_23_.slots, f32[128,512]{1,0:T(8,128)S(1)} %copy-done.2, bf16[128,48,512]{2,1,0:T(8,128)(2,1)S(1)} %all_to_all.21.answers, bf16[512,512]{1,0:T(8,128)(2,1)S(1)} %get-tuple-element.48.hidden), custom_call_target="tpu_custom_call" | custom-call | tf_op jit(solution)/shard_map/combine/pallas_call | solution.py:368
  313.1 12.3 %all_to_all.22 = bf16[8,64,512]{2,1,0:T(8,128)(2,1)S(1)} all-to-all(bf16[8,64,512]{2,1,0:T(8,128)(2,1)S(1)} %bitcast.43), channel_id=1, replica_groups=mesh['zh'=2,'y'=4,'x'=4,'c'=2,'zl'=2] {'zh','c','zl'}, dimensions={0} | all-to-all | bytes 1048576 | tf_op jit(solution)/shard_map/all_to_all | solution.py:516
  325.4 0.8 copy.40
  (60 shorter events, 0.6 us)
Async XLA Ops:
  6.5 7.0 %copy-start.6 = (bf16[64,4096]{1,0:T(8,128)(2,1)S(1)}, bf16[64,4096]{1,0:T(8,128)(2,1)}, u32[]{:S(2)}) copy-start(bf16[64,4096]{1,0:T(8,128)(2,1)} %param.18) | copy-start | bytes 1572868
  8.1 14.9 %collective-permute-start.2 = (bf16[128,256]{1,0:T(8,128)(2,1)S(1)}, bf16[128,256]{1,0:T(8,128)(2,1)S(1)}, u32[]{:S(2)}, u32[]{:S(2)}) collective-permute-start(bf16[128,256]{1,0:T(8,128)(2,1)S(1)} %get-tuple-element.52), channel_id=1, source_target_pairs={{0,12},{4,0},{8,4},{12,8},{1,13},{5,1},{9,5},{13,9},{2,14},{6,2},{... | collective-permute-start | bytes 196616 | tf_op jit(solution)/shard_map/ppermute | solution.py:387
  8.5 14.6 %collective-permute-start.1 = (bf16[128,256]{1,0:T(8,128)(2,1)S(1)}, bf16[128,256]{1,0:T(8,128)(2,1)S(1)}, u32[]{:S(2)}, u32[]{:S(2)}) collective-permute-start(bf16[128,256]{1,0:T(8,128)(2,1)S(1)} %get-tuple-element.52), channel_id=1, source_target_pairs={{0,8},{4,12},{8,0},{12,4},{1,9},{5,13},{9,1},{13,5},{2,10},{6,14},... | collective-permute-start | bytes 196616 | tf_op jit(solution)/shard_map/ppermute | solution.py:387
  10.9 12.1 %collective-permute-start = (bf16[128,256]{1,0:T(8,128)(2,1)S(1)}, bf16[128,256]{1,0:T(8,128)(2,1)S(1)}, u32[]{:S(2)}, u32[]{:S(2)}) collective-permute-start(bf16[128,256]{1,0:T(8,128)(2,1)S(1)} %get-tuple-element.52), channel_id=1, source_target_pairs={{0,4},{4,8},{8,12},{12,0},{1,5},{5,9},{9,13},{13,1},{2,6},{6,10},{... | collective-permute-start | bytes 196616 | tf_op jit(solution)/shard_map/ppermute | solution.py:387
  14.6 6.8 %copy-start.8 = (s32[8]{0:T(128)S(1)}, s32[8]{0:T(128)}, u32[]{:S(2)}) copy-start(s32[8]{0:T(128)} %param.16) | copy-start | bytes 100
  14.6 7.1 %copy-start.7 = (s32[17]{0:T(128)S(1)}, s32[17]{0:T(128)}, u32[]{:S(2)}) copy-start(s32[17]{0:T(128)} %constant.90) | copy-start | bytes 208
  14.6 31.6 %all-to-all-start = ((bf16[8,112,512]{2,1,0:T(8,128)(2,1)}), bf16[8,112,512]{2,1,0:T(8,128)(2,1)S(1)}, u32[]{:S(2)}, u32[]{:S(2)}) async-start(bf16[8,112,512]{2,1,0:T(8,128)(2,1)} %pad_maximum_fusion), calls=%async_computation | async-start | bytes 1835008 | tf_op jit(solution)/shard_map/all_to_all | solution.py:477
  21.3 74.9 %all-gather.2.cloned.1.call-start = ((), (), s32[]{:S(2)}) async-start(), calls=%async_computation.4 | async-start | bytes 4456448 | tf_op jit(solution)/shard_map/all_gather | solution.py:487
  23.1 11.8 %collective-permute-start.4 = (bf16[512,256]{1,0:T(8,128)(2,1)S(1)}, bf16[512,256]{1,0:T(8,128)(2,1)S(1)}, u32[]{:S(2)}, u32[]{:S(2)}) collective-permute-start(bf16[512,256]{1,0:T(8,128)(2,1)S(1)} %pad_maximum_fusion.1), channel_id=1, source_target_pairs={{0,48},{16,64},{32,80},{48,96},{64,112},{80,0},{96,16},{112,32},{1... | collective-permute-start | bytes 786440 | tf_op jit(solution)/shard_map/ppermute | solution.py:392
  25.9 12.9 %collective-permute-start.3 = (bf16[512,256]{1,0:T(8,128)(2,1)S(1)}, bf16[512,256]{1,0:T(8,128)(2,1)S(1)}, u32[]{:S(2)}, u32[]{:S(2)}) collective-permute-start(bf16[512,256]{1,0:T(8,128)(2,1)S(1)} %pad_maximum_fusion.1), channel_id=1, source_target_pairs={{0,16},{16,32},{32,48},{48,64},{64,80},{80,96},{96,112},{112,0},{1... | collective-permute-start | bytes 786440 | tf_op jit(solution)/shard_map/ppermute | solution.py:392
  46.2 12.3 %copy-start.4 = (bf16[8,112,512]{2,1,0:T(8,128)(2,1)}, bf16[8,112,512]{2,1,0:T(8,128)(2,1)S(1)}, u32[]{:S(2)}) copy-start(bf16[8,112,512]{2,1,0:T(8,128)(2,1)S(1)} %all-to-all-done) | copy-start | bytes 2752516
  47.0 11.3 %collective-permute-start.7 = (bf16[512,256]{1,0:T(8,128)(2,1)S(1)}, bf16[512,256]{1,0:T(8,128)(2,1)S(1)}, u32[]{:S(2)}, u32[]{:S(2)}) collective-permute-start(bf16[512,256]{1,0:T(8,128)(2,1)S(1)} %pad_maximum_fusion.1), channel_id=1, source_target_pairs={{0,64},{16,80},{32,96},{48,112},{64,0},{80,16},{96,32},{112,48},{1... | collective-permute-start | bytes 786440 | tf_op jit(solution)/shard_map/ppermute | solution.py:392
  47.7 10.6 %collective-permute-start.6 = (bf16[256,256]{1,0:T(8,128)(2,1)S(1)}, bf16[256,256]{1,0:T(8,128)(2,1)S(1)}, u32[]{:S(2)}, u32[]{:S(2)}) collective-permute-start(bf16[256,256]{1,0:T(8,128)(2,1)S(1)} %slice.56), channel_id=1, source_target_pairs={{0,112},{16,0},{32,16},{48,32},{64,48},{80,64},{96,80},{112,96},{1... | collective-permute-start | bytes 393224 | tf_op jit(solution)/shard_map/ppermute | solution.py:392
  47.8 10.5 %collective-permute-start.5 = (bf16[256,256]{1,0:T(8,128)(2,1)S(1)}, bf16[256,256]{1,0:T(8,128)(2,1)S(1)}, u32[]{:S(2)}, u32[]{:S(2)}) collective-permute-start(bf16[256,256]{1,0:T(8,128)(2,1)S(1)} %slice.55), channel_id=1, source_target_pairs={{0,16},{16,32},{32,48},{48,64},{64,80},{80,96},{96,112},{112,0},{1... | collective-permute-start | bytes 393224 | tf_op jit(solution)/shard_map/ppermute | solution.py:392
  58.6 4.4 %collective-permute-start.8 = (bf16[2176,256]{1,0:T(8,128)(2,1)S(1)}, bf16[2176,256]{1,0:T(8,128)(2,1)S(1)}, u32[]{:S(2)}, u32[]{:S(2)}) collective-permute-start(bf16[2176,256]{1,0:T(8,128)(2,1)S(1)} %constant_dynamic-update-slice_fusion.2.kv), channel_id=1, source_target_pairs={{0,2},{2,0},{1,3},{3,1},{4,6},{6,4},{5,7},{7,5},{8,10},{10,8},{9,1... | collective-permute-start | bytes 3342344 | tf_op jit(solution)/shard_map/ppermute | solution.py:401
  63.0 1.0 copy-start.3
  64.0 16.8 %copy-start.5 = (bf16[8,112,512]{2,1,0:T(8,128)(2,1)S(1)}, bf16[8,112,512]{2,1,0:T(8,128)(2,1)}, u32[]{:S(2)}) copy-start(bf16[8,112,512]{2,1,0:T(8,128)(2,1)} %copy-done.4) | copy-start | bytes 2752516
  70.0 22.9 %collective-permute-start.10 = (bf16[128,2048]{1,0:T(8,128)(2,1)S(1)}, bf16[128,2048]{1,0:T(8,128)(2,1)S(1)}, u32[]{:S(2)}, u32[]{:S(2)}) collective-permute-start(bf16[128,2048]{1,0:T(8,128)(2,1)S(1)} %attention.1.refs_1_.refs_2_), channel_id=1, source_target_pairs={{0,65},{1,64},{64,1},{65,0},{2,67},{3,66},{66,3},{67,2},{4,69},{5,... | collective-permute-start | bytes 1572872 | tf_op jit(solution)/shard_map/ppermute | solution.py:436
  80.8 12.9 %collective-permute-start.9 = (bf16[128,2048]{1,0:T(8,128)(2,1)S(1)}, bf16[128,2048]{1,0:T(8,128)(2,1)S(1)}, u32[]{:S(2)}, u32[]{:S(2)}) collective-permute-start(bf16[128,2048]{1,0:T(8,128)(2,1)S(1)} %attention.1.refs_1_.refs_2_), channel_id=1, source_target_pairs={{0,1},{1,0},{64,65},{65,64},{2,3},{3,2},{66,67},{67,66},{4,5},{5,4... | collective-permute-start | bytes 1572872 | tf_op jit(solution)/shard_map/ppermute | solution.py:435
  82.1 0.7 copy-start.1
  82.8 24.9 %collective-permute-start.11 = (bf16[128,2048]{1,0:T(8,128)(2,1)S(1)}, bf16[128,2048]{1,0:T(8,128)(2,1)S(1)}, u32[]{:S(2)}, u32[]{:S(2)}) collective-permute-start(bf16[128,2048]{1,0:T(8,128)(2,1)S(1)} %attention.1.refs_1_.refs_2_), channel_id=1, source_target_pairs={{0,2},{2,0},{1,3},{3,1},{4,6},{6,4},{5,7},{7,5},{8,10},{10,8},{9,1... | collective-permute-start | bytes 1572872 | tf_op jit(solution)/shard_map/ppermute | solution.py:433
  96.1 7.4 %collective-permute-start.16 = (bf16[64,2048]{1,0:T(8,128)(2,1)S(1)}, bf16[64,2048]{1,0:T(8,128)(2,1)}, u32[]{:S(2)}, u32[]{:S(2)}) collective-permute-start(bf16[64,2048]{1,0:T(8,128)(2,1)S(1)} %slice.65), channel_id=1, source_target_pairs={{0,1},{1,0},{64,65},{65,64},{2,3},{3,2},{66,67},{67,66},{4,5},{5,4... | collective-permute-start | bytes 786440 | tf_op jit(solution)/shard_map/ppermute | solution.py:440
  97.5 8.3 %collective-permute-start.14 = (bf16[64,2048]{1,0:T(8,128)(2,1)S(1)}, bf16[64,2048]{1,0:T(8,128)(2,1)}, u32[]{:S(2)}, u32[]{:S(2)}) collective-permute-start(bf16[64,2048]{1,0:T(8,128)(2,1)S(1)} %slice.64), channel_id=1, source_target_pairs={{0,65},{1,64},{64,1},{65,0},{2,67},{3,66},{66,3},{67,2},{4,69},{5,... | collective-permute-start | bytes 786440 | tf_op jit(solution)/shard_map/ppermute | solution.py:439
  99.5 9.7 %collective-permute-start.12 = (bf16[128,2048]{1,0:T(8,128)(2,1)S(1)}, bf16[128,2048]{1,0:T(8,128)(2,1)S(1)}, u32[]{:S(2)}, u32[]{:S(2)}) collective-permute-start(bf16[128,2048]{1,0:T(8,128)(2,1)S(1)} %collective-permute-done.9.refs_5_.refs_6_), channel_id=1, source_target_pairs={{0,2},{2,0},{1,3},{3,1},{4,6},{6,4},{5,7},{7,5},{8,10},{10,8},{9,1... | collective-permute-start | bytes 1572872 | tf_op jit(solution)/shard_map/ppermute | solution.py:433
  100.7 8.4 %collective-permute-start.13 = (bf16[128,2048]{1,0:T(8,128)(2,1)S(1)}, bf16[128,2048]{1,0:T(8,128)(2,1)}, u32[]{:S(2)}, u32[]{:S(2)}) collective-permute-start(bf16[128,2048]{1,0:T(8,128)(2,1)S(1)} %collective-permute-done.10.refs_9_.refs_10_), channel_id=1, source_target_pairs={{0,2},{2,0},{1,3},{3,1},{4,6},{6,4},{5,7},{7,5},{8,10},{10,8},{9,1... | collective-permute-start | bytes 1572872 | tf_op jit(solution)/shard_map/ppermute | solution.py:433
  103.5 4.2 %collective-permute-start.17 = (bf16[64,2048]{1,0:T(8,128)(2,1)}, bf16[64,2048]{1,0:T(8,128)(2,1)}, u32[]{:S(2)}, u32[]{:S(2)}) collective-permute-start(bf16[64,2048]{1,0:T(8,128)(2,1)} %collective-permute-done.16.refs_17_.refs_18_), channel_id=1, source_target_pairs={{0,2},{2,0},{1,3},{3,1},{4,6},{6,4},{5,7},{7,5},{8,10},{10,8},{9,1... | collective-permute-start | bytes 786440 | tf_op jit(solution)/shard_map/ppermute | solution.py:433
  105.8 3.4 %collective-permute-start.15 = (bf16[64,2048]{1,0:T(8,128)(2,1)}, bf16[64,2048]{1,0:T(8,128)(2,1)}, u32[]{:S(2)}, u32[]{:S(2)}) collective-permute-start(bf16[64,2048]{1,0:T(8,128)(2,1)} %collective-permute-done.14.refs_13_.refs_14_), channel_id=1, source_target_pairs={{0,2},{2,0},{1,3},{3,1},{4,6},{6,4},{5,7},{7,5},{8,10},{10,8},{9,1... | collective-permute-start | bytes 786440 | tf_op jit(solution)/shard_map/ppermute | solution.py:433
  109.1 2.2 copy-start
  227.4 81.5 %copy-start.2 = (f32[128,512]{1,0:T(8,128)S(1)}, f32[128,512]{1,0:T(8,128)}, u32[]{:S(2)}) copy-start(f32[128,512]{1,0:T(8,128)} %copy-done.1) | copy-start | bytes 786436
Sparse Core Ops, SparseCore 0:
  47.1 48.9 all-gather.1

commit v5 on v4

--- a/solution.py
+++ b/solution.py
@@ -476,9 +476,7 @@
     )
     got = lax.all_to_all(sent, LINE, split_axis=0, concat_axis=0, tiled=True)
     tables = key_tables(tokens) + query_tables(tokens, lengths)
-    got, before, third, *tables = lax.optimization_barrier(
-        (got, shift_row(row, 1), shift_row(row, 3)) + tables
-    )
+    got, before, third = lax.optimization_barrier((got, shift_row(row, 1), shift_row(row, 3)))
     half = row.shape[0] // 2
     second, rest, oldest = lax.optimization_barrier(
         (shift_row(before[:half], 1), shift_row(third[half:], -1), shift_row(row, 4))
@@ -503,8 +501,8 @@
                 halves.append((high_part * 2 + c) * 2 + (zl ^ k))
     places = [(zh ^ h) * 2 + (core ^ c) for h in range(2) for c in range(2)]
     table = jnp.stack(halves + places).astype(jnp.int32)
-    blocks, (line_residual, slots, weights, weight) = gather_attended(
-        attended, (line_residual, slots, weights, weight)
+    blocks, (line_residual, slots, weights) = gather_attended(
+        attended, (line_residual, slots, weights)
     )
     hidden, outgoing = project(table, blocks, weight, line_residual, slots)
     incoming = lax.all_to_all(outgoing, AXES, split_axis=0, concat_axis=0, tiled=True)

time: 335 us -> 328 us (0.979)
  blocking collectives: 175 us -> 184 us
  starting transfers between devices: 37.3 us -> 29.4 us
  waiting for transfers between devices: 45.2 us -> 38.7 us
    ppermute x1, starting transfers between devices: 10.8 us -> 2.26 us  [gather_attended(): far = lax.ppermute(own, Z, flipped(4, 3))]
    all_to_all x1, blocking collectives: 81.7 us -> 90.2 us  [body(): lax.all_to_all(outgoing, AXES, split_axis=0, concat_axis=0, tiled=True)]
    ppermute x3, waiting for transfers between devices: 0.01 us -> 4.17 us  [gather_row(): row = [own] + [lax.ppermute(own, 'x', rotated(4, k)) for k in range(1, 4)]]
    all_to_all x1, waiting for transfers between devices: 7.34 us -> 3.39 us  [body(): got = lax.all_to_all(sent, LINE, split_axis=0, concat_axis=0, tiled=True)]
  transfers between devices with their start and end apart: 20 -> 20, of which waited for: 11 -> 12; matrix products, arithmetic and copies ran while one was open for 3% -> 2% of each run, Pallas kernels for 2% -> 2%
where the time goes in v5:
time: 328 us
  blocking collectives  184 us (56%)
  Pallas kernels  45.7 us (14%)
  waiting for transfers between devices  38.7 us (12%)
  starting transfers between devices  29.4 us (9%)
  between operations  13.7 us (4%)
  local copies, waits for them, and re-layouts  10.7 us (3%)
  other arithmetic  5.83 us (2%)
    all_to_all x1, blocking collectives, body(): lax.all_to_all(outgoing, AXES, split_axis=0, concat_axis=0, tiled=True)  90.2 us
    all_to_all x1, blocking collectives, body(): lax.all_to_all(produced, AXES, split_axis=0, concat_axis=0, tiled=True)  81.5 us
    pallas_call x1, Pallas kernels, expert(): pl.pallas_call(expert_kernel, grid=(FIRST + SECOND,), in_specs=[pl.BlockS...  23.8 us
    ppermute x5, waiting for transfers between devices, shift_row(): return lax.ppermute(row, ('zh', 'y'), rotated(8, step))  16.4 us
    all_to_all x1, blocking collectives, body(): lax.all_to_all(mixed.reshape(GROUP, own_rows, width), LINE, split_axis=0,...  12.3 us
    pallas_call x1, Pallas kernels, project(): pl.pallas_call(functools.partial(projection_kernel, steps), grid=(steps +...  10.6 us
    ppermute x1, waiting for transfers between devices, gather_attended(): far = lax.ppermute(own, Z, flipped(4, 3))  9.25 us
  transfers between devices with their start and end apart: 20, of which 12 were waited for; matrix products, arithmetic and copies ran while one was open for 2% of the time, Pallas kernels for 2%

profile of v5, /device:TPU:5, one launch (start us, length us, event | category | flops | bytes accessed | tf_op | source)
XLA Modules:
  0.0 327.9 jit_solution(1598494525747166741)
XLA Ops:
  6.5 0.7 convert_element_type.14
  7.2 0.7 convert_element_type.15
  7.9 0.1 copy.40
  8.0 0.1 reshape.142
  8.1 1.0 copy.52
  9.1 1.1 copy.51
  10.2 1.0 pad_maximum_fusion
  11.2 6.1 %all-to-all-start = ((bf16[8,112,512]{2,1,0:T(8,128)(2,1)}), bf16[8,112,512]{2,1,0:T(8,128)(2,1)S(1)}, u32[]{:S(2)}, u32[]{:S(2)}) async-start(bf16[8,112,512]{2,1,0:T(8,128)(2,1)} %pad_maximum_fusion), calls=%async_computation | async-start | bytes 1835008 | tf_op jit(solution)/shard_map/all_to_all | solution.py:477
  17.5 0.3 collective-permute-start.2
  17.8 2.5 collective-permute-start.1
  20.2 1.0 collective-permute-done.2
  21.2 1.5 collective-permute-done.1
  22.7 1.7 collective-permute-done
  24.4 2.8 collective-permute-start.4
  27.2 1.3 collective-permute-start.3
  28.5 5.5 %collective-permute-done.4 = bf16[512,256]{1,0:T(8,128)(2,1)S(1)} collective-permute-done((bf16[512,256]{1,0:T(8,128)(2,1)S(1)}, bf16[512,256]{1,0:T(8,128)(2,1)S(1)}, u32[]{:S(2)}, u32[]{:S(2)}) %collective-permute-start.4) | collective-permute-done | bytes 262176 | tf_op jit(solution)/shard_map/ppermute | solution.py:392
  34.0 4.9 %collective-permute-done.3 = bf16[512,256]{1,0:T(8,128)(2,1)S(1)} collective-permute-done((bf16[512,256]{1,0:T(8,128)(2,1)S(1)}, bf16[512,256]{1,0:T(8,128)(2,1)S(1)}, u32[]{:S(2)}, u32[]{:S(2)}) %collective-permute-start.3) | collective-permute-done | bytes 262176 | tf_op jit(solution)/shard_map/ppermute | solution.py:392
  38.9 3.4 %all-to-all-done = bf16[8,112,512]{2,1,0:T(8,128)(2,1)S(1)} async-done(((bf16[8,112,512]{2,1,0:T(8,128)(2,1)}), bf16[8,112,512]{2,1,0:T(8,128)(2,1)S(1)}, u32[]{:S(2)}, u32[]{:S(2)}) %all-to-all-start) | async-done | bytes 917536 | tf_op jit(solution)/shard_map/all_to_all | solution.py:477
  42.3 0.7 slice.65
  43.2 0.1 reshape.138
  43.3 0.2 reduce-window.9
  43.5 0.1 select_reduce_fusion
  43.6 0.1 broadcast_bitcast_fusion
  43.7 0.1 fusion.3
  43.7 0.1 broadcast_multiply_fusion
  43.8 0.7 fusion.7
  44.6 0.1 reshape.139
  44.7 0.7 slice.55
  45.3 0.6 slice.56
  46.0 1.5 collective-permute-start.5
  47.4 0.1 fusion.6
  47.7 0.1 copy.43.qstart
  47.8 4.5 %collective-permute-done.7 = bf16[512,256]{1,0:T(8,128)(2,1)S(1)} collective-permute-done((bf16[512,256]{1,0:T(8,128)(2,1)S(1)}, bf16[512,256]{1,0:T(8,128)(2,1)S(1)}, u32[]{:S(2)}, u32[]{:S(2)}) %collective-permute-start.7) | collective-permute-done | bytes 262176 | tf_op jit(solution)/shard_map/ppermute | solution.py:392
  52.3 1.5 collective-permute-done.5
  53.8 0.1 fusion
  54.0 0.9 constant_dynamic-update-slice_fusion.4
  54.9 3.4 %collective-permute-start.8 = (bf16[2176,256]{1,0:T(8,128)(2,1)S(1)}, bf16[2176,256]{1,0:T(8,128)(2,1)S(1)}, u32[]{:S(2)}, u32[]{:S(2)}) collective-permute-start(bf16[2176,256]{1,0:T(8,128)(2,1)S(1)} %constant_dynamic-update-slice_fusion.2.kv), channel_id=1, source_target_pairs={{0,2},{2,0},{1,3},{3,1},{4,6},{6,4},{5,7},{7,5},{8,10},{10,8},{9,1... | collective-permute-start | bytes 3342344 | tf_op jit(solution)/shard_map/ppermute | solution.py:401
  58.4 2.6 pad_add_fusion.lim
  61.1 6.1 %attention.1.refs_1_.refs_2_ = bf16[128,2048]{1,0:T(8,128)(2,1)S(1)} custom-call(s32[4]{0:T(128)S(1)} %pad_add_fusion.lim, s32[6]{0:T(128)S(1)} %get-tuple-element.52.low, s32[6]{0:T(128)S(1)} %get-tuple-element.51.high, bf16[128,2048]{1,0:T(8,128)(2,1)S(1)} %copy-done.3, bf16[2176,256]{1,0:T(8,128)(2,1)S(1)} %constant_dynamic-update-slice_fusion.2.kv, ...), custom_call_target="tpu_custom_call" | custom-call | flops 10000000000 | bytes 4000000 | tf_op jit(solution)/shard_map/attention/pallas_call | solution.py:104
  67.2 2.3 collective-permute-start.10
  69.5 0.9 collective-permute-start.9
  70.4 0.1 reshape.143
  70.6 0.1 copy.44
  70.7 0.9 routing.1
  71.6 0.7 copy-done.1
  72.3 0.6 collective-permute-start.11
  72.9 9.2 %collective-permute-done.10.refs_9_.refs_10_ = bf16[128,2048]{1,0:T(8,128)(2,1)S(1)} collective-permute-done((bf16[128,2048]{1,0:T(8,128)(2,1)S(1)}, bf16[128,2048]{1,0:T(8,128)(2,1)S(1)}, u32[]{:S(2)}, u32[]{:S(2)}) %collective-permute-start.10) | collective-permute-done | bytes 524320 | tf_op jit(solution)/shard_map/ppermute | solution.py:436
  82.1 0.7 collective-permute-done.9.refs_5_.refs_6_
  82.8 0.9 collective-permute-start.16
  83.8 1.3 collective-permute-start.14
  85.1 1.3 collective-permute-start.12
  86.4 3.4 %collective-permute-done.16.refs_17_.refs_18_ = bf16[64,2048]{1,0:T(8,128)(2,1)} collective-permute-done((bf16[64,2048]{1,0:T(8,128)(2,1)S(1)}, bf16[64,2048]{1,0:T(8,128)(2,1)}, u32[]{:S(2)}, u32[]{:S(2)}) %collective-permute-start.16) | collective-permute-done | bytes 262176 | tf_op jit(solution)/shard_map/ppermute | solution.py:440
  89.8 2.0 collective-permute-start.17
  91.7 2.2 collective-permute-start.15
  93.9 0.1 stack.55.refs_0_
  94.0 1.4 collective-permute-done.15.refs_15_.refs_16_
  95.4 2.2 copy-done
  97.6 10.6 %projection.1 = (bf16[512,512]{1,0:T(8,128)(2,1)S(1)}, bf16[128,48,512]{2,1,0:T(8,128)(2,1)S(1)}) custom-call(s32[12]{0:T(128)S(1)} %stack.55.refs_0_, bf16[128,2048]{1,0:T(8,128)(2,1)S(1)} %attention.1.refs_1_.refs_2_, bf16[128,2048]{1,0:T(8,128)(2,1)S(1)} %attention.1.refs_1_.refs_2_, bf16[128,2048]{1,0:T(8,128)(2,1)S(1)} %collective-permute-done.11.refs_3_.refs_4_, ...), custom_call_target="tpu_custom_call" | custom-call | tf_op jit(solution)/shard_map/projection/pallas_call | solution.py:191
  108.2 90.2 %all_to_all.20 = bf16[128,48,512]{2,1,0:T(8,128)(2,1)} all-to-all(bf16[128,48,512]{2,1,0:T(8,128)(2,1)S(1)} %get-tuple-element.33), channel_id=1, replica_groups=mesh['zh'=2,'y'=4,'x'=4,'c'=2,'zl'=2] {'zh','y','x','c','zl'}, dimensions={0} | all-to-all | bytes 12582912 | tf_op jit(solution)/shard_map/all_to_all | solution.py:508
  198.4 23.8 %expert.1 = bf16[2,16,4,48,512]{4,3,2,1,0:T(8,128)(2,1)} custom-call(bf16[2,16,4,48,512]{4,3,2,1,0:T(8,128)(2,1)} %bitcast.44, bf16[1,4096,768]{2,1,0:T(8,128)(2,1)} %gate_w.1, bf16[1,4096,768]{2,1,0:T(8,128)(2,1)} %up_w.1, bf16[1,768,4096]{2,1,0:T(8,128)(2,1)} %down_w.1), custom_call_target="tpu_custom_call" | custom-call | tf_op jit(solution)/shard_map/expert/pallas_call | solution.py:312
  222.2 81.5 %all_to_all.21.answers = bf16[128,48,512]{2,1,0:T(8,128)(2,1)S(1)} all-to-all(bf16[128,48,512]{2,1,0:T(8,128)(2,1)} %bitcast.45), channel_id=1, replica_groups=mesh['zh'=2,'y'=4,'x'=4,'c'=2,'zl'=2] {'zh','y','x','c','zl'}, dimensions={0} | all-to-all | bytes 12582912 | tf_op jit(solution)/shard_map/all_to_all | solution.py:512
  303.7 4.2 %combine.1 = bf16[512,512]{1,0:T(8,128)(2,1)S(1)} custom-call(f32[128,512]{1,0:T(8,128)S(1)} %get-tuple-element.28.refs_23_.slots, f32[128,512]{1,0:T(8,128)S(1)} %copy-done.2, bf16[128,48,512]{2,1,0:T(8,128)(2,1)S(1)} %all_to_all.21.answers, bf16[512,512]{1,0:T(8,128)(2,1)S(1)} %get-tuple-element.34.hidden), custom_call_target="tpu_custom_call" | custom-call | tf_op jit(solution)/shard_map/combine/pallas_call | solution.py:368
  307.9 12.3 %all_to_all.22 = bf16[8,64,512]{2,1,0:T(8,128)(2,1)S(1)} all-to-all(bf16[8,64,512]{2,1,0:T(8,128)(2,1)S(1)} %bitcast.43), channel_id=1, replica_groups=mesh['zh'=2,'y'=4,'x'=4,'c'=2,'zl'=2] {'zh','c','zl'}, dimensions={0} | all-to-all | bytes 1048576 | tf_op jit(solution)/shard_map/all_to_all | solution.py:514
  320.2 0.8 copy.48
  (58 shorter events, 0.7 us)
Async XLA Ops:
  11.2 6.2 %copy-start.4 = (bf16[128,128]{1,0:T(8,128)(2,1)S(1)}, bf16[128,128]{1,0:T(8,128)(2,1)}, u32[]{:S(2)}) copy-start(bf16[128,128]{1,0:T(8,128)(2,1)} %param.14) | copy-start | bytes 98308
  11.2 6.2 %copy-start.5 = (bf16[128,128]{1,0:T(8,128)(2,1)S(1)}, bf16[128,128]{1,0:T(8,128)(2,1)}, u32[]{:S(2)}) copy-start(bf16[128,128]{1,0:T(8,128)(2,1)} %param.15) | copy-start | bytes 98308
  11.2 31.1 %all-to-all-start = ((bf16[8,112,512]{2,1,0:T(8,128)(2,1)}), bf16[8,112,512]{2,1,0:T(8,128)(2,1)S(1)}, u32[]{:S(2)}, u32[]{:S(2)}) async-start(bf16[8,112,512]{2,1,0:T(8,128)(2,1)} %pad_maximum_fusion), calls=%async_computation | async-start | bytes 1835008 | tf_op jit(solution)/shard_map/all_to_all | solution.py:477
  17.4 25.9 %copy-start.7 = (s32[8]{0:T(128)S(1)}, s32[8]{0:T(128)}, u32[]{:S(2)}) copy-start(s32[8]{0:T(128)} %param.16) | copy-start | bytes 100
  17.4 26.3 %copy-start.6 = (s32[17]{0:T(128)S(1)}, s32[17]{0:T(128)}, u32[]{:S(2)}) copy-start(s32[17]{0:T(128)} %constant.90) | copy-start | bytes 208
  17.4 78.1 %all-gather.2.cloned.1.call-start = ((), (), s32[]{:S(2)}) async-start(), calls=%async_computation.4 | async-start | bytes 4456448 | tf_op jit(solution)/shard_map/all_gather | solution.py:485
  17.5 3.8 %collective-permute-start.2 = (bf16[128,256]{1,0:T(8,128)(2,1)S(1)}, bf16[128,256]{1,0:T(8,128)(2,1)S(1)}, u32[]{:S(2)}, u32[]{:S(2)}) collective-permute-start(bf16[128,256]{1,0:T(8,128)(2,1)S(1)} %get-tuple-element.37), channel_id=1, source_target_pairs={{0,12},{4,0},{8,4},{12,8},{1,13},{5,1},{9,5},{13,9},{2,14},{6,2},{... | collective-permute-start | bytes 196616 | tf_op jit(solution)/shard_map/ppermute | solution.py:387
  17.8 4.9 %collective-permute-start.1 = (bf16[128,256]{1,0:T(8,128)(2,1)S(1)}, bf16[128,256]{1,0:T(8,128)(2,1)S(1)}, u32[]{:S(2)}, u32[]{:S(2)}) collective-permute-start(bf16[128,256]{1,0:T(8,128)(2,1)S(1)} %get-tuple-element.37), channel_id=1, source_target_pairs={{0,8},{4,12},{8,0},{12,4},{1,9},{5,13},{9,1},{13,5},{2,10},{6,14},... | collective-permute-start | bytes 196616 | tf_op jit(solution)/shard_map/ppermute | solution.py:387
  20.2 4.2 %collective-permute-start = (bf16[128,256]{1,0:T(8,128)(2,1)S(1)}, bf16[128,256]{1,0:T(8,128)(2,1)S(1)}, u32[]{:S(2)}, u32[]{:S(2)}) collective-permute-start(bf16[128,256]{1,0:T(8,128)(2,1)S(1)} %get-tuple-element.37), channel_id=1, source_target_pairs={{0,4},{4,8},{8,12},{12,0},{1,5},{5,9},{9,13},{13,1},{2,6},{6,10},{... | collective-permute-start | bytes 196616 | tf_op jit(solution)/shard_map/ppermute | solution.py:387
  24.4 9.5 %collective-permute-start.4 = (bf16[512,256]{1,0:T(8,128)(2,1)S(1)}, bf16[512,256]{1,0:T(8,128)(2,1)S(1)}, u32[]{:S(2)}, u32[]{:S(2)}) collective-permute-start(bf16[512,256]{1,0:T(8,128)(2,1)S(1)} %pad_maximum_fusion.1), channel_id=1, source_target_pairs={{0,48},{16,64},{32,80},{48,96},{64,112},{80,0},{96,16},{112,32},{1... | collective-permute-start | bytes 786440 | tf_op jit(solution)/shard_map/ppermute | solution.py:392
  27.2 11.7 %collective-permute-start.3 = (bf16[512,256]{1,0:T(8,128)(2,1)S(1)}, bf16[512,256]{1,0:T(8,128)(2,1)S(1)}, u32[]{:S(2)}, u32[]{:S(2)}) collective-permute-start(bf16[512,256]{1,0:T(8,128)(2,1)S(1)} %pad_maximum_fusion.1), channel_id=1, source_target_pairs={{0,16},{16,32},{32,48},{48,64},{64,80},{80,96},{96,112},{112,0},{1... | collective-permute-start | bytes 786440 | tf_op jit(solution)/shard_map/ppermute | solution.py:392
  43.8 8.5 %collective-permute-start.7 = (bf16[512,256]{1,0:T(8,128)(2,1)S(1)}, bf16[512,256]{1,0:T(8,128)(2,1)S(1)}, u32[]{:S(2)}, u32[]{:S(2)}) collective-permute-start(bf16[512,256]{1,0:T(8,128)(2,1)S(1)} %pad_maximum_fusion.1), channel_id=1, source_target_pairs={{0,64},{16,80},{32,96},{48,112},{64,0},{80,16},{96,32},{112,48},{1... | collective-permute-start | bytes 786440 | tf_op jit(solution)/shard_map/ppermute | solution.py:392
  46.0 6.3 %collective-permute-start.6 = (bf16[256,256]{1,0:T(8,128)(2,1)}, bf16[256,256]{1,0:T(8,128)(2,1)S(1)}, u32[]{:S(2)}, u32[]{:S(2)}) collective-permute-start(bf16[256,256]{1,0:T(8,128)(2,1)} %slice.56), channel_id=1, source_target_pairs={{0,112},{16,0},{32,16},{48,32},{64,48},{80,64},{96,80},{112,96},{1... | collective-permute-start | bytes 393224 | tf_op jit(solution)/shard_map/ppermute | solution.py:392
  46.0 7.8 %collective-permute-start.5 = (bf16[256,256]{1,0:T(8,128)(2,1)}, bf16[256,256]{1,0:T(8,128)(2,1)}, u32[]{:S(2)}, u32[]{:S(2)}) collective-permute-start(bf16[256,256]{1,0:T(8,128)(2,1)} %slice.55), channel_id=1, source_target_pairs={{0,16},{16,32},{32,48},{48,64},{64,80},{80,96},{96,112},{112,0},{1... | collective-permute-start | bytes 393224 | tf_op jit(solution)/shard_map/ppermute | solution.py:392
  53.8 7.3 %copy-start.3 = (bf16[128,2048]{1,0:T(8,128)(2,1)S(1)}, bf16[128,2048]{1,0:T(8,128)(2,1)}, u32[]{:S(2)}) copy-start(bf16[128,2048]{1,0:T(8,128)(2,1)} %q.1) | copy-start | bytes 1572868
  54.9 6.1 %collective-permute-start.8 = (bf16[2176,256]{1,0:T(8,128)(2,1)S(1)}, bf16[2176,256]{1,0:T(8,128)(2,1)S(1)}, u32[]{:S(2)}, u32[]{:S(2)}) collective-permute-start(bf16[2176,256]{1,0:T(8,128)(2,1)S(1)} %constant_dynamic-update-slice_fusion.2.kv), channel_id=1, source_target_pairs={{0,2},{2,0},{1,3},{3,1},{4,6},{6,4},{5,7},{7,5},{8,10},{10,8},{9,1... | collective-permute-start | bytes 3342344 | tf_op jit(solution)/shard_map/ppermute | solution.py:401
  67.2 14.9 %collective-permute-start.10 = (bf16[128,2048]{1,0:T(8,128)(2,1)S(1)}, bf16[128,2048]{1,0:T(8,128)(2,1)S(1)}, u32[]{:S(2)}, u32[]{:S(2)}) collective-permute-start(bf16[128,2048]{1,0:T(8,128)(2,1)S(1)} %attention.1.refs_1_.refs_2_), channel_id=1, source_target_pairs={{0,65},{1,64},{64,1},{65,0},{2,67},{3,66},{66,3},{67,2},{4,69},{5,... | collective-permute-start | bytes 1572872 | tf_op jit(solution)/shard_map/ppermute | solution.py:436
  69.5 13.3 %collective-permute-start.9 = (bf16[128,2048]{1,0:T(8,128)(2,1)S(1)}, bf16[128,2048]{1,0:T(8,128)(2,1)S(1)}, u32[]{:S(2)}, u32[]{:S(2)}) collective-permute-start(bf16[128,2048]{1,0:T(8,128)(2,1)S(1)} %attention.1.refs_1_.refs_2_), channel_id=1, source_target_pairs={{0,1},{1,0},{64,65},{65,64},{2,3},{3,2},{66,67},{67,66},{4,5},{5,4... | collective-permute-start | bytes 1572872 | tf_op jit(solution)/shard_map/ppermute | solution.py:435
  71.6 0.7 copy-start.1
  72.3 21.7 %collective-permute-start.11 = (bf16[128,2048]{1,0:T(8,128)(2,1)S(1)}, bf16[128,2048]{1,0:T(8,128)(2,1)S(1)}, u32[]{:S(2)}, u32[]{:S(2)}) collective-permute-start(bf16[128,2048]{1,0:T(8,128)(2,1)S(1)} %attention.1.refs_1_.refs_2_), channel_id=1, source_target_pairs={{0,2},{2,0},{1,3},{3,1},{4,6},{6,4},{5,7},{7,5},{8,10},{10,8},{9,1... | collective-permute-start | bytes 1572872 | tf_op jit(solution)/shard_map/ppermute | solution.py:433
  82.8 6.9 %collective-permute-start.16 = (bf16[64,2048]{1,0:T(8,128)(2,1)S(1)}, bf16[64,2048]{1,0:T(8,128)(2,1)}, u32[]{:S(2)}, u32[]{:S(2)}) collective-permute-start(bf16[64,2048]{1,0:T(8,128)(2,1)S(1)} %slice.64), channel_id=1, source_target_pairs={{0,1},{1,0},{64,65},{65,64},{2,3},{3,2},{66,67},{67,66},{4,5},{5,4... | collective-permute-start | bytes 786440 | tf_op jit(solution)/shard_map/ppermute | solution.py:440
  83.8 7.9 %collective-permute-start.14 = (bf16[64,2048]{1,0:T(8,128)(2,1)S(1)}, bf16[64,2048]{1,0:T(8,128)(2,1)}, u32[]{:S(2)}, u32[]{:S(2)}) collective-permute-start(bf16[64,2048]{1,0:T(8,128)(2,1)S(1)} %slice.63), channel_id=1, source_target_pairs={{0,65},{1,64},{64,1},{65,0},{2,67},{3,66},{66,3},{67,2},{4,69},{5,... | collective-permute-start | bytes 786440 | tf_op jit(solution)/shard_map/ppermute | solution.py:439
  85.1 10.3 %collective-permute-start.12 = (bf16[128,2048]{1,0:T(8,128)(2,1)S(1)}, bf16[128,2048]{1,0:T(8,128)(2,1)S(1)}, u32[]{:S(2)}, u32[]{:S(2)}) collective-permute-start(bf16[128,2048]{1,0:T(8,128)(2,1)S(1)} %collective-permute-done.9.refs_5_.refs_6_), channel_id=1, source_target_pairs={{0,2},{2,0},{1,3},{3,1},{4,6},{6,4},{5,7},{7,5},{8,10},{10,8},{9,1... | collective-permute-start | bytes 1572872 | tf_op jit(solution)/shard_map/ppermute | solution.py:433
  86.4 9.0 %collective-permute-start.13 = (bf16[128,2048]{1,0:T(8,128)(2,1)S(1)}, bf16[128,2048]{1,0:T(8,128)(2,1)}, u32[]{:S(2)}, u32[]{:S(2)}) collective-permute-start(bf16[128,2048]{1,0:T(8,128)(2,1)S(1)} %collective-permute-done.10.refs_9_.refs_10_), channel_id=1, source_target_pairs={{0,2},{2,0},{1,3},{3,1},{4,6},{6,4},{5,7},{7,5},{8,10},{10,8},{9,1... | collective-permute-start | bytes 1572872 | tf_op jit(solution)/shard_map/ppermute | solution.py:433
  89.8 4.2 %collective-permute-start.17 = (bf16[64,2048]{1,0:T(8,128)(2,1)}, bf16[64,2048]{1,0:T(8,128)(2,1)}, u32[]{:S(2)}, u32[]{:S(2)}) collective-permute-start(bf16[64,2048]{1,0:T(8,128)(2,1)} %collective-permute-done.16.refs_17_.refs_18_), channel_id=1, source_target_pairs={{0,2},{2,0},{1,3},{3,1},{4,6},{6,4},{5,7},{7,5},{8,10},{10,8},{9,1... | collective-permute-start | bytes 786440 | tf_op jit(solution)/shard_map/ppermute | solution.py:433
  91.7 3.7 %collective-permute-start.15 = (bf16[64,2048]{1,0:T(8,128)(2,1)}, bf16[64,2048]{1,0:T(8,128)(2,1)}, u32[]{:S(2)}, u32[]{:S(2)}) collective-permute-start(bf16[64,2048]{1,0:T(8,128)(2,1)} %collective-permute-done.14.refs_13_.refs_14_), channel_id=1, source_target_pairs={{0,2},{2,0},{1,3},{3,1},{4,6},{6,4},{5,7},{7,5},{8,10},{10,8},{9,1... | collective-permute-start | bytes 786440 | tf_op jit(solution)/shard_map/ppermute | solution.py:433
  95.4 2.2 copy-start
  222.2 81.5 %copy-start.2 = (f32[128,512]{1,0:T(8,128)S(1)}, f32[128,512]{1,0:T(8,128)}, u32[]{:S(2)}) copy-start(f32[128,512]{1,0:T(8,128)} %copy-done.1) | copy-start | bytes 786436
Sparse Core Ops, SparseCore 0:
  43.2 48.4 all-gather.1

commit v6 on v5

--- a/solution.py
+++ b/solution.py
@@ -478,8 +478,8 @@
     tables = key_tables(tokens) + query_tables(tokens, lengths)
     got, before, third = lax.optimization_barrier((got, shift_row(row, 1), shift_row(row, 3)))
     half = row.shape[0] // 2
-    second, rest, oldest = lax.optimization_barrier(
-        (shift_row(before[:half], 1), shift_row(third[half:], -1), shift_row(row, 4))
+    second, rest, oldest, *tables = lax.optimization_barrier(
+        (shift_row(before[:half], 1), shift_row(third[half:], -1), shift_row(row, 4)) + tables
     )
     kv, other = gather_kv(row, [before, jnp.concatenate([second, rest]), third, oldest])
     weight = lax.all_gather(got[:, :weight_rows], ("y", "x"), axis=0, tiled=True)

time: 328 us -> 326 us (level)
  starting transfers between devices: 29.4 us -> 25 us
  waiting for transfers between devices: 38.7 us -> 42.6 us
where the time goes in v6:
time: 326 us; the launch traced here: 325 us
  blocking collectives  183 us (56%)
  Pallas kernels  45.4 us (14%)
  waiting for transfers between devices  42.6 us (13%)
  starting transfers between devices  25 us (8%)
  between operations  13.8 us (4%)
  local copies, waits for them, and re-layouts  9.57 us (3%)
  other arithmetic  5.74 us (2%)
    all_to_all x1, blocking collectives, body(): lax.all_to_all(outgoing, AXES, split_axis=0, concat_axis=0, tiled=True)  89 us
    all_to_all x1, blocking collectives, body(): lax.all_to_all(produced, AXES, split_axis=0, concat_axis=0, tiled=True)  81.4 us
    pallas_call x1, Pallas kernels, expert(): pl.pallas_call(expert_kernel, grid=(FIRST + SECOND,), in_specs=[pl.BlockS...  23.7 us
    ppermute x5, waiting for transfers between devices, shift_row(): return lax.ppermute(row, ('zh', 'y'), rotated(8, step))  16.9 us
    all_to_all x1, blocking collectives, body(): lax.all_to_all(mixed.reshape(GROUP, own_rows, width), LINE, split_axis=0,...  12.3 us
    ppermute x1, waiting for transfers between devices, gather_attended(): far = lax.ppermute(own, Z, flipped(4, 3))  10.8 us
    pallas_call x1, Pallas kernels, project(): pl.pallas_call(functools.partial(projection_kernel, steps), grid=(steps +...  10.6 us
  transfers between devices with their start and end apart: 20, of which 12 were waited for; matrix products, arithmetic and copies ran while one was open for 2% of the time, Pallas kernels for 2%

profile of v6, /device:TPU:5, one launch (start us, length us, event | category | flops | bytes accessed | tf_op | source)
XLA Modules:
  0.0 324.8 jit_solution(4628773736172562209)
XLA Ops:
  6.5 0.7 convert_element_type.14
  7.2 0.7 convert_element_type.15
  7.9 0.1 copy.33
  8.0 0.1 reshape.139
  8.1 1.0 copy.44
  9.1 1.1 copy.43
  10.2 1.0 pad_maximum_fusion
  11.2 6.1 %all-to-all-start = ((bf16[8,112,512]{2,1,0:T(8,128)(2,1)}), bf16[8,112,512]{2,1,0:T(8,128)(2,1)S(1)}, u32[]{:S(2)}, u32[]{:S(2)}) async-start(bf16[8,112,512]{2,1,0:T(8,128)(2,1)} %pad_maximum_fusion), calls=%async_computation | async-start | bytes 1835008 | tf_op jit(solution)/shard_map/all_to_all | solution.py:477
  17.5 0.3 collective-permute-start.2
  17.8 2.5 collective-permute-start.1
  20.2 1.0 collective-permute-done.2
  21.2 1.5 collective-permute-done.1
  22.7 1.7 collective-permute-done
  24.4 2.8 collective-permute-start.4
  27.2 1.3 collective-permute-start.3
  28.5 5.5 %collective-permute-done.4 = bf16[512,256]{1,0:T(8,128)(2,1)S(1)} collective-permute-done((bf16[512,256]{1,0:T(8,128)(2,1)S(1)}, bf16[512,256]{1,0:T(8,128)(2,1)S(1)}, u32[]{:S(2)}, u32[]{:S(2)}) %collective-permute-start.4) | collective-permute-done | bytes 262176 | tf_op jit(solution)/shard_map/ppermute | solution.py:392
  34.0 4.9 %collective-permute-done.3 = bf16[512,256]{1,0:T(8,128)(2,1)S(1)} collective-permute-done((bf16[512,256]{1,0:T(8,128)(2,1)S(1)}, bf16[512,256]{1,0:T(8,128)(2,1)S(1)}, u32[]{:S(2)}, u32[]{:S(2)}) %collective-permute-start.3) | collective-permute-done | bytes 262176 | tf_op jit(solution)/shard_map/ppermute | solution.py:392
  38.9 3.4 %all-to-all-done = bf16[8,112,512]{2,1,0:T(8,128)(2,1)S(1)} async-done(((bf16[8,112,512]{2,1,0:T(8,128)(2,1)}), bf16[8,112,512]{2,1,0:T(8,128)(2,1)S(1)}, u32[]{:S(2)}, u32[]{:S(2)}) %all-to-all-start) | async-done | bytes 917536 | tf_op jit(solution)/shard_map/all_to_all | solution.py:477
  42.3 0.8 slice.65
  43.2 0.1 reshape.140
  43.3 0.1 fusion.3
  43.4 0.1 broadcast_add_fusion.1
  43.5 0.1 slice.52
  43.6 0.1 reshape.141
  43.8 0.2 reduce-window.9
  43.9 0.1 fusion.6
  44.1 0.1 select_reduce_fusion
  44.3 0.1 collective-permute-start.7
  44.4 0.7 fusion.7
  45.1 0.1 collective-permute-start.6
  45.2 1.5 collective-permute-start.5
  46.6 2.6 pad_add_fusion.lim
  49.2 6.4 %collective-permute-done.7 = bf16[512,256]{1,0:T(8,128)(2,1)S(1)} collective-permute-done((bf16[512,256]{1,0:T(8,128)(2,1)S(1)}, bf16[512,256]{1,0:T(8,128)(2,1)S(1)}, u32[]{:S(2)}, u32[]{:S(2)}) %collective-permute-start.7) | collective-permute-done | bytes 262176 | tf_op jit(solution)/shard_map/ppermute | solution.py:392
  55.7 0.1 fusion
  55.9 2.0 collective-permute-start.8
  57.9 0.1 copy.35.qstart
  58.0 2.3 collective-permute-done.8.other
  60.3 1.0 copy-done.3
  61.3 6.0 %attention.1.refs_1_.refs_2_ = bf16[128,2048]{1,0:T(8,128)(2,1)S(1)} custom-call(s32[4]{0:T(128)S(1)} %pad_add_fusion.lim, s32[6]{0:T(128)S(1)} %get-tuple-element.29.low, s32[6]{0:T(128)S(1)} %get-tuple-element.30.high, bf16[128,2048]{1,0:T(8,128)(2,1)S(1)} %copy-done.3, bf16[2176,256]{1,0:T(8,128)(2,1)S(1)} %constant_dynamic-update-slice_fusion.2.kv, ...), custom_call_target="tpu_custom_call" | custom-call | flops 10000000000 | bytes 4000000 | tf_op jit(solution)/shard_map/attention/pallas_call | solution.py:104
  67.3 0.3 collective-permute-start.10
  67.6 0.5 collective-permute-start.9
  68.2 0.1 reshape.144
  68.3 0.1 copy.36
  68.4 0.9 routing.1
  69.4 0.7 copy-done.1
  70.1 0.9 collective-permute-start.11
  71.0 10.8 %collective-permute-done.10.refs_9_.refs_10_ = bf16[128,2048]{1,0:T(8,128)(2,1)S(1)} collective-permute-done((bf16[128,2048]{1,0:T(8,128)(2,1)S(1)}, bf16[128,2048]{1,0:T(8,128)(2,1)S(1)}, u32[]{:S(2)}, u32[]{:S(2)}) %collective-permute-start.10) | collective-permute-done | bytes 524320 | tf_op jit(solution)/shard_map/ppermute | solution.py:436
  81.9 0.1 collective-permute-start.16
  82.0 1.5 collective-permute-start.14
  83.5 1.7 collective-permute-start.12
  85.2 3.6 %collective-permute-done.16.refs_17_.refs_18_ = bf16[64,2048]{1,0:T(8,128)(2,1)} collective-permute-done((bf16[64,2048]{1,0:T(8,128)(2,1)S(1)}, bf16[64,2048]{1,0:T(8,128)(2,1)}, u32[]{:S(2)}, u32[]{:S(2)}) %collective-permute-start.16) | collective-permute-done | bytes 262176 | tf_op jit(solution)/shard_map/ppermute | solution.py:440
  88.8 2.0 collective-permute-start.17
  90.8 1.3 collective-permute-start.15
  92.1 0.1 stack.55.refs_0_
  92.2 0.1 collective-permute-done.17.refs_19_.refs_20_
  92.3 1.3 collective-permute-done.15.refs_15_.refs_16_
  93.6 2.2 copy-done
  95.8 10.6 %projection.1 = (bf16[512,512]{1,0:T(8,128)(2,1)S(1)}, bf16[128,48,512]{2,1,0:T(8,128)(2,1)S(1)}) custom-call(s32[12]{0:T(128)S(1)} %stack.55.refs_0_, bf16[128,2048]{1,0:T(8,128)(2,1)S(1)} %attention.1.refs_1_.refs_2_, bf16[128,2048]{1,0:T(8,128)(2,1)S(1)} %attention.1.refs_1_.refs_2_, bf16[128,2048]{1,0:T(8,128)(2,1)S(1)} %collective-permute-done.11.refs_3_.refs_4_, ...), custom_call_target="tpu_custom_call" | custom-call | tf_op jit(solution)/shard_map/projection/pallas_call | solution.py:191
  106.4 89.0 %all_to_all.20 = bf16[128,48,512]{2,1,0:T(8,128)(2,1)} all-to-all(bf16[128,48,512]{2,1,0:T(8,128)(2,1)S(1)} %get-tuple-element.45), channel_id=1, replica_groups=mesh['zh'=2,'y'=4,'x'=4,'c'=2,'zl'=2] {'zh','y','x','c','zl'}, dimensions={0} | all-to-all | bytes 12582912 | tf_op jit(solution)/shard_map/all_to_all | solution.py:508
  195.4 23.7 %expert.1 = bf16[2,16,4,48,512]{4,3,2,1,0:T(8,128)(2,1)} custom-call(bf16[2,16,4,48,512]{4,3,2,1,0:T(8,128)(2,1)} %bitcast.44, bf16[1,4096,768]{2,1,0:T(8,128)(2,1)} %gate_w.1, bf16[1,4096,768]{2,1,0:T(8,128)(2,1)} %up_w.1, bf16[1,768,4096]{2,1,0:T(8,128)(2,1)} %down_w.1), custom_call_target="tpu_custom_call" | custom-call | tf_op jit(solution)/shard_map/expert/pallas_call | solution.py:312
  219.2 81.4 %all_to_all.21.answers = bf16[128,48,512]{2,1,0:T(8,128)(2,1)S(1)} all-to-all(bf16[128,48,512]{2,1,0:T(8,128)(2,1)} %bitcast.45), channel_id=1, replica_groups=mesh['zh'=2,'y'=4,'x'=4,'c'=2,'zl'=2] {'zh','y','x','c','zl'}, dimensions={0} | all-to-all | bytes 12582912 | tf_op jit(solution)/shard_map/all_to_all | solution.py:512
  300.6 4.2 %combine.1 = bf16[512,512]{1,0:T(8,128)(2,1)S(1)} custom-call(f32[128,512]{1,0:T(8,128)S(1)} %get-tuple-element.40.refs_23_.slots, f32[128,512]{1,0:T(8,128)S(1)} %copy-done.2, bf16[128,48,512]{2,1,0:T(8,128)(2,1)S(1)} %all_to_all.21.answers, bf16[512,512]{1,0:T(8,128)(2,1)S(1)} %get-tuple-element.46.hidden), custom_call_target="tpu_custom_call" | custom-call | tf_op jit(solution)/shard_map/combine/pallas_call | solution.py:368
  304.8 12.3 %all_to_all.22 = bf16[8,64,512]{2,1,0:T(8,128)(2,1)S(1)} all-to-all(bf16[8,64,512]{2,1,0:T(8,128)(2,1)S(1)} %bitcast.43), channel_id=1, replica_groups=mesh['zh'=2,'y'=4,'x'=4,'c'=2,'zl'=2] {'zh','c','zl'}, dimensions={0} | all-to-all | bytes 1048576 | tf_op jit(solution)/shard_map/all_to_all | solution.py:514
  317.1 0.8 copy.40
  (62 shorter events, 0.7 us)
Async XLA Ops:
  11.2 6.2 %copy-start.6 = (bf16[128,128]{1,0:T(8,128)(2,1)S(1)}, bf16[128,128]{1,0:T(8,128)(2,1)}, u32[]{:S(2)}) copy-start(bf16[128,128]{1,0:T(8,128)(2,1)} %param.14) | copy-start | bytes 98308
  11.2 6.2 %copy-start.7 = (bf16[128,128]{1,0:T(8,128)(2,1)S(1)}, bf16[128,128]{1,0:T(8,128)(2,1)}, u32[]{:S(2)}) copy-start(bf16[128,128]{1,0:T(8,128)(2,1)} %param.15) | copy-start | bytes 98308
  11.2 31.1 %all-to-all-start = ((bf16[8,112,512]{2,1,0:T(8,128)(2,1)}), bf16[8,112,512]{2,1,0:T(8,128)(2,1)S(1)}, u32[]{:S(2)}, u32[]{:S(2)}) async-start(bf16[8,112,512]{2,1,0:T(8,128)(2,1)} %pad_maximum_fusion), calls=%async_computation | async-start | bytes 1835008 | tf_op jit(solution)/shard_map/all_to_all | solution.py:477
  17.4 26.0 %copy-start.8 = (s32[17]{0:T(128)S(1)}, s32[17]{0:T(128)}, u32[]{:S(2)}) copy-start(s32[17]{0:T(128)} %constant.90) | copy-start | bytes 208
  17.4 26.4 %copy-start.9 = (s32[8]{0:T(128)S(1)}, s32[8]{0:T(128)}, u32[]{:S(2)}) copy-start(s32[8]{0:T(128)} %param.16) | copy-start | bytes 100
  17.4 76.3 %all-gather.2.cloned.1.call-start = ((), (), s32[]{:S(2)}) async-start(), calls=%async_computation.4 | async-start | bytes 4456448 | tf_op jit(solution)/shard_map/all_gather | solution.py:485
  17.5 3.8 %collective-permute-start.2 = (bf16[128,256]{1,0:T(8,128)(2,1)S(1)}, bf16[128,256]{1,0:T(8,128)(2,1)S(1)}, u32[]{:S(2)}, u32[]{:S(2)}) collective-permute-start(bf16[128,256]{1,0:T(8,128)(2,1)S(1)} %get-tuple-element.50), channel_id=1, source_target_pairs={{0,12},{4,0},{8,4},{12,8},{1,13},{5,1},{9,5},{13,9},{2,14},{6,2},{... | collective-permute-start | bytes 196616 | tf_op jit(solution)/shard_map/ppermute | solution.py:387
  17.8 4.9 %collective-permute-start.1 = (bf16[128,256]{1,0:T(8,128)(2,1)S(1)}, bf16[128,256]{1,0:T(8,128)(2,1)S(1)}, u32[]{:S(2)}, u32[]{:S(2)}) collective-permute-start(bf16[128,256]{1,0:T(8,128)(2,1)S(1)} %get-tuple-element.50), channel_id=1, source_target_pairs={{0,8},{4,12},{8,0},{12,4},{1,9},{5,13},{9,1},{13,5},{2,10},{6,14},... | collective-permute-start | bytes 196616 | tf_op jit(solution)/shard_map/ppermute | solution.py:387
  20.2 4.2 %collective-permute-start = (bf16[128,256]{1,0:T(8,128)(2,1)S(1)}, bf16[128,256]{1,0:T(8,128)(2,1)S(1)}, u32[]{:S(2)}, u32[]{:S(2)}) collective-permute-start(bf16[128,256]{1,0:T(8,128)(2,1)S(1)} %get-tuple-element.50), channel_id=1, source_target_pairs={{0,4},{4,8},{8,12},{12,0},{1,5},{5,9},{9,13},{13,1},{2,6},{6,10},{... | collective-permute-start | bytes 196616 | tf_op jit(solution)/shard_map/ppermute | solution.py:387
  24.4 9.5 %collective-permute-start.4 = (bf16[512,256]{1,0:T(8,128)(2,1)S(1)}, bf16[512,256]{1,0:T(8,128)(2,1)S(1)}, u32[]{:S(2)}, u32[]{:S(2)}) collective-permute-start(bf16[512,256]{1,0:T(8,128)(2,1)S(1)} %pad_maximum_fusion.1), channel_id=1, source_target_pairs={{0,48},{16,64},{32,80},{48,96},{64,112},{80,0},{96,16},{112,32},{1... | collective-permute-start | bytes 786440 | tf_op jit(solution)/shard_map/ppermute | solution.py:392
  27.2 11.7 %collective-permute-start.3 = (bf16[512,256]{1,0:T(8,128)(2,1)S(1)}, bf16[512,256]{1,0:T(8,128)(2,1)S(1)}, u32[]{:S(2)}, u32[]{:S(2)}) collective-permute-start(bf16[512,256]{1,0:T(8,128)(2,1)S(1)} %pad_maximum_fusion.1), channel_id=1, source_target_pairs={{0,16},{16,32},{32,48},{48,64},{64,80},{80,96},{96,112},{112,0},{1... | collective-permute-start | bytes 786440 | tf_op jit(solution)/shard_map/ppermute | solution.py:392
  42.3 2.0 copy-start.4
  44.3 11.3 %collective-permute-start.7 = (bf16[512,256]{1,0:T(8,128)(2,1)S(1)}, bf16[512,256]{1,0:T(8,128)(2,1)S(1)}, u32[]{:S(2)}, u32[]{:S(2)}) collective-permute-start(bf16[512,256]{1,0:T(8,128)(2,1)S(1)} %pad_maximum_fusion.1), channel_id=1, source_target_pairs={{0,64},{16,80},{32,96},{48,112},{64,0},{80,16},{96,32},{112,48},{1... | collective-permute-start | bytes 786440 | tf_op jit(solution)/shard_map/ppermute | solution.py:392
  45.1 10.6 %collective-permute-start.6 = (bf16[256,256]{1,0:T(8,128)(2,1)S(1)}, bf16[256,256]{1,0:T(8,128)(2,1)S(1)}, u32[]{:S(2)}, u32[]{:S(2)}) collective-permute-start(bf16[256,256]{1,0:T(8,128)(2,1)S(1)} %slice.51), channel_id=1, source_target_pairs={{0,112},{16,0},{32,16},{48,32},{64,48},{80,64},{96,80},{112,96},{1... | collective-permute-start | bytes 393224 | tf_op jit(solution)/shard_map/ppermute | solution.py:392
  45.2 10.5 %collective-permute-start.5 = (bf16[256,256]{1,0:T(8,128)(2,1)S(1)}, bf16[256,256]{1,0:T(8,128)(2,1)S(1)}, u32[]{:S(2)}, u32[]{:S(2)}) collective-permute-start(bf16[256,256]{1,0:T(8,128)(2,1)S(1)} %slice.50), channel_id=1, source_target_pairs={{0,16},{16,32},{32,48},{48,64},{64,80},{80,96},{96,112},{112,0},{1... | collective-permute-start | bytes 393224 | tf_op jit(solution)/shard_map/ppermute | solution.py:392
  55.9 4.4 %collective-permute-start.8 = (bf16[2176,256]{1,0:T(8,128)(2,1)S(1)}, bf16[2176,256]{1,0:T(8,128)(2,1)S(1)}, u32[]{:S(2)}, u32[]{:S(2)}) collective-permute-start(bf16[2176,256]{1,0:T(8,128)(2,1)S(1)} %constant_dynamic-update-slice_fusion.2.kv), channel_id=1, source_target_pairs={{0,2},{2,0},{1,3},{3,1},{4,6},{6,4},{5,7},{7,5},{8,10},{10,8},{9,1... | collective-permute-start | bytes 3342344 | tf_op jit(solution)/shard_map/ppermute | solution.py:401
  60.3 1.0 copy-start.3
  61.3 6.8 %copy-start.5 = (bf16[8,112,512]{2,1,0:T(8,128)(2,1)S(1)}, bf16[8,112,512]{2,1,0:T(8,128)(2,1)}, u32[]{:S(2)}) copy-start(bf16[8,112,512]{2,1,0:T(8,128)(2,1)} %copy-done.4) | copy-start | bytes 2752516
  67.3 14.5 %collective-permute-start.10 = (bf16[128,2048]{1,0:T(8,128)(2,1)S(1)}, bf16[128,2048]{1,0:T(8,128)(2,1)S(1)}, u32[]{:S(2)}, u32[]{:S(2)}) collective-permute-start(bf16[128,2048]{1,0:T(8,128)(2,1)S(1)} %attention.1.refs_1_.refs_2_), channel_id=1, source_target_pairs={{0,65},{1,64},{64,1},{65,0},{2,67},{3,66},{66,3},{67,2},{4,69},{5,... | collective-permute-start | bytes 1572872 | tf_op jit(solution)/shard_map/ppermute | solution.py:436
  67.6 14.2 %collective-permute-start.9 = (bf16[128,2048]{1,0:T(8,128)(2,1)S(1)}, bf16[128,2048]{1,0:T(8,128)(2,1)S(1)}, u32[]{:S(2)}, u32[]{:S(2)}) collective-permute-start(bf16[128,2048]{1,0:T(8,128)(2,1)S(1)} %attention.1.refs_1_.refs_2_), channel_id=1, source_target_pairs={{0,1},{1,0},{64,65},{65,64},{2,3},{3,2},{66,67},{67,66},{4,5},{5,4... | collective-permute-start | bytes 1572872 | tf_op jit(solution)/shard_map/ppermute | solution.py:435
  69.4 0.7 copy-start.1
  70.1 22.1 %collective-permute-start.11 = (bf16[128,2048]{1,0:T(8,128)(2,1)S(1)}, bf16[128,2048]{1,0:T(8,128)(2,1)S(1)}, u32[]{:S(2)}, u32[]{:S(2)}) collective-permute-start(bf16[128,2048]{1,0:T(8,128)(2,1)S(1)} %attention.1.refs_1_.refs_2_), channel_id=1, source_target_pairs={{0,2},{2,0},{1,3},{3,1},{4,6},{6,4},{5,7},{7,5},{8,10},{10,8},{9,1... | collective-permute-start | bytes 1572872 | tf_op jit(solution)/shard_map/ppermute | solution.py:433
  81.9 6.9 %collective-permute-start.16 = (bf16[64,2048]{1,0:T(8,128)(2,1)S(1)}, bf16[64,2048]{1,0:T(8,128)(2,1)}, u32[]{:S(2)}, u32[]{:S(2)}) collective-permute-start(bf16[64,2048]{1,0:T(8,128)(2,1)S(1)} %slice.64), channel_id=1, source_target_pairs={{0,1},{1,0},{64,65},{65,64},{2,3},{3,2},{66,67},{67,66},{4,5},{5,4... | collective-permute-start | bytes 786440 | tf_op jit(solution)/shard_map/ppermute | solution.py:440
  82.0 8.8 %collective-permute-start.14 = (bf16[64,2048]{1,0:T(8,128)(2,1)S(1)}, bf16[64,2048]{1,0:T(8,128)(2,1)}, u32[]{:S(2)}, u32[]{:S(2)}) collective-permute-start(bf16[64,2048]{1,0:T(8,128)(2,1)S(1)} %slice.63), channel_id=1, source_target_pairs={{0,65},{1,64},{64,1},{65,0},{2,67},{3,66},{66,3},{67,2},{4,69},{5,... | collective-permute-start | bytes 786440 | tf_op jit(solution)/shard_map/ppermute | solution.py:439
  83.5 10.1 %collective-permute-start.12 = (bf16[128,2048]{1,0:T(8,128)(2,1)S(1)}, bf16[128,2048]{1,0:T(8,128)(2,1)S(1)}, u32[]{:S(2)}, u32[]{:S(2)}) collective-permute-start(bf16[128,2048]{1,0:T(8,128)(2,1)S(1)} %collective-permute-done.9.refs_5_.refs_6_), channel_id=1, source_target_pairs={{0,2},{2,0},{1,3},{3,1},{4,6},{6,4},{5,7},{7,5},{8,10},{10,8},{9,1... | collective-permute-start | bytes 1572872 | tf_op jit(solution)/shard_map/ppermute | solution.py:433
  85.2 8.4 %collective-permute-start.13 = (bf16[128,2048]{1,0:T(8,128)(2,1)S(1)}, bf16[128,2048]{1,0:T(8,128)(2,1)}, u32[]{:S(2)}, u32[]{:S(2)}) collective-permute-start(bf16[128,2048]{1,0:T(8,128)(2,1)S(1)} %collective-permute-done.10.refs_9_.refs_10_), channel_id=1, source_target_pairs={{0,2},{2,0},{1,3},{3,1},{4,6},{6,4},{5,7},{7,5},{8,10},{10,8},{9,1... | collective-permute-start | bytes 1572872 | tf_op jit(solution)/shard_map/ppermute | solution.py:433
  88.8 3.5 %collective-permute-start.17 = (bf16[64,2048]{1,0:T(8,128)(2,1)}, bf16[64,2048]{1,0:T(8,128)(2,1)}, u32[]{:S(2)}, u32[]{:S(2)}) collective-permute-start(bf16[64,2048]{1,0:T(8,128)(2,1)} %collective-permute-done.16.refs_17_.refs_18_), channel_id=1, source_target_pairs={{0,2},{2,0},{1,3},{3,1},{4,6},{6,4},{5,7},{7,5},{8,10},{10,8},{9,1... | collective-permute-start | bytes 786440 | tf_op jit(solution)/shard_map/ppermute | solution.py:433
  90.8 2.8 collective-permute-start.15
  93.6 2.2 copy-start
  219.2 81.4 %copy-start.2 = (f32[128,512]{1,0:T(8,128)S(1)}, f32[128,512]{1,0:T(8,128)}, u32[]{:S(2)}) copy-start(f32[128,512]{1,0:T(8,128)} %copy-done.1) | copy-start | bytes 786436
Sparse Core Ops, SparseCore 0:
  43.2 48.4 all-gather.1
